TPU v7x, 32 devices: a whole 2x2x4 slice. The times are simulated.
32 devices in a mesh: seq: 4 (over z), chan: 2 (over x), batch: 4 (over y, core).
Axes of the slice: x: 2, y: 2, z: 4, core: 2. Of those that a mesh axis runs over, the one named last changes fastest.
Arguments:
- tokens: bfloat16 [131072, 1024], P(('batch', 'seq'), 'chan'), parts along dimension 0, may hold values from -6 to 6
- gate_in: bfloat16 [131072, 1024], P(('batch', 'seq'), 'chan'), parts along dimension 0, may hold values from -6 to 6
- mix_first: bfloat16 [512, 512], replicated, may hold values from -0.25 to 0.25
- mix_second: bfloat16 [64, 64], replicated, may hold values from -0.75 to 0.75
- twiddle: float32 [64, 512], P('seq'), may hold values from 0.5 to 2
- out_proj: bfloat16 [1024, 1024], replicated, may hold values from -0.1875 to 0.1875
Outputs:
- mixed: bfloat16 [131072, 1024], P(('batch', 'seq'), 'chan'), parts along dimension 0
There are 4 independent parts, one for each index of `batch`. A program takes and returns all parts, laid end to end along the dimension named above; an argument that names none is the same for every part. Nothing has to cross between parts.
All inputs are finite; a program needn't handle non-finite values.
Results may differ from a plain program's by a relative error of at most 0.012.
Values may be sent and summed in bfloat16 or wider, within the bound.
No kernel may reach another device: no remote copies, remote signals or barrier semaphores. Data moves between devices by JAX's collectives and lax.ppermute only.
A program may use at most 128 MiB of HBM per device.

v0:
```python
import jax
import jax.numpy as jnp
from jax import lax
from jax.sharding import PartitionSpec as P

B1 = 512


def body(tokens, gate_in, mix_first, mix_second, twiddle, out_proj):
    seq_rows, chan_cols = tokens.shape
    blocks_here = seq_rows // B1
    blocked = tokens.reshape(blocks_here, B1, chan_cols)
    first_mixed = jnp.einsum("ik,bkc->bic", mix_first, blocked, preferred_element_type=jnp.float32)
    first_mixed = (first_mixed * twiddle[:, :, None]).astype(jnp.bfloat16)
    second_mixed = jnp.einsum(
        "jb,bic->jic",
        mix_second,
        lax.all_to_all(first_mixed, "seq", split_axis=1, concat_axis=0, tiled=True),
        preferred_element_type=jnp.float32,
    )
    second_mixed = second_mixed.astype(jnp.bfloat16)
    returned = lax.all_to_all(second_mixed, "seq", split_axis=0, concat_axis=1, tiled=True)
    hidden = (
        returned.reshape(seq_rows, chan_cols).astype(jnp.float32) * gate_in.astype(jnp.float32)
    ).astype(jnp.bfloat16)
    chan_count = lax.axis_size("chan")
    full_rows = lax.all_to_all(hidden, "chan", split_axis=0, concat_axis=1, tiled=True)
    running = jnp.zeros((full_rows.shape[0], out_proj.shape[1]), jnp.float32)
    for group in range(chan_count):
        columns = full_rows[:, group * chan_cols : (group + 1) * chan_cols]
        weight_rows = out_proj[group * chan_cols : (group + 1) * chan_cols, :]
        partial_term = jnp.dot(columns, weight_rows, preferred_element_type=jnp.float32).astype(
            jnp.bfloat16
        )
        partial_term = lax.optimization_barrier(partial_term)
        running = running + partial_term.astype(jnp.float32)
    projected = running.astype(jnp.bfloat16)
    return lax.all_to_all(projected, "chan", split_axis=1, concat_axis=0, tiled=True)


def solution(mesh):
    placed = (
        P(("batch", "seq"), "chan"),
        P(("batch", "seq"), "chan"),
        P(),
        P(),
        P("seq", None),
        P(),
    )
    return jax.shard_map(
        body, mesh=mesh, in_specs=placed, out_specs=P(("batch", "seq"), "chan"), check_vma=False
    )
```

profile of v0, /device:TPU:0, one launch (start us, length us, event | category | flops | bytes accessed | tf_op | source)
XLA Modules:
  0.0 701.6 jit_solution(13724287313506133174)
XLA Ops:
  0.0 0.0 copy-start
  0.0 1.0 copy-done
  1.0 10.3 %fusion.1 = bf16[16,512,512]{1,2,0:T(8,128)(2,1)} fusion(f32[16,512]{1,0:T(8,128)} %param.10, bf16[16,512,512]{2,1,0:T(8,128)(2,1)} %bitcast.45, bf16[512,512]{1,0:T(8,128)(2,1)S(1)} %copy-done), kind=kOutput, calls=%fused_computation.8 | convolution fusion | flops 4303355904 | bytes 17334272 | tf_op jit(solution)/shard_map/ik,bkc->bic/dot_general | solution.py:13
  11.3 14.9 %copy.21 = bf16[16,512,512]{2,0,1:T(8,128)(2,1)} copy(bf16[16,512,512]{1,2,0:T(8,128)(2,1)} %fusion.1) | data formatting | bytes 16777216 | tf_op jit(solution)/shard_map/convert_element_type | solution.py:14
  26.2 192.1 %all_to_all.65 = bf16[16,512,512]{2,0,1:T(8,128)(2,1)} all-to-all(bf16[16,512,512]{2,0,1:T(8,128)(2,1)} %copy.21), channel_id=1, replica_groups=mesh['seq'=4,'chan'=2,'batch'=4] {'seq'}, dimensions={1} | all-to-all | bytes 16777216 | tf_op jit(solution)/shard_map/all_to_all | solution.py:18
  218.4 0.0 copy-start.2
  218.4 8.2 %copy.22 = bf16[16,4,128,512]{3,0,1,2:T(8,128)(2,1)} copy(bf16[16,4,128,512]{3,0,2,1:T(8,128)(2,1)} %bitcast.38) | data formatting | bytes 16777216 | tf_op jit(solution)/shard_map/all_to_all | solution.py:18
  226.6 0.0 copy-done.2
  226.6 8.9 %convert_bitcast_fusion = bf16[64,128,512]{2,0,1:T(8,128)(2,1)} fusion(bf16[64,128,512]{2,0,1:T(8,128)(2,1)} %bitcast.37, bf16[64,64]{1,0:T(8,128)(2,1)S(1)} %copy-done.2), kind=kOutput, calls=%fused_computation.5 | convolution fusion | flops 541065216 | bytes 16785408 | tf_op jit(solution)/shard_map/jb,bic->jic/dot_general | solution.py:15
  235.5 11.5 %copy.23 = bf16[64,128,512]{2,1,0:T(8,128)(2,1)} copy(bf16[64,128,512]{2,0,1:T(8,128)(2,1)} %convert_bitcast_fusion) | data formatting | bytes 16777216 | tf_op jit(solution)/shard_map/convert_element_type | solution.py:21
  247.0 190.2 %all_to_all.66 = bf16[64,128,512]{2,1,0:T(8,128)(2,1)} all-to-all(bf16[64,128,512]{2,1,0:T(8,128)(2,1)} %copy.23), channel_id=1, replica_groups=mesh['seq'=4,'chan'=2,'batch'=4] {'seq'}, dimensions={0} | all-to-all | bytes 16777216 | tf_op jit(solution)/shard_map/all_to_all | solution.py:22
  437.3 11.5 %copy.24 = f32[4,16,128,512]{3,2,0,1:T(8,128)} copy(bf16[4,16,128,512]{3,2,1,0:T(8,128)(2,1)} %bitcast.36) | data formatting | bytes 25165824 | tf_op jit(solution)/shard_map/convert_element_type | solution.py:24
  448.8 9.2 %fusion = bf16[8192,512]{1,0:T(8,128)(2,1)S(1)} fusion(f32[4,16,128,512]{3,2,0,1:T(8,128)} %copy.24, bf16[8192,512]{1,0:T(8,128)(2,1)} %param.7), kind=kLoop, calls=%fused_computation.1 | loop fusion | flops 12582912 | bytes 33554432 | tf_op jit(solution)/shard_map/convert_element_type | solution.py:25
  458.0 95.7 %all_to_all.67 = bf16[2,4096,512]{2,1,0:T(8,128)(2,1)} all-to-all(bf16[2,4096,512]{2,1,0:T(8,128)(2,1)S(1)} %bitcast.42), channel_id=1, replica_groups=mesh['seq'=4,'chan'=2,'batch'=4] {'chan'}, dimensions={0} | all-to-all | bytes 16777216 | tf_op jit(solution)/shard_map/all_to_all | solution.py:27
  553.7 0.0 copy-start.3
  553.7 12.1 %copy.25 = bf16[4096,2,512]{0,2,1:T(8,128)(2,1)} copy(bf16[4096,2,512]{2,0,1:T(8,128)(2,1)} %bitcast.39) | data formatting | bytes 16777216 | tf_op jit(solution)/shard_map/all_to_all | solution.py:27
  565.8 0.0 copy-done.3
  565.8 7.0 convolution_convert_fusion
  572.8 7.0 convolution_convert_fusion.1
  579.8 5.7 add_convert_fusion
  585.5 7.3 %copy.30 = bf16[512,2,8,512]{3,2,0,1:T(8,128)(2,1)} copy(bf16[512,2,8,512]{3,2,1,0:T(8,128)(2,1)} %bitcast.35) | data formatting | bytes 16777216 | tf_op jit(solution)/shard_map/all_to_all | solution.py:38
  592.8 101.5 %all_to_all.68 = bf16[4096,2,512]{2,0,1:T(8,128)(2,1)} all-to-all(bf16[4096,2,512]{2,0,1:T(8,128)(2,1)} %bitcast.40), channel_id=1, replica_groups=mesh['seq'=4,'chan'=2,'batch'=4] {'chan'}, dimensions={1} | all-to-all | bytes 16777216 | tf_op jit(solution)/shard_map/all_to_all | solution.py:38
  694.2 7.4 %copy.32 = bf16[8192,512]{1,0:T(8,128)(2,1)} copy(bf16[8192,512]{1,0:T(8,128)(2,1)} %bitcast.41) | data formatting | bytes 16777216
  701.6 0.0 copy-done.1
  (1 shorter events, 0.0 us)
Async XLA Ops:
  0.0 1.0 copy-start
  218.4 8.2 %copy-start.2 = (bf16[64,64]{1,0:T(8,128)(2,1)S(1)}, bf16[64,64]{1,0:T(8,128)(2,1)}, u32[]{:S(2)}) copy-start(bf16[64,64]{1,0:T(8,128)(2,1)} %param.9) | copy-start | bytes 24580
  553.7 12.1 %copy-start.3 = (bf16[1024,1024]{1,0:T(8,128)(2,1)S(1)}, bf16[1024,1024]{1,0:T(8,128)(2,1)}, u32[]{:S(2)}) copy-start(bf16[1024,1024]{1,0:T(8,128)(2,1)} %param.11) | copy-start | bytes 6291460
  694.2 7.4 %copy-start.1 = (bf16[512,512]{1,0:T(8,128)(2,1)S(1)}, bf16[512,512]{1,0:T(8,128)(2,1)}, u32[]{:S(2)}) copy-start(bf16[512,512]{1,0:T(8,128)(2,1)} %param.8) | copy-start | bytes 1572868
where the time goes:
time: 703 us; the launch traced here: 702 us
  blocking collectives  580 us (83%)
  local copies, waits for them, and re-layouts  73.9 us (11%)
  matrix products  33.2 us (5%)
  other arithmetic  14.9 us (2%)
    all_to_all x1, blocking collectives, body(): lax.all_to_all(first_mixed, 'seq', split_axis=1, concat_axis=0, tiled=True)  192 us
    all_to_all x1, blocking collectives, body(): lax.all_to_all(second_mixed, 'seq', split_axis=0, concat_axis=1, tiled=True)  190 us
    all_to_all x1, blocking collectives, body(): lax.all_to_all(projected, 'chan', split_axis=1, concat_axis=0, tiled=True)  101 us
    all_to_all x1, blocking collectives, body(): lax.all_to_all(hidden, 'chan', split_axis=0, concat_axis=1, tiled=True)  95.7 us
    convert_element_type x1, local copies, waits for them, and re-layouts, body(): first_mixed = (first_mixed * twiddle[:, :, None]).astype(jnp.bfloat16)  14.9 us

commit v1 on v0

v1 whole, which is shorter than its diff:
```python
import functools

import jax
import jax.numpy as jnp
from jax import lax
from jax.experimental import pallas as pl
from jax.experimental.pallas import tpu as pltpu
from jax.sharding import PartitionSpec as P

ROWS = 16
VMEM = 56 * 1024 * 1024
BF16 = jnp.bfloat16
F32 = jnp.float32
ANY = pl.BlockSpec(memory_space=pl.ANY)


def call(kernel, grid, in_specs, out_specs, out_shape, scalar, args, deps=(), scratch=(), aliases=None, flops=0, nbytes=0):
    def run(scalar_ref, *refs):
        n = len(args)
        kernel(scalar_ref, refs[:n], refs[n + len(deps) :])

    return pl.pallas_call(
        run,
        grid_spec=pltpu.PrefetchScalarGridSpec(
            num_scalar_prefetch=1,
            grid=grid,
            in_specs=list(in_specs) + [ANY] * len(deps),
            out_specs=out_specs,
            scratch_shapes=list(scratch),
        ),
        out_shape=out_shape,
        input_output_aliases=aliases or {},
        compiler_params=pltpu.CompilerParams(vmem_limit_bytes=VMEM),
        cost_estimate=pl.CostEstimate(flops=flops, bytes_accessed=nbytes, transcendentals=0),
    )(scalar, *args, *deps)


def first_factor(place, tokens, weights, scale, step, size, seqs, deps):
    blocks, inner, cols = tokens.shape
    sub = size // seqs
    per = scale.shape[2]

    def kernel(place_ref, ins, outs):
        tok, wt, sc = ins
        me = place_ref[0]
        starts = [pl.multiple_of((me ^ m) * sub, sub) for m in range(seqs)]
        lhs = jnp.concatenate([wt[pl.ds(s, sub), :] for s in starts], axis=0)
        rows = jnp.concatenate([sc[0, pl.ds(s, sub), :] for s in starts], axis=0)
        for b in range(per):
            got = jnp.dot(lhs, tok[b], preferred_element_type=F32)
            got = (got * rows[:, b : b + 1]).astype(BF16)
            for m in range(seqs):
                outs[m][b] = got[m * sub : (m + 1) * sub]

    return call(
        kernel,
        (blocks // per,),
        [
            pl.BlockSpec((per, inner, cols), lambda g, p: (g, 0, 0)),
            pl.BlockSpec((size, inner), lambda g, p: (step, 0)),
            pl.BlockSpec((1, size, per), lambda g, p: (g, step, 0)),
        ],
        [pl.BlockSpec((per, sub, cols), lambda g, p: (g, 0, 0))] * seqs,
        [jax.ShapeDtypeStruct((blocks, sub, cols), BF16)] * seqs,
        place,
        (tokens, weights, scale),
        deps,
        flops=2 * blocks * size * inner * cols,
        nbytes=2 * blocks * cols * (inner + size),
    )


def second_factor(place, parts, spread, deps):
    seqs = len(parts)
    blocks, sub, cols = parts[0].shape
    height = blocks * sub
    width = min(cols, 256)

    def kernel(place_ref, ins, outs):
        sp = ins[-1]
        rhs = [ins[m][...].reshape(height, width) for m in range(seqs)]
        for o in range(seqs):
            total = None
            for m in range(seqs):
                term = jnp.dot(
                    sp[o * height : (o + 1) * height, m * height : (m + 1) * height],
                    rhs[m],
                    preferred_element_type=F32,
                )
                total = term if total is None else total + term
            outs[o][...] = total.astype(BF16).reshape(blocks, sub, width)

    spec = pl.BlockSpec((blocks, sub, width), lambda g, p: (0, 0, g))
    return call(
        kernel,
        (cols // width,),
        [spec] * seqs + [pl.BlockSpec(spread.shape, lambda g, p: (0, 0))],
        [spec] * seqs,
        [jax.ShapeDtypeStruct((blocks, sub, cols), BF16)] * seqs,
        place,
        (*parts, spread),
        deps,
        flops=2 * (seqs * height) ** 2 * cols,
        nbytes=4 * seqs * height * cols,
    )


def gate_project(place, parts, gate, proj, step, chans, deps):
    seqs = len(parts)
    blocks, sub, cols = parts[0].shape
    size = seqs * sub
    per = min(4, blocks)

    def kernel(place_ref, ins, outs):
        got, gt, ws = ins[:seqs], ins[seqs], ins[seqs + 1 :]
        outs, hidden = outs[:-1], outs[-1]
        me = place_ref[0]
        for m in range(seqs):
            rows = pl.ds(pl.multiple_of((me ^ m) * sub, sub), sub)
            hidden[:, rows, :] = (got[m][...].astype(F32) * gt[:, rows, :].astype(F32)).astype(BF16)
        lhs = hidden[...].reshape(per * size, cols)
        for q in range(chans):
            term = jnp.dot(lhs, ws[q][...], preferred_element_type=F32)
            outs[q][...] = term.astype(BF16).reshape(per, size, cols)

    out = pl.BlockSpec((per, size, cols), lambda g, p: (g, 0, 0))
    return call(
        kernel,
        (blocks // per,),
        [pl.BlockSpec((per, sub, cols), lambda g, p: (g, 0, 0))] * seqs
        + [pl.BlockSpec((per, size, cols), lambda g, p: (g, step, 0))]
        + [pl.BlockSpec((cols, cols), functools.partial(lambda q, g, p: (p[1], p[1] ^ q), q)) for q in range(chans)],
        [out] * chans,
        [jax.ShapeDtypeStruct((blocks, size, cols), BF16)] * chans,
        place,
        (*parts, gate) + (proj,) * chans,
        deps,
        scratch=[pltpu.VMEM((per, size, cols), BF16)],
        flops=2 * blocks * size * cols * cols * chans,
        nbytes=2 * blocks * size * cols * (2 + chans),
    )


def add_up(place, parts, held, shape, step, deps):
    chans = len(parts)
    blocks, size, cols = parts[0].shape
    per = min(4, blocks)

    def kernel(place_ref, ins, outs):
        total = ins[0][...].astype(F32)
        for q in range(1, chans):
            total = total + ins[q][...].astype(F32)
        outs[0][...] = total.astype(BF16)

    spec = pl.BlockSpec((per, size, cols), lambda g, p: (g, 0, 0))
    carried = () if held is None else (held,)
    return call(
        kernel,
        (blocks // per,),
        [spec] * chans,
        [pl.BlockSpec((per, size, cols), lambda g, p: (g, step, 0))],
        [jax.ShapeDtypeStruct(shape, BF16)],
        place,
        tuple(parts),
        carried + tuple(deps),
        aliases={} if held is None else {1 + chans: 0},
        flops=blocks * size * cols * chans,
        nbytes=2 * blocks * size * cols * (1 + chans),
    )[0]


def by_offset(x, axis, me, count):
    bit = 1
    while bit < count:
        shape = x.shape
        split = x.reshape(shape[:axis] + (count // (2 * bit), 2, bit) + shape[axis + 1 :])
        x = jnp.where((me & bit) != 0, jnp.flip(split, axis + 1), split).reshape(shape)
        bit *= 2
    return x


def exchange(parts, axis):
    n = len(parts)
    order = sorted(range(1, n), reverse=True)
    got = {0: parts[0]}
    for m in order:
        got[m] = lax.ppermute(parts[m], axis, [(d, d ^ m) for d in range(n)])
    return [got[m] for m in range(n)]


def body(tokens, gate_in, mix_first, mix_second, twiddle, out_proj):
    rows, cols = tokens.shape
    inner = mix_first.shape[0]
    blocks = rows // inner
    seqs, chans = lax.axis_size("seq"), lax.axis_size("chan")
    seq, chan = lax.axis_index("seq"), lax.axis_index("chan")
    steps = max(1, min(8, inner // (seqs * ROWS)))
    size = inner // steps
    sub = size // seqs
    per = min(4, blocks)
    place = jnp.stack([seq, chan]).astype(jnp.int32)
    tokens = tokens.reshape(blocks, inner, cols)
    gate = gate_in.reshape(blocks, inner, cols)
    scale = twiddle.reshape(blocks // per, per, inner).transpose(0, 2, 1)
    order = mix_second.shape[0]
    mixer = mix_second.reshape(seqs, blocks, seqs, blocks)
    mixer = by_offset(by_offset(mixer, 0, seq, seqs), 2, seq, seqs).reshape(order, order)
    spread = jnp.where(
        jnp.eye(sub, dtype=bool)[None, :, None, :], mixer[:, None, :, None], jnp.zeros((), BF16)
    ).reshape(order * sub, order * sub)

    gone, back, firsts = {}, {}, {}
    sums, out = {}, None

    def first(t, deps):
        firsts[t] = exchange(first_factor(place, tokens, mix_first, scale, t, size, seqs, deps), "seq")

    first(0, ())
    first(1, (firsts[0][0],)) if steps > 1 else None
    last = None
    for t in range(steps + 2):
        if t < steps:
            got = second_factor(place, firsts[t], spread, () if last is None else (last,))
            last = got[0]
            back[t] = exchange(got, "seq")
            if t + 2 < steps:
                first(t + 2, (last,))
                last = firsts[t + 2][0]
        if 0 <= t - 1 < steps:
            got = gate_project(place, back[t - 1], gate, out_proj, t - 1, chans, (last,))
            last = got[0]
            sums[t - 1] = exchange(got, "chan")
        if 0 <= t - 2 < steps:
            out = add_up(place, sums[t - 2], out, (blocks, inner, cols), t - 2, (last,))
            last = out if t - 2 == steps - 1 else last
    return out.reshape(rows, cols)


def solution(mesh):
    placed = (
        P(("batch", "seq"), "chan"),
        P(("batch", "seq"), "chan"),
        P(),
        P(),
        P("seq", None),
        P(),
    )
    return jax.shard_map(
        body, mesh=mesh, in_specs=placed, out_specs=P(("batch", "seq"), "chan"), check_vma=False
    )
```

time: 703 us -> 515 us (0.73)
  blocking collectives: 580 us -> 0 us
  Pallas kernels: 0 us -> 171 us
  starting transfers between devices: 0 us -> 156 us
  waiting for transfers between devices: 0 us -> 141 us
  local copies, waits for them, and re-layouts: 73.9 us -> 37.9 us
  matrix products: 33.2 us -> 0 us
  other arithmetic: 14.9 us -> 6.92 us
    all_to_all x4 -> x0, blocking collectives: 580 us -> none  [the longest x1 192 us: body(): lax.all_to_all(first_mixed, 'seq', split_axis=1, concat_axis=0, tiled=True)]
    pallas_call x0 -> x32, Pallas kernels: none -> 171 us  [call(): pl.pallas_call(run, grid_spec=pltpu.PrefetchScalarGridSpec(num_scalar_pre...]
    ppermute x0 -> x56, starting transfers between devices: none -> 156 us  [exchange(): got[m] = lax.ppermute(parts[m], axis, [(d, d ^ m) for d in range(n)])]
    ppermute x0 -> x56, waiting for transfers between devices: none -> 141 us  [exchange(): got[m] = lax.ppermute(parts[m], axis, [(d, d ^ m) for d in range(n)])]
    convert_element_type x3 -> x0, local copies, waits for them, and re-layouts: 37.9 us -> none  [the longest x1 14.9 us: body(): first_mixed = (first_mixed * twiddle[:, :, None]).astype(jnp.bfloat16)]
    dot_general x4 -> x0, matrix products: 33.2 us -> none  [the longest x2 14 us: body(): jnp.dot(columns, weight_rows, preferred_element_type=jnp.float32)]
    select_n x0 -> x1, local copies, waits for them, and re-layouts: none -> 29.8 us  [body(): jnp.where(jnp.eye(sub, dtype=bool)[None, :, None, :], mixer[:, None, :, N...]
    all_to_all x3 -> x0, local copies, waits for them, and re-layouts: 27.6 us -> none  [the longest x1 12.1 us: body(): lax.all_to_all(hidden, 'chan', split_axis=0, concat_axis=1, tiled=True)]
  transfers between devices with their start and end apart: 0 -> 56, of which waited for: 0 -> 17; matrix products, arithmetic and copies ran while one was open for 0% -> 7% of each run, Pallas kernels for 0% -> 31%
where the time goes in v1:
time: 515 us; the launch traced here: 513 us
  Pallas kernels  171 us (33%)
  starting transfers between devices  156 us (30%)
  waiting for transfers between devices  141 us (27%)
  local copies, waits for them, and re-layouts  37.9 us (7%)
  other arithmetic  6.92 us (1%)
    pallas_call x32, Pallas kernels, call(): pl.pallas_call(run, grid_spec=pltpu.PrefetchScalarGridSpec(num_scalar_pre...  171 us
    ppermute x56, starting transfers between devices, exchange(): got[m] = lax.ppermute(parts[m], axis, [(d, d ^ m) for d in range(n)])  156 us
    ppermute x56, waiting for transfers between devices, exchange(): got[m] = lax.ppermute(parts[m], axis, [(d, d ^ m) for d in range(n)])  141 us
    select_n x1, local copies, waits for them, and re-layouts, body(): jnp.where(jnp.eye(sub, dtype=bool)[None, :, None, :], mixer[:, None, :, N...  29.8 us
  transfers between devices with their start and end apart: 56, of which 17 were waited for; matrix products, arithmetic and copies ran while one was open for 7% of the time, Pallas kernels for 31%

profile of v1, /device:TPU:0, one launch (start us, length us, event | category | flops | bytes accessed | tf_op | source)
XLA Modules:
  0.0 513.0 jit_solution(5214020489442052498)
XLA Ops:
  2.7 7.1 %shard_map.64 = (bf16[16,16,512]{2,1,0:T(8,128)(2,1)}, bf16[16,16,512]{2,1,0:T(8,128)(2,1)}, bf16[16,16,512]{2,1,0:T(8,128)(2,1)}, bf16[16,16,512]{2,1,0:T(8,128)(2,1)}) custom-call(s32[2]{0:T(128)} %pad_add_fusion.scalar_ref, bf16[16,512,512]{2,1,0:T(8,128)(2,1)} %bitcast.15, bf16[512,512]{1,0:T(8,128)(2,1)} %refs_1_.15, f32[4,512,4]{2,1,0:T(8,128)} %bitcast.31), custom_call_target="tpu_custom_call" | custom-call | flops 536870912 | bytes 9437184 | tf_op jit(solution)/shard_map/pallas_call | solution.py:22
  15.5 6.5 %shard_map.65 = (bf16[16,16,512]{2,1,0:T(8,128)(2,1)}, bf16[16,16,512]{2,1,0:T(8,128)(2,1)}, bf16[16,16,512]{2,1,0:T(8,128)(2,1)}, bf16[16,16,512]{2,1,0:T(8,128)(2,1)}) custom-call(s32[2]{0:T(128)} %pad_add_fusion.scalar_ref, bf16[16,512,512]{2,1,0:T(8,128)(2,1)} %bitcast.16, bf16[512,512]{1,0:T(8,128)(2,1)} %refs_1_.15, f32[4,512,4]{2,1,0:T(8,128)} %bitcast.32, ...), custom_call_target="tpu_custom_call" | custom-call | flops 536870912 | bytes 9437184 | tf_op jit(solution)/shard_map/pallas_call | solution.py:22
  27.1 6.1 %broadcast_select_fusion = bf16[64,16,64,16]{3,2,1,0:T(8,128)(2,1)} fusion(pred[16,16]{1,0:T(8,128)(4,1)S(1)} %iota_compare_fusion, bf16[64,64]{1,0:T(8,128)(2,1)S(1)} %broadcast_in_dim.24), kind=kLoop, calls=%fused_computation | loop fusion | flops 1048576 | bytes 2105600 | tf_op jit(solution)/shard_map/jit(_where)/select_n | solution.py:208
  33.2 29.8 %select_n.49.refs_4_ = bf16[1024,1024]{1,0:T(8,128)(2,1)} reshape(bf16[64,16,64,16]{3,2,1,0:T(8,128)(2,1)} %broadcast_select_fusion) | data formatting | bytes 4194304 | tf_op jit(solution)/shard_map/jit(_where)/select_n | solution.py:208
  73.8 6.5 %shard_map.67 = (bf16[16,16,512]{2,1,0:T(8,128)(2,1)}, bf16[16,16,512]{2,1,0:T(8,128)(2,1)}, bf16[16,16,512]{2,1,0:T(8,128)(2,1)}, bf16[16,16,512]{2,1,0:T(8,128)(2,1)}) custom-call(s32[2]{0:T(128)} %pad_add_fusion.scalar_ref, bf16[16,512,512]{2,1,0:T(8,128)(2,1)} %bitcast.17, bf16[512,512]{1,0:T(8,128)(2,1)} %refs_1_.15, f32[4,512,4]{2,1,0:T(8,128)} %bitcast.33, ...), custom_call_target="tpu_custom_call" | custom-call | flops 536870912 | bytes 9437184 | tf_op jit(solution)/shard_map/pallas_call | solution.py:22
  89.5 6.6 %collective-permute-done.16.refs_2_ = bf16[16,16,512]{2,1,0:T(8,128)(2,1)S(1)} collective-permute-done((bf16[16,16,512]{2,1,0:T(8,128)(2,1)}, bf16[16,16,512]{2,1,0:T(8,128)(2,1)S(1)}, u32[]{:S(2)}, u32[]{:S(2)}) %collective-permute-start.16) | collective-permute-done | bytes 262176 | tf_op jit(solution)/shard_map/ppermute | solution.py:187
  96.3 6.5 %shard_map.69 = (bf16[16,16,512]{2,1,0:T(8,128)(2,1)}, bf16[16,16,512]{2,1,0:T(8,128)(2,1)}, bf16[16,16,512]{2,1,0:T(8,128)(2,1)}, bf16[16,16,512]{2,1,0:T(8,128)(2,1)}) custom-call(s32[2]{0:T(128)} %pad_add_fusion.scalar_ref, bf16[16,512,512]{2,1,0:T(8,128)(2,1)} %bitcast.18, bf16[512,512]{1,0:T(8,128)(2,1)} %refs_1_.15, f32[4,512,4]{2,1,0:T(8,128)} %bitcast.34, ...), custom_call_target="tpu_custom_call" | custom-call | flops 536870912 | bytes 9437184 | tf_op jit(solution)/shard_map/pallas_call | solution.py:22
  102.8 26.7 %collective-permute-start.9 = (bf16[16,16,512]{2,1,0:T(8,128)(2,1)S(1)}, bf16[16,16,512]{2,1,0:T(8,128)(2,1)S(1)}, u32[]{:S(2)}, u32[]{:S(2)}) collective-permute-start(bf16[16,16,512]{2,1,0:T(8,128)(2,1)S(1)} %copy-done.58), channel_id=1, source_target_pairs={{0,8},{8,0},{16,24},{24,16},{1,9},{9,1},{17,25},{25,17},{2,10},{10... | collective-permute-start | bytes 786440 | tf_op jit(solution)/shard_map/ppermute | solution.py:187
  144.7 11.3 %collective-permute-start.27 = (bf16[16,16,512]{2,1,0:T(8,128)(2,1)}, bf16[16,16,512]{2,1,0:T(8,128)(2,1)S(1)}, u32[]{:S(2)}, u32[]{:S(2)}) collective-permute-start(bf16[16,16,512]{2,1,0:T(8,128)(2,1)} %get-tuple-element.124), channel_id=1, source_target_pairs={{0,8},{8,0},{16,24},{24,16},{1,9},{9,1},{17,25},{25,17},{2,10},{10... | collective-permute-start | bytes 786440 | tf_op jit(solution)/shard_map/ppermute | solution.py:187
  156.0 6.5 %shard_map.72 = (bf16[16,16,512]{2,1,0:T(8,128)(2,1)}, bf16[16,16,512]{2,1,0:T(8,128)(2,1)}, bf16[16,16,512]{2,1,0:T(8,128)(2,1)}, bf16[16,16,512]{2,1,0:T(8,128)(2,1)}) custom-call(s32[2]{0:T(128)} %pad_add_fusion.scalar_ref, bf16[16,512,512]{2,1,0:T(8,128)(2,1)} %bitcast.19, bf16[512,512]{1,0:T(8,128)(2,1)} %refs_1_.15, f32[4,512,4]{2,1,0:T(8,128)} %bitcast.35, ...), custom_call_target="tpu_custom_call" | custom-call | flops 536870912 | bytes 9437184 | tf_op jit(solution)/shard_map/pallas_call | solution.py:22
  171.9 9.2 %collective-permute-start.25 = (bf16[16,16,512]{2,1,0:T(8,128)(2,1)S(1)}, bf16[16,16,512]{2,1,0:T(8,128)(2,1)S(1)}, u32[]{:S(2)}, u32[]{:S(2)}) collective-permute-start(bf16[16,16,512]{2,1,0:T(8,128)(2,1)S(1)} %copy-done.60), channel_id=1, source_target_pairs={{0,16},{8,24},{16,0},{24,8},{1,17},{9,25},{17,1},{25,9},{2,18},{10... | collective-permute-start | bytes 786440 | tf_op jit(solution)/shard_map/ppermute | solution.py:187
  204.4 6.5 %shard_map.75 = (bf16[16,16,512]{2,1,0:T(8,128)(2,1)}, bf16[16,16,512]{2,1,0:T(8,128)(2,1)}, bf16[16,16,512]{2,1,0:T(8,128)(2,1)}, bf16[16,16,512]{2,1,0:T(8,128)(2,1)}) custom-call(s32[2]{0:T(128)} %pad_add_fusion.scalar_ref, bf16[16,512,512]{2,1,0:T(8,128)(2,1)} %bitcast.20, bf16[512,512]{1,0:T(8,128)(2,1)} %refs_1_.15, f32[4,512,4]{2,1,0:T(8,128)} %bitcast.36, ...), custom_call_target="tpu_custom_call" | custom-call | flops 536870912 | bytes 9437184 | tf_op jit(solution)/shard_map/pallas_call | solution.py:22
  210.9 7.0 %collective-permute-done.25.refs_2_ = bf16[16,16,512]{2,1,0:T(8,128)(2,1)S(1)} collective-permute-done((bf16[16,16,512]{2,1,0:T(8,128)(2,1)S(1)}, bf16[16,16,512]{2,1,0:T(8,128)(2,1)S(1)}, u32[]{:S(2)}, u32[]{:S(2)}) %collective-permute-start.25) | collective-permute-done | bytes 262176 | tf_op jit(solution)/shard_map/ppermute | solution.py:187
  245.5 6.5 %shard_map.78 = (bf16[16,16,512]{2,1,0:T(8,128)(2,1)}, bf16[16,16,512]{2,1,0:T(8,128)(2,1)}, bf16[16,16,512]{2,1,0:T(8,128)(2,1)}, bf16[16,16,512]{2,1,0:T(8,128)(2,1)}) custom-call(s32[2]{0:T(128)} %pad_add_fusion.scalar_ref, bf16[16,512,512]{2,1,0:T(8,128)(2,1)} %bitcast.21, bf16[512,512]{1,0:T(8,128)(2,1)} %refs_1_.15, f32[4,512,4]{2,1,0:T(8,128)} %bitcast.37, ...), custom_call_target="tpu_custom_call" | custom-call | flops 536870912 | bytes 9437184 | tf_op jit(solution)/shard_map/pallas_call | solution.py:22
  255.9 7.0 %collective-permute-done.19.refs_2_ = bf16[16,16,512]{2,1,0:T(8,128)(2,1)S(1)} collective-permute-done((bf16[16,16,512]{2,1,0:T(8,128)(2,1)}, bf16[16,16,512]{2,1,0:T(8,128)(2,1)S(1)}, u32[]{:S(2)}, u32[]{:S(2)}) %collective-permute-start.19) | collective-permute-done | bytes 262176 | tf_op jit(solution)/shard_map/ppermute | solution.py:187
  282.8 9.1 %collective-permute-start.34 = (bf16[16,16,512]{2,1,0:T(8,128)(2,1)}, bf16[16,16,512]{2,1,0:T(8,128)(2,1)S(1)}, u32[]{:S(2)}, u32[]{:S(2)}) collective-permute-start(bf16[16,16,512]{2,1,0:T(8,128)(2,1)} %get-tuple-element.137), channel_id=1, source_target_pairs={{0,16},{8,24},{16,0},{24,8},{1,17},{9,25},{17,1},{25,9},{2,18},{10... | collective-permute-start | bytes 786440 | tf_op jit(solution)/shard_map/ppermute | solution.py:187
  295.7 6.5 %shard_map.81 = (bf16[16,16,512]{2,1,0:T(8,128)(2,1)}, bf16[16,16,512]{2,1,0:T(8,128)(2,1)}, bf16[16,16,512]{2,1,0:T(8,128)(2,1)}, bf16[16,16,512]{2,1,0:T(8,128)(2,1)}) custom-call(s32[2]{0:T(128)} %pad_add_fusion.scalar_ref, bf16[16,512,512]{2,1,0:T(8,128)(2,1)} %bitcast.22, bf16[512,512]{1,0:T(8,128)(2,1)} %refs_1_.15, f32[4,512,4]{2,1,0:T(8,128)} %bitcast.38, ...), custom_call_target="tpu_custom_call" | custom-call | flops 536870912 | bytes 9437184 | tf_op jit(solution)/shard_map/pallas_call | solution.py:22
  316.8 13.5 %collective-permute-done.34.refs_2_ = bf16[16,16,512]{2,1,0:T(8,128)(2,1)S(1)} collective-permute-done((bf16[16,16,512]{2,1,0:T(8,128)(2,1)}, bf16[16,16,512]{2,1,0:T(8,128)(2,1)S(1)}, u32[]{:S(2)}, u32[]{:S(2)}) %collective-permute-start.34) | collective-permute-done | bytes 262176 | tf_op jit(solution)/shard_map/ppermute | solution.py:187
  380.4 10.4 %collective-permute-done.43.refs_2_ = bf16[16,16,512]{2,1,0:T(8,128)(2,1)S(1)} collective-permute-done((bf16[16,16,512]{2,1,0:T(8,128)(2,1)}, bf16[16,16,512]{2,1,0:T(8,128)(2,1)S(1)}, u32[]{:S(2)}, u32[]{:S(2)}) %collective-permute-start.43) | collective-permute-done | bytes 262176 | tf_op jit(solution)/shard_map/ppermute | solution.py:187
  415.9 8.1 %collective-permute-done.52.refs_1_ = bf16[16,64,512]{2,1,0:T(8,128)(2,1)S(1)} collective-permute-done((bf16[16,64,512]{2,1,0:T(8,128)(2,1)}, bf16[16,64,512]{2,1,0:T(8,128)(2,1)S(1)}, u32[]{:S(2)}, u32[]{:S(2)}) %collective-permute-start.52) | collective-permute-done | bytes 1048608 | tf_op jit(solution)/shard_map/ppermute | solution.py:187
  429.2 17.2 %collective-permute-done.51.refs_1_ = bf16[16,64,512]{2,1,0:T(8,128)(2,1)S(1)} collective-permute-done((bf16[16,64,512]{2,1,0:T(8,128)(2,1)}, bf16[16,64,512]{2,1,0:T(8,128)(2,1)S(1)}, u32[]{:S(2)}, u32[]{:S(2)}) %collective-permute-start.51) | collective-permute-done | bytes 1048608 | tf_op jit(solution)/shard_map/ppermute | solution.py:187
  451.7 17.2 %collective-permute-done.50.refs_1_ = bf16[16,64,512]{2,1,0:T(8,128)(2,1)S(1)} collective-permute-done((bf16[16,64,512]{2,1,0:T(8,128)(2,1)}, bf16[16,64,512]{2,1,0:T(8,128)(2,1)S(1)}, u32[]{:S(2)}, u32[]{:S(2)}) %collective-permute-start.50) | collective-permute-done | bytes 1048608 | tf_op jit(solution)/shard_map/ppermute | solution.py:187
  474.2 17.2 %collective-permute-done.49.refs_1_ = bf16[16,64,512]{2,1,0:T(8,128)(2,1)S(1)} collective-permute-done((bf16[16,64,512]{2,1,0:T(8,128)(2,1)}, bf16[16,64,512]{2,1,0:T(8,128)(2,1)S(1)}, u32[]{:S(2)}, u32[]{:S(2)}) %collective-permute-start.49) | collective-permute-done | bytes 1048608 | tf_op jit(solution)/shard_map/ppermute | solution.py:187
  496.6 12.1 %collective-permute-done.48.refs_1_ = bf16[16,64,512]{2,1,0:T(8,128)(2,1)} collective-permute-done((bf16[16,64,512]{2,1,0:T(8,128)(2,1)}, bf16[16,64,512]{2,1,0:T(8,128)(2,1)}, u32[]{:S(2)}, u32[]{:S(2)}) %collective-permute-start.48) | collective-permute-done | bytes 1048608 | tf_op jit(solution)/shard_map/ppermute | solution.py:187
  (269 shorter events, 251.6 us)
Async XLA Ops:
  9.8 53.2 %collective-permute-start.3 = (bf16[16,16,512]{2,1,0:T(8,128)(2,1)}, bf16[16,16,512]{2,1,0:T(8,128)(2,1)S(1)}, u32[]{:S(2)}, u32[]{:S(2)}) collective-permute-start(bf16[16,16,512]{2,1,0:T(8,128)(2,1)} %get-tuple-element.90), channel_id=1, source_target_pairs={{0,8},{8,0},{16,24},{24,16},{1,9},{9,1},{17,25},{25,17},{2,10},{10... | collective-permute-start | bytes 786440 | tf_op jit(solution)/shard_map/ppermute | solution.py:187
  12.9 50.2 %collective-permute-start.4 = (bf16[16,16,512]{2,1,0:T(8,128)(2,1)}, bf16[16,16,512]{2,1,0:T(8,128)(2,1)S(1)}, u32[]{:S(2)}, u32[]{:S(2)}) collective-permute-start(bf16[16,16,512]{2,1,0:T(8,128)(2,1)} %get-tuple-element.91), channel_id=1, source_target_pairs={{0,16},{8,24},{16,0},{24,8},{1,17},{9,25},{17,1},{25,9},{2,18},{10... | collective-permute-start | bytes 786440 | tf_op jit(solution)/shard_map/ppermute | solution.py:187
  15.5 47.7 %collective-permute-start.5 = (bf16[16,16,512]{2,1,0:T(8,128)(2,1)}, bf16[16,16,512]{2,1,0:T(8,128)(2,1)S(1)}, u32[]{:S(2)}, u32[]{:S(2)}) collective-permute-start(bf16[16,16,512]{2,1,0:T(8,128)(2,1)} %get-tuple-element.92), channel_id=1, source_target_pairs={{0,24},{8,16},{16,8},{24,0},{1,25},{9,17},{17,9},{25,1},{2,26},{10... | collective-permute-start | bytes 786440 | tf_op jit(solution)/shard_map/ppermute | solution.py:187
  21.9 51.8 %collective-permute-start = (bf16[16,16,512]{2,1,0:T(8,128)(2,1)}, bf16[16,16,512]{2,1,0:T(8,128)(2,1)S(1)}, u32[]{:S(2)}, u32[]{:S(2)}) collective-permute-start(bf16[16,16,512]{2,1,0:T(8,128)(2,1)} %get-tuple-element.87), channel_id=1, source_target_pairs={{0,8},{8,0},{16,24},{24,16},{1,9},{9,1},{17,25},{25,17},{2,10},{10... | collective-permute-start | bytes 786440 | tf_op jit(solution)/shard_map/ppermute | solution.py:187
  22.8 57.4 %collective-permute-start.1 = (bf16[16,16,512]{2,1,0:T(8,128)(2,1)}, bf16[16,16,512]{2,1,0:T(8,128)(2,1)S(1)}, u32[]{:S(2)}, u32[]{:S(2)}) collective-permute-start(bf16[16,16,512]{2,1,0:T(8,128)(2,1)} %get-tuple-element.88), channel_id=1, source_target_pairs={{0,16},{8,24},{16,0},{24,8},{1,17},{9,25},{17,1},{25,9},{2,18},{10... | collective-permute-start | bytes 786440 | tf_op jit(solution)/shard_map/ppermute | solution.py:187
  80.9 54.3 %collective-permute-start.13 = (bf16[16,16,512]{2,1,0:T(8,128)(2,1)}, bf16[16,16,512]{2,1,0:T(8,128)(2,1)S(1)}, u32[]{:S(2)}, u32[]{:S(2)}) collective-permute-start(bf16[16,16,512]{2,1,0:T(8,128)(2,1)} %get-tuple-element.104), channel_id=1, source_target_pairs={{0,16},{8,24},{16,0},{24,8},{1,17},{9,25},{17,1},{25,9},{2,18},{10... | collective-permute-start | bytes 786440 | tf_op jit(solution)/shard_map/ppermute | solution.py:187
  84.7 50.7 %collective-permute-start.14 = (bf16[16,16,512]{2,1,0:T(8,128)(2,1)}, bf16[16,16,512]{2,1,0:T(8,128)(2,1)S(1)}, u32[]{:S(2)}, u32[]{:S(2)}) collective-permute-start(bf16[16,16,512]{2,1,0:T(8,128)(2,1)} %get-tuple-element.105), channel_id=1, source_target_pairs={{0,24},{8,16},{16,8},{24,0},{1,25},{9,17},{17,9},{25,1},{2,26},{10... | collective-permute-start | bytes 786440 | tf_op jit(solution)/shard_map/ppermute | solution.py:187
  96.2 47.5 %collective-permute-start.10 = (bf16[16,16,512]{2,1,0:T(8,128)(2,1)}, bf16[16,16,512]{2,1,0:T(8,128)(2,1)S(1)}, u32[]{:S(2)}, u32[]{:S(2)}) collective-permute-start(bf16[16,16,512]{2,1,0:T(8,128)(2,1)} %get-tuple-element.101), channel_id=1, source_target_pairs={{0,16},{8,24},{16,0},{24,8},{1,17},{9,25},{17,1},{25,9},{2,18},{10... | collective-permute-start | bytes 786440 | tf_op jit(solution)/shard_map/ppermute | solution.py:187
  96.2 48.5 %collective-permute-start.11 = (bf16[16,16,512]{2,1,0:T(8,128)(2,1)}, bf16[16,16,512]{2,1,0:T(8,128)(2,1)S(1)}, u32[]{:S(2)}, u32[]{:S(2)}) collective-permute-start(bf16[16,16,512]{2,1,0:T(8,128)(2,1)} %get-tuple-element.102), channel_id=1, source_target_pairs={{0,24},{8,16},{16,8},{24,0},{1,25},{9,17},{17,9},{25,1},{2,26},{10... | collective-permute-start | bytes 786440 | tf_op jit(solution)/shard_map/ppermute | solution.py:187
  102.8 53.2 %collective-permute-start.9 = (bf16[16,16,512]{2,1,0:T(8,128)(2,1)S(1)}, bf16[16,16,512]{2,1,0:T(8,128)(2,1)S(1)}, u32[]{:S(2)}, u32[]{:S(2)}) collective-permute-start(bf16[16,16,512]{2,1,0:T(8,128)(2,1)S(1)} %copy-done.58), channel_id=1, source_target_pairs={{0,8},{8,0},{16,24},{24,16},{1,9},{9,1},{17,25},{25,17},{2,10},{10... | collective-permute-start | bytes 786440 | tf_op jit(solution)/shard_map/ppermute | solution.py:187
  171.9 45.9 %collective-permute-start.25 = (bf16[16,16,512]{2,1,0:T(8,128)(2,1)S(1)}, bf16[16,16,512]{2,1,0:T(8,128)(2,1)S(1)}, u32[]{:S(2)}, u32[]{:S(2)}) collective-permute-start(bf16[16,16,512]{2,1,0:T(8,128)(2,1)S(1)} %copy-done.60), channel_id=1, source_target_pairs={{0,16},{8,24},{16,0},{24,8},{1,17},{9,25},{17,1},{25,9},{2,18},{10... | collective-permute-start | bytes 786440 | tf_op jit(solution)/shard_map/ppermute | solution.py:187
  195.4 44.9 %collective-permute-start.22 = (bf16[16,16,512]{2,1,0:T(8,128)(2,1)}, bf16[16,16,512]{2,1,0:T(8,128)(2,1)S(1)}, u32[]{:S(2)}, u32[]{:S(2)}) collective-permute-start(bf16[16,16,512]{2,1,0:T(8,128)(2,1)} %get-tuple-element.119), channel_id=1, source_target_pairs={{0,16},{8,24},{16,0},{24,8},{1,17},{9,25},{17,1},{25,9},{2,18},{10... | collective-permute-start | bytes 786440 | tf_op jit(solution)/shard_map/ppermute | solution.py:187
  217.9 45.0 %collective-permute-start.19 = (bf16[16,16,512]{2,1,0:T(8,128)(2,1)}, bf16[16,16,512]{2,1,0:T(8,128)(2,1)S(1)}, u32[]{:S(2)}, u32[]{:S(2)}) collective-permute-start(bf16[16,16,512]{2,1,0:T(8,128)(2,1)} %get-tuple-element.116), channel_id=1, source_target_pairs={{0,16},{8,24},{16,0},{24,8},{1,17},{9,25},{17,1},{25,9},{2,18},{10... | collective-permute-start | bytes 786440 | tf_op jit(solution)/shard_map/ppermute | solution.py:187
  240.3 42.4 %collective-permute-start.40 = (bf16[16,16,512]{2,1,0:T(8,128)(2,1)}, bf16[16,16,512]{2,1,0:T(8,128)(2,1)S(1)}, u32[]{:S(2)}, u32[]{:S(2)}) collective-permute-start(bf16[16,16,512]{2,1,0:T(8,128)(2,1)} %get-tuple-element.143), channel_id=1, source_target_pairs={{0,16},{8,24},{16,0},{24,8},{1,17},{9,25},{17,1},{25,9},{2,18},{10... | collective-permute-start | bytes 786440 | tf_op jit(solution)/shard_map/ppermute | solution.py:187
  262.9 44.9 %collective-permute-start.37 = (bf16[16,16,512]{2,1,0:T(8,128)(2,1)}, bf16[16,16,512]{2,1,0:T(8,128)(2,1)S(1)}, u32[]{:S(2)}, u32[]{:S(2)}) collective-permute-start(bf16[16,16,512]{2,1,0:T(8,128)(2,1)} %get-tuple-element.140), channel_id=1, source_target_pairs={{0,16},{8,24},{16,0},{24,8},{1,17},{9,25},{17,1},{25,9},{2,18},{10... | collective-permute-start | bytes 786440 | tf_op jit(solution)/shard_map/ppermute | solution.py:187
  282.8 47.5 %collective-permute-start.34 = (bf16[16,16,512]{2,1,0:T(8,128)(2,1)}, bf16[16,16,512]{2,1,0:T(8,128)(2,1)S(1)}, u32[]{:S(2)}, u32[]{:S(2)}) collective-permute-start(bf16[16,16,512]{2,1,0:T(8,128)(2,1)} %get-tuple-element.137), channel_id=1, source_target_pairs={{0,16},{8,24},{16,0},{24,8},{1,17},{9,25},{17,1},{25,9},{2,18},{10... | collective-permute-start | bytes 786440 | tf_op jit(solution)/shard_map/ppermute | solution.py:187
  291.9 39.9 %collective-permute-start.35 = (bf16[16,16,512]{2,1,0:T(8,128)(2,1)}, bf16[16,16,512]{2,1,0:T(8,128)(2,1)S(1)}, u32[]{:S(2)}, u32[]{:S(2)}) collective-permute-start(bf16[16,16,512]{2,1,0:T(8,128)(2,1)} %get-tuple-element.138), channel_id=1, source_target_pairs={{0,24},{8,16},{16,8},{24,0},{1,25},{9,17},{17,9},{25,1},{2,26},{10... | collective-permute-start | bytes 786440 | tf_op jit(solution)/shard_map/ppermute | solution.py:187
  330.2 62.6 %collective-permute-start.55 = (bf16[16,64,512]{2,1,0:T(8,128)(2,1)}, bf16[16,64,512]{2,1,0:T(8,128)(2,1)S(1)}, u32[]{:S(2)}, u32[]{:S(2)}) collective-permute-start(bf16[16,64,512]{2,1,0:T(8,128)(2,1)} %get-tuple-element.164), channel_id=1, source_target_pairs={{0,4},{4,0},{1,5},{5,1},{2,6},{6,2},{3,7},{7,3},{8,12},{12,8},{9,1... | collective-permute-start | bytes 3145736 | tf_op jit(solution)/shard_map/ppermute | solution.py:187
  331.7 62.6 %collective-permute-start.54 = (bf16[16,64,512]{2,1,0:T(8,128)(2,1)}, bf16[16,64,512]{2,1,0:T(8,128)(2,1)S(1)}, u32[]{:S(2)}, u32[]{:S(2)}) collective-permute-start(bf16[16,64,512]{2,1,0:T(8,128)(2,1)} %get-tuple-element.163), channel_id=1, source_target_pairs={{0,4},{4,0},{1,5},{5,1},{2,6},{6,2},{3,7},{7,3},{8,12},{12,8},{9,1... | collective-permute-start | bytes 3145736 | tf_op jit(solution)/shard_map/ppermute | solution.py:187
  332.3 69.2 %collective-permute-start.53 = (bf16[16,64,512]{2,1,0:T(8,128)(2,1)}, bf16[16,64,512]{2,1,0:T(8,128)(2,1)S(1)}, u32[]{:S(2)}, u32[]{:S(2)}) collective-permute-start(bf16[16,64,512]{2,1,0:T(8,128)(2,1)} %get-tuple-element.162), channel_id=1, source_target_pairs={{0,4},{4,0},{1,5},{5,1},{2,6},{6,2},{3,7},{7,3},{8,12},{12,8},{9,1... | collective-permute-start | bytes 3145736 | tf_op jit(solution)/shard_map/ppermute | solution.py:187
  392.3 54.1 %collective-permute-start.51 = (bf16[16,64,512]{2,1,0:T(8,128)(2,1)}, bf16[16,64,512]{2,1,0:T(8,128)(2,1)S(1)}, u32[]{:S(2)}, u32[]{:S(2)}) collective-permute-start(bf16[16,64,512]{2,1,0:T(8,128)(2,1)} %get-tuple-element.160), channel_id=1, source_target_pairs={{0,4},{4,0},{1,5},{5,1},{2,6},{6,2},{3,7},{7,3},{8,12},{12,8},{9,1... | collective-permute-start | bytes 3145736 | tf_op jit(solution)/shard_map/ppermute | solution.py:187
  392.9 76.0 %collective-permute-start.50 = (bf16[16,64,512]{2,1,0:T(8,128)(2,1)}, bf16[16,64,512]{2,1,0:T(8,128)(2,1)S(1)}, u32[]{:S(2)}, u32[]{:S(2)}) collective-permute-start(bf16[16,64,512]{2,1,0:T(8,128)(2,1)} %get-tuple-element.159), channel_id=1, source_target_pairs={{0,4},{4,0},{1,5},{5,1},{2,6},{6,2},{3,7},{7,3},{8,12},{12,8},{9,1... | collective-permute-start | bytes 3145736 | tf_op jit(solution)/shard_map/ppermute | solution.py:187
  394.4 97.0 %collective-permute-start.49 = (bf16[16,64,512]{2,1,0:T(8,128)(2,1)}, bf16[16,64,512]{2,1,0:T(8,128)(2,1)S(1)}, u32[]{:S(2)}, u32[]{:S(2)}) collective-permute-start(bf16[16,64,512]{2,1,0:T(8,128)(2,1)} %get-tuple-element.158), channel_id=1, source_target_pairs={{0,4},{4,0},{1,5},{5,1},{2,6},{6,2},{3,7},{7,3},{8,12},{12,8},{9,1... | collective-permute-start | bytes 3145736 | tf_op jit(solution)/shard_map/ppermute | solution.py:187
  401.5 107.2 %collective-permute-start.48 = (bf16[16,64,512]{2,1,0:T(8,128)(2,1)}, bf16[16,64,512]{2,1,0:T(8,128)(2,1)}, u32[]{:S(2)}, u32[]{:S(2)}) collective-permute-start(bf16[16,64,512]{2,1,0:T(8,128)(2,1)} %get-tuple-element.157), channel_id=1, source_target_pairs={{0,4},{4,0},{1,5},{5,1},{2,6},{6,2},{3,7},{7,3},{8,12},{12,8},{9,1... | collective-permute-start | bytes 3145736 | tf_op jit(solution)/shard_map/ppermute | solution.py:187
  (100 other events, 2111.0 us)

commit v2 on v1

v2 whole, which is shorter than its diff:
```python
import functools

import jax
import jax.numpy as jnp
from jax import lax
from jax.experimental import pallas as pl
from jax.experimental.pallas import tpu as pltpu
from jax.sharding import PartitionSpec as P

ROWS = 16
PER_A = 4
PER_C = 8
PER_D = 8
WIDTH = 512
TAIL = 2
ORDER = 'ABGP'
LEAD = 2
ZORDER = (3, 2, 1)
LAG = 3
COST = 1
VMEM = 56 * 1024 * 1024
BF16 = jnp.bfloat16
F32 = jnp.float32
ANY = pl.BlockSpec(memory_space=pl.ANY)


def call(kernel, grid, in_specs, out_specs, out_shape, scalar, args, deps=(), scratch=(), aliases=None, flops=0, nbytes=0):
    def run(scalar_ref, *refs):
        n = len(args)
        kernel(scalar_ref, refs[:n], refs[n + len(deps) :])

    return pl.pallas_call(
        run,
        grid_spec=pltpu.PrefetchScalarGridSpec(
            num_scalar_prefetch=1,
            grid=grid,
            in_specs=list(in_specs) + [ANY] * len(deps),
            out_specs=out_specs,
            scratch_shapes=list(scratch),
        ),
        out_shape=out_shape,
        input_output_aliases=aliases or {},
        compiler_params=pltpu.CompilerParams(vmem_limit_bytes=VMEM),
        cost_estimate=pl.CostEstimate(flops=int(flops * COST), bytes_accessed=int(nbytes * COST), transcendentals=0),
    )(scalar, *args, *deps)


def first_factor(place, tokens, weights, twiddle, steps, size, seqs, deps):
    blocks, inner, cols = tokens.shape
    sub = size // seqs
    per = min(PER_A, blocks)
    n = len(steps)
    low = steps[0] * size

    def kernel(place_ref, ins, outs):
        tok, wt, tw = ins
        outs, lhs, turned = outs[:-2], outs[-2], outs[-1]
        me = place_ref[0]
        g = pl.program_id(0)

        @pl.when(g == 0)
        def _():
            for k in range(n):
                for m in range(seqs):
                    at = pl.ds(pl.multiple_of(low + k * size + (me ^ m) * sub, sub), sub)
                    lhs[k * size + m * sub : k * size + (m + 1) * sub, :] = wt[at, :]

        turned[...] = tw[...].T
        for k in range(n):
            rows = jnp.concatenate(
                [
                    turned[pl.ds(pl.multiple_of(low + k * size + (me ^ m) * sub, sub), sub), :]
                    for m in range(seqs)
                ],
                axis=0,
            )
            for b in range(per):
                got = jnp.dot(lhs[k * size : (k + 1) * size, :], tok[b], preferred_element_type=F32)
                got = (got * rows[:, b : b + 1]).astype(BF16)
                for m in range(seqs):
                    outs[k * seqs + m][b] = got[m * sub : (m + 1) * sub]

    return call(
        kernel,
        (blocks // per,),
        [
            pl.BlockSpec((per, inner, cols), lambda g, p: (g, 0, 0)),
            pl.BlockSpec((inner, inner), lambda g, p: (0, 0)),
            pl.BlockSpec((None, per, inner), lambda g, p: (g, 0, 0)),
        ],
        [pl.BlockSpec((per, sub, cols), lambda g, p: (g, 0, 0))] * (n * seqs),
        [jax.ShapeDtypeStruct((blocks, sub, cols), BF16)] * (n * seqs),
        place,
        (tokens, weights, twiddle.reshape(blocks // per, per, inner)),
        deps,
        scratch=[pltpu.VMEM((n * size, inner), BF16), pltpu.VMEM((inner, per), F32)],
        flops=2 * blocks * n * size * inner * cols,
        nbytes=2 * blocks * cols * (inner + n * size),
    )


def spread_out(place, mixer, blocks, sub, seqs, deps):
    order = mixer.shape[0]
    height = order * sub
    here = blocks * sub
    tall = min(height, 1024)

    def source(rows, me):
        return ((rows // here) ^ me) * blocks + (rows % here) // sub

    def kernel(place_ref, ins, outs):
        me = place_ref[0]
        base = pl.program_id(0) * tall
        down = lax.broadcasted_iota(jnp.int32, (tall, order), 0) + base
        left = (source(down, me) == lax.broadcasted_iota(jnp.int32, (tall, order), 1)).astype(BF16)
        over = lax.broadcasted_iota(jnp.int32, (order, height), 1)
        right = (source(over, me) == lax.broadcasted_iota(jnp.int32, (order, height), 0)).astype(BF16)
        some = jnp.dot(left, ins[0][...], preferred_element_type=F32).astype(BF16)
        full = jnp.dot(some, right, preferred_element_type=F32).astype(BF16)
        same = (lax.broadcasted_iota(jnp.int32, (tall, height), 0) % sub) == (
            lax.broadcasted_iota(jnp.int32, (tall, height), 1) % sub
        )
        outs[0][...] = jnp.where(same, full, jnp.zeros_like(full))

    return call(
        kernel,
        (height // tall,),
        [pl.BlockSpec((order, order), lambda g, p: (0, 0))],
        [pl.BlockSpec((tall, height), lambda g, p: (g, 0))],
        [jax.ShapeDtypeStruct((height, height), BF16)],
        place,
        (mixer,),
        deps,
        flops=2 * height * height * order,
        nbytes=2 * height * height,
    )[0]


def second_factor(place, parts, spread, cuts, deps):
    seqs = len(parts)
    blocks, sub, cols = parts[0].shape
    height = blocks * sub
    width = min(cols, WIDTH)

    def kernel(place_ref, ins, outs):
        sp = ins[-1]
        rhs = [ins[m][...].reshape(height, width) for m in range(seqs)]
        for o in range(seqs):
            total = None
            for m in range(seqs):
                term = jnp.dot(
                    sp[o * height : (o + 1) * height, m * height : (m + 1) * height],
                    rhs[m],
                    preferred_element_type=F32,
                )
                total = term if total is None else total + term
            got = total.astype(BF16).reshape(blocks, sub, width)
            for c in range(cuts):
                outs[c * seqs + o][...] = got[c * some : (c + 1) * some]

    some = blocks // cuts
    spec = pl.BlockSpec((blocks, sub, width), lambda g, p: (0, 0, g))
    out = pl.BlockSpec((some, sub, width), lambda g, p: (0, 0, g))
    return call(
        kernel,
        (cols // width,),
        [spec] * seqs + [pl.BlockSpec(spread.shape, lambda g, p: (0, 0))],
        [out] * (seqs * cuts),
        [jax.ShapeDtypeStruct((some, sub, cols), BF16)] * (seqs * cuts),
        place,
        (*parts, spread),
        deps,
        flops=2 * (seqs * height) ** 2 * cols,
        nbytes=4 * seqs * height * cols,
    )


def gate_project(place, parts, gate, proj, step, cut, chans, deps):
    seqs = len(parts)
    blocks, sub, cols = parts[0].shape
    size = seqs * sub
    per = min(PER_C, blocks)

    def kernel(place_ref, ins, outs):
        got, gt, ws = ins[:seqs], ins[seqs], ins[seqs + 1 :]
        outs, hidden = outs[:-1], outs[-1]
        me = place_ref[0]
        for m in range(seqs):
            rows = pl.ds(pl.multiple_of((me ^ m) * sub, sub), sub)
            hidden[:, rows, :] = (got[m][...].astype(F32) * gt[:, rows, :].astype(F32)).astype(BF16)
        lhs = hidden[...].reshape(per * size, cols)
        for q in range(chans):
            term = jnp.dot(lhs, ws[q][...], preferred_element_type=F32)
            outs[q][...] = term.astype(BF16).reshape(per, size, cols)

    out = pl.BlockSpec((per, size, cols), lambda g, p: (g, 0, 0))
    return call(
        kernel,
        (blocks // per,),
        [pl.BlockSpec((per, sub, cols), lambda g, p: (g, 0, 0))] * seqs
        + [pl.BlockSpec((per, size, cols), lambda g, p: (cut * (blocks // per) + g, step, 0))]
        + [pl.BlockSpec((cols, cols), functools.partial(lambda q, g, p: (p[1], p[1] ^ q), q)) for q in range(chans)],
        [out] * chans,
        [jax.ShapeDtypeStruct((blocks, size, cols), BF16)] * chans,
        place,
        (*parts, gate) + (proj,) * chans,
        deps,
        scratch=[pltpu.VMEM((per, size, cols), BF16)],
        flops=2 * blocks * size * cols * cols * chans,
        nbytes=2 * blocks * size * cols * (2 + chans),
    )


def add_up(place, parts, held, shape, step, cut, deps):
    chans = len(parts)
    blocks, size, cols = parts[0].shape
    per = min(PER_D, blocks)

    def kernel(place_ref, ins, outs):
        total = ins[0][...].astype(F32)
        for q in range(1, chans):
            total = total + ins[q][...].astype(F32)
        outs[0][...] = total.astype(BF16)

    spec = pl.BlockSpec((per, size, cols), lambda g, p: (g, 0, 0))
    carried = () if held is None else (held,)
    deps = [d for d in deps if d is not held]
    return call(
        kernel,
        (blocks // per,),
        [spec] * chans,
        [pl.BlockSpec((per, size, cols), lambda g, p: (cut * (blocks // per) + g, step, 0))],
        [jax.ShapeDtypeStruct(shape, BF16)],
        place,
        tuple(parts),
        carried + tuple(deps),
        aliases={} if held is None else {1 + chans: 0},
        flops=blocks * size * cols * chans,
        nbytes=2 * blocks * size * cols * (1 + chans),
    )[0]


def exchange(parts, axis):
    n = len(parts)
    order = [m for m in ZORDER if m < n] + [m for m in range(1, n) if m not in ZORDER]
    got = {0: parts[0]}
    for m in order:
        got[m] = lax.ppermute(parts[m], axis, [(d, d ^ m) for d in range(n)])
    return [got[m] for m in range(n)]


def body(tokens, gate_in, mix_first, mix_second, twiddle, out_proj):
    rows, cols = tokens.shape
    inner = mix_first.shape[0]
    blocks = rows // inner
    seqs, chans = lax.axis_size("seq"), lax.axis_size("chan")
    seq, chan = lax.axis_index("seq"), lax.axis_index("chan")
    steps = max(1, min(8, inner // (seqs * ROWS)))
    size = inner // steps
    sub = size // seqs
    place = jnp.stack([seq, chan]).astype(jnp.int32)
    tokens = tokens.reshape(blocks, inner, cols)
    gate = gate_in.reshape(blocks, inner, cols)
    back, firsts, sums, out = {}, {}, {}, None
    whole = (blocks, inner, cols)

    def first(t, deps):
        got = first_factor(place, tokens, mix_first, twiddle, [t], size, seqs, deps)
        firsts[t] = exchange(got, "seq")
        return got[0]

    def cuts(t):
        return TAIL if t == steps - 1 else 1

    def step_units(t):
        if t < steps - 1:
            return [(t, 0)] if t >= 0 else []
        t -= steps - 1
        return [(steps - 1, t)] if t < TAIL else []

    last = first(0, ())
    for t in range(1, min(LEAD, steps)):
        last = first(t, (last,))
    spread = spread_out(place, mix_second, blocks, sub, seqs, (last,))
    last = spread
    for t in range(steps + TAIL + LAG):
        for what in ORDER:
            if what == "B" and t < steps:
                got = second_factor(place, firsts[t], spread, cuts(t), (last,))
                last = got[0]
                for c in range(cuts(t)):
                    back[t, c] = exchange(got[c * seqs : (c + 1) * seqs], "seq")
            if what == "A" and t + LEAD < steps:
                last = first(t + LEAD, (last,))
            if what == "G":
                for u in step_units(t - 1):
                    got = gate_project(place, back[u], gate, out_proj, *u, chans, (last,))
                    last = got[0]
                    sums[u] = exchange(got, "chan")
            if what == "P":
                for u in step_units(t - LAG):
                    out = add_up(place, sums[u], out, whole, *u, (last,))
                    last = out
    return out.reshape(rows, cols)


def solution(mesh):
    placed = (
        P(("batch", "seq"), "chan"),
        P(("batch", "seq"), "chan"),
        P(),
        P(),
        P("seq", None),
        P(),
    )
    return jax.shard_map(
        body, mesh=mesh, in_specs=placed, out_specs=P(("batch", "seq"), "chan"), check_vma=False
    )
```

time: 515 us -> 415 us (0.81)
  waiting for transfers between devices: 141 us -> 63.1 us
  local copies, waits for them, and re-layouts: 37.9 us -> 5.74 us
  starting transfers between devices: 156 us -> 180 us
  Pallas kernels: 171 us -> 164 us
  other arithmetic: 6.92 us -> 0.59 us
    ppermute x56 -> x60, waiting for transfers between devices: 141 us -> 63.1 us  [exchange(): got[m] = lax.ppermute(parts[m], axis, [(d, d ^ m) for d in range(n)])]
    select_n x1 -> x0, local copies, waits for them, and re-layouts: 29.8 us -> none  [body(): jnp.where(jnp.eye(sub, dtype=bool)[None, :, None, :], mixer[:, None, :, N...]
    ppermute x56 -> x60, starting transfers between devices: 156 us -> 180 us  [exchange(): got[m] = lax.ppermute(parts[m], axis, [(d, d ^ m) for d in range(n)])]
    pallas_call x32 -> x35, Pallas kernels: 171 us -> 164 us  [call(): pl.pallas_call(run, grid_spec=pltpu.PrefetchScalarGridSpec(num_scalar_pre...]
    select_n x3 -> x0, other arithmetic: 6.22 us -> none  [the longest x1 6.11 us: body(): jnp.where(jnp.eye(sub, dtype=bool)[None, :, None, :], mixer[:, None, :, N...]
  transfers between devices with their start and end apart: 56 -> 60, of which waited for: 17 -> 14; matrix products, arithmetic and copies ran while one was open for 7% -> 0% of each run, Pallas kernels for 31% -> 37%
where the time goes in v2:
time: 415 us; the launch traced here: 413 us
  starting transfers between devices  180 us (43%)
  Pallas kernels  164 us (40%)
  waiting for transfers between devices  63.1 us (15%)
  local copies, waits for them, and re-layouts  5.74 us (1%)
    ppermute x60, starting transfers between devices, exchange(): got[m] = lax.ppermute(parts[m], axis, [(d, d ^ m) for d in range(n)])  180 us
    pallas_call x35, Pallas kernels, call(): pl.pallas_call(run, grid_spec=pltpu.PrefetchScalarGridSpec(num_scalar_pre...  164 us
    ppermute x60, waiting for transfers between devices, exchange(): got[m] = lax.ppermute(parts[m], axis, [(d, d ^ m) for d in range(n)])  63.1 us
  transfers between devices with their start and end apart: 60, of which 14 were waited for; matrix products, arithmetic and copies ran while one was open for 0% of the time, Pallas kernels for 37%

profile of v2, /device:TPU:0, one launch (start us, length us, event | category | flops | bytes accessed | tf_op | source)
XLA Modules:
  0.0 413.4 jit_solution(1610378917184643765)
XLA Ops:
  2.0 6.6 %shard_map.64 = (bf16[16,16,512]{2,1,0:T(8,128)(2,1)}, bf16[16,16,512]{2,1,0:T(8,128)(2,1)}, bf16[16,16,512]{2,1,0:T(8,128)(2,1)}, bf16[16,16,512]{2,1,0:T(8,128)(2,1)}) custom-call(s32[2]{0:T(128)} %pad_add_fusion.scalar_ref, bf16[16,512,512]{2,1,0:T(8,128)(2,1)} %bitcast.14, bf16[512,512]{1,0:T(8,128)(2,1)} %refs_1_.15, f32[4,4,512]{2,1,0:T(4,128)} %reshape.9.refs_2_), custom_call_target="tpu_custom_call" | custom-call | flops 536870912 | bytes 9437184 | tf_op jit(solution)/shard_map/pallas_call | solution.py:32
  14.2 6.6 %shard_map.65 = (bf16[16,16,512]{2,1,0:T(8,128)(2,1)}, bf16[16,16,512]{2,1,0:T(8,128)(2,1)}, bf16[16,16,512]{2,1,0:T(8,128)(2,1)}, bf16[16,16,512]{2,1,0:T(8,128)(2,1)}) custom-call(s32[2]{0:T(128)} %pad_add_fusion.scalar_ref, bf16[16,512,512]{2,1,0:T(8,128)(2,1)} %bitcast.15, bf16[512,512]{1,0:T(8,128)(2,1)} %refs_1_.15, f32[4,4,512]{2,1,0:T(4,128)} %reshape.9.refs_2_, ...), custom_call_target="tpu_custom_call" | custom-call | flops 536870912 | bytes 9437184 | tf_op jit(solution)/shard_map/pallas_call | solution.py:32
  29.8 6.6 %shard_map.67 = (bf16[16,16,512]{2,1,0:T(8,128)(2,1)}, bf16[16,16,512]{2,1,0:T(8,128)(2,1)}, bf16[16,16,512]{2,1,0:T(8,128)(2,1)}, bf16[16,16,512]{2,1,0:T(8,128)(2,1)}) custom-call(s32[2]{0:T(128)} %pad_add_fusion.scalar_ref, bf16[16,512,512]{2,1,0:T(8,128)(2,1)} %bitcast.16, bf16[512,512]{1,0:T(8,128)(2,1)} %refs_1_.15, f32[4,4,512]{2,1,0:T(4,128)} %reshape.9.refs_2_, ...), custom_call_target="tpu_custom_call" | custom-call | flops 536870912 | bytes 9437184 | tf_op jit(solution)/shard_map/pallas_call | solution.py:32
  36.5 15.2 %collective-permute-start.10 = (bf16[16,16,512]{2,1,0:T(8,128)(2,1)}, bf16[16,16,512]{2,1,0:T(8,128)(2,1)S(1)}, u32[]{:S(2)}, u32[]{:S(2)}) collective-permute-start(bf16[16,16,512]{2,1,0:T(8,128)(2,1)} %get-tuple-element.107), channel_id=1, source_target_pairs={{0,16},{8,24},{16,0},{24,8},{1,17},{9,25},{17,1},{25,9},{2,18},{10... | collective-permute-start | bytes 786440 | tf_op jit(solution)/shard_map/ppermute | solution.py:248
  64.0 6.6 %shard_map.69 = (bf16[16,16,512]{2,1,0:T(8,128)(2,1)}, bf16[16,16,512]{2,1,0:T(8,128)(2,1)}, bf16[16,16,512]{2,1,0:T(8,128)(2,1)}, bf16[16,16,512]{2,1,0:T(8,128)(2,1)}) custom-call(s32[2]{0:T(128)} %pad_add_fusion.scalar_ref, bf16[16,512,512]{2,1,0:T(8,128)(2,1)} %bitcast.17, bf16[512,512]{1,0:T(8,128)(2,1)} %refs_1_.15, f32[4,4,512]{2,1,0:T(4,128)} %reshape.9.refs_2_, ...), custom_call_target="tpu_custom_call" | custom-call | flops 536870912 | bytes 9437184 | tf_op jit(solution)/shard_map/pallas_call | solution.py:32
  76.7 12.7 %collective-permute-done.10.refs_2_ = bf16[16,16,512]{2,1,0:T(8,128)(2,1)S(1)} collective-permute-done((bf16[16,16,512]{2,1,0:T(8,128)(2,1)}, bf16[16,16,512]{2,1,0:T(8,128)(2,1)S(1)}, u32[]{:S(2)}, u32[]{:S(2)}) %collective-permute-start.10) | collective-permute-done | bytes 262176 | tf_op jit(solution)/shard_map/ppermute | solution.py:248
  89.5 8.4 %collective-permute-start.6 = (bf16[16,16,512]{2,1,0:T(8,128)(2,1)}, bf16[16,16,512]{2,1,0:T(8,128)(2,1)S(1)}, u32[]{:S(2)}, u32[]{:S(2)}) collective-permute-start(bf16[16,16,512]{2,1,0:T(8,128)(2,1)} %get-tuple-element.103), channel_id=1, source_target_pairs={{0,8},{8,0},{16,24},{24,16},{1,9},{9,1},{17,25},{25,17},{2,10},{10... | collective-permute-start | bytes 786440 | tf_op jit(solution)/shard_map/ppermute | solution.py:248
  100.5 9.6 %collective-permute-start.20 = (bf16[16,16,512]{2,1,0:T(8,128)(2,1)}, bf16[16,16,512]{2,1,0:T(8,128)(2,1)S(1)}, u32[]{:S(2)}, u32[]{:S(2)}) collective-permute-start(bf16[16,16,512]{2,1,0:T(8,128)(2,1)} %get-tuple-element.121), channel_id=1, source_target_pairs={{0,8},{8,0},{16,24},{24,16},{1,9},{9,1},{17,25},{25,17},{2,10},{10... | collective-permute-start | bytes 786440 | tf_op jit(solution)/shard_map/ppermute | solution.py:248
  120.7 6.6 %shard_map.72 = (bf16[16,16,512]{2,1,0:T(8,128)(2,1)}, bf16[16,16,512]{2,1,0:T(8,128)(2,1)}, bf16[16,16,512]{2,1,0:T(8,128)(2,1)}, bf16[16,16,512]{2,1,0:T(8,128)(2,1)}) custom-call(s32[2]{0:T(128)} %pad_add_fusion.scalar_ref, bf16[16,512,512]{2,1,0:T(8,128)(2,1)} %bitcast.18, bf16[512,512]{1,0:T(8,128)(2,1)} %refs_1_.15, f32[4,4,512]{2,1,0:T(4,128)} %reshape.9.refs_2_, ...), custom_call_target="tpu_custom_call" | custom-call | flops 536870912 | bytes 9437184 | tf_op jit(solution)/shard_map/pallas_call | solution.py:32
  141.7 6.7 %collective-permute-done.21.refs_2_ = bf16[16,16,512]{2,1,0:T(8,128)(2,1)S(1)} collective-permute-done((bf16[16,16,512]{2,1,0:T(8,128)(2,1)S(1)}, bf16[16,16,512]{2,1,0:T(8,128)(2,1)S(1)}, u32[]{:S(2)}, u32[]{:S(2)}) %collective-permute-start.21) | collective-permute-done | bytes 262176 | tf_op jit(solution)/shard_map/ppermute | solution.py:248
  148.4 8.2 %collective-permute-start.19 = (bf16[16,16,512]{2,1,0:T(8,128)(2,1)}, bf16[16,16,512]{2,1,0:T(8,128)(2,1)S(1)}, u32[]{:S(2)}, u32[]{:S(2)}) collective-permute-start(bf16[16,16,512]{2,1,0:T(8,128)(2,1)} %get-tuple-element.120), channel_id=1, source_target_pairs={{0,24},{8,16},{16,8},{24,0},{1,25},{9,17},{17,9},{25,1},{2,26},{10... | collective-permute-start | bytes 786440 | tf_op jit(solution)/shard_map/ppermute | solution.py:248
  156.7 4.9 %shard_map.74 = (bf16[16,64,512]{2,1,0:T(8,128)(2,1)}, bf16[16,64,512]{2,1,0:T(8,128)(2,1)}) custom-call(s32[2]{0:T(128)} %pad_add_fusion.scalar_ref, bf16[16,16,512]{2,1,0:T(8,128)(2,1)} %get-tuple-element.102.refs_7_.refs_0_, bf16[16,16,512]{2,1,0:T(8,128)(2,1)} %copy-done.13, bf16[16,16,512]{2,1,0:T(8,128)(2,1)} %copy-done.18, ...), custom_call_target="tpu_custom_call" | custom-call | flops 1073741824 | bytes 4194304 | tf_op jit(solution)/shard_map/pallas_call | solution.py:32
  171.4 6.6 %shard_map.75 = (bf16[16,16,512]{2,1,0:T(8,128)(2,1)}, bf16[16,16,512]{2,1,0:T(8,128)(2,1)}, bf16[16,16,512]{2,1,0:T(8,128)(2,1)}, bf16[16,16,512]{2,1,0:T(8,128)(2,1)}) custom-call(s32[2]{0:T(128)} %pad_add_fusion.scalar_ref, bf16[16,512,512]{2,1,0:T(8,128)(2,1)} %bitcast.19, bf16[512,512]{1,0:T(8,128)(2,1)} %refs_1_.15, f32[4,4,512]{2,1,0:T(4,128)} %reshape.9.refs_2_, ...), custom_call_target="tpu_custom_call" | custom-call | flops 536870912 | bytes 9437184 | tf_op jit(solution)/shard_map/pallas_call | solution.py:32
  182.8 15.9 %collective-permute-start.23 = (bf16[16,16,512]{2,1,0:T(8,128)(2,1)}, bf16[16,16,512]{2,1,0:T(8,128)(2,1)S(1)}, u32[]{:S(2)}, u32[]{:S(2)}) collective-permute-start(bf16[16,16,512]{2,1,0:T(8,128)(2,1)} %get-tuple-element.127), channel_id=1, source_target_pairs={{0,8},{8,0},{16,24},{24,16},{1,9},{9,1},{17,25},{25,17},{2,10},{10... | collective-permute-start | bytes 786440 | tf_op jit(solution)/shard_map/ppermute | solution.py:248
  201.2 4.9 %shard_map.77 = (bf16[16,64,512]{2,1,0:T(8,128)(2,1)}, bf16[16,64,512]{2,1,0:T(8,128)(2,1)}) custom-call(s32[2]{0:T(128)} %pad_add_fusion.scalar_ref, bf16[16,16,512]{2,1,0:T(8,128)(2,1)} %get-tuple-element.114.refs_7_.refs_0_, bf16[16,16,512]{2,1,0:T(8,128)(2,1)} %copy-done.14, bf16[16,16,512]{2,1,0:T(8,128)(2,1)} %copy-done.19, ...), custom_call_target="tpu_custom_call" | custom-call | flops 1073741824 | bytes 4194304 | tf_op jit(solution)/shard_map/pallas_call | solution.py:32
  208.4 9.9 %collective-permute-done.24.refs_2_ = bf16[16,16,512]{2,1,0:T(8,128)(2,1)S(1)} collective-permute-done((bf16[16,16,512]{2,1,0:T(8,128)(2,1)}, bf16[16,16,512]{2,1,0:T(8,128)(2,1)S(1)}, u32[]{:S(2)}, u32[]{:S(2)}) %collective-permute-start.24) | collective-permute-done | bytes 262176 | tf_op jit(solution)/shard_map/ppermute | solution.py:248
  229.3 6.7 %shard_map.79 = (bf16[16,16,512]{2,1,0:T(8,128)(2,1)}, bf16[16,16,512]{2,1,0:T(8,128)(2,1)}, bf16[16,16,512]{2,1,0:T(8,128)(2,1)}, bf16[16,16,512]{2,1,0:T(8,128)(2,1)}) custom-call(s32[2]{0:T(128)} %pad_add_fusion.scalar_ref, bf16[16,512,512]{2,1,0:T(8,128)(2,1)} %bitcast.20, bf16[512,512]{1,0:T(8,128)(2,1)} %refs_1_.15, f32[4,4,512]{2,1,0:T(4,128)} %reshape.9.refs_2_, ...), custom_call_target="tpu_custom_call" | custom-call | flops 536870912 | bytes 9437184 | tf_op jit(solution)/shard_map/pallas_call | solution.py:32
  245.1 4.9 %shard_map.81 = (bf16[16,64,512]{2,1,0:T(8,128)(2,1)}, bf16[16,64,512]{2,1,0:T(8,128)(2,1)}) custom-call(s32[2]{0:T(128)} %pad_add_fusion.scalar_ref, bf16[16,16,512]{2,1,0:T(8,128)(2,1)} %get-tuple-element.125.refs_7_.refs_0_, bf16[16,16,512]{2,1,0:T(8,128)(2,1)} %copy-done.11, bf16[16,16,512]{2,1,0:T(8,128)(2,1)} %copy-done.16, ...), custom_call_target="tpu_custom_call" | custom-call | flops 1073741824 | bytes 4194304 | tf_op jit(solution)/shard_map/pallas_call | solution.py:32
  251.5 13.1 %collective-permute-start.43 = (bf16[16,16,512]{2,1,0:T(8,128)(2,1)S(1)}, bf16[16,16,512]{2,1,0:T(8,128)(2,1)S(1)}, u32[]{:S(2)}, u32[]{:S(2)}) collective-permute-start(bf16[16,16,512]{2,1,0:T(8,128)(2,1)S(1)} %copy-done.65), channel_id=1, source_target_pairs={{0,8},{8,0},{16,24},{24,16},{1,9},{9,1},{17,25},{25,17},{2,10},{10... | collective-permute-start | bytes 786440 | tf_op jit(solution)/shard_map/ppermute | solution.py:248
  273.9 6.6 %shard_map.83 = (bf16[16,16,512]{2,1,0:T(8,128)(2,1)}, bf16[16,16,512]{2,1,0:T(8,128)(2,1)}, bf16[16,16,512]{2,1,0:T(8,128)(2,1)}, bf16[16,16,512]{2,1,0:T(8,128)(2,1)}) custom-call(s32[2]{0:T(128)} %pad_add_fusion.scalar_ref, bf16[16,512,512]{2,1,0:T(8,128)(2,1)} %bitcast.21, bf16[512,512]{1,0:T(8,128)(2,1)} %refs_1_.15, f32[4,4,512]{2,1,0:T(4,128)} %reshape.9.refs_2_, ...), custom_call_target="tpu_custom_call" | custom-call | flops 536870912 | bytes 9437184 | tf_op jit(solution)/shard_map/pallas_call | solution.py:32
  285.1 10.9 %collective-permute-start.40 = (bf16[16,16,512]{2,1,0:T(8,128)(2,1)}, bf16[16,16,512]{2,1,0:T(8,128)(2,1)S(1)}, u32[]{:S(2)}, u32[]{:S(2)}) collective-permute-start(bf16[16,16,512]{2,1,0:T(8,128)(2,1)} %get-tuple-element.150), channel_id=1, source_target_pairs={{0,8},{8,0},{16,24},{24,16},{1,9},{9,1},{17,25},{25,17},{2,10},{10... | collective-permute-start | bytes 786440 | tf_op jit(solution)/shard_map/ppermute | solution.py:248
  323.2 8.5 %collective-permute-done.30.refs_2_ = bf16[16,16,512]{2,1,0:T(8,128)(2,1)S(1)} collective-permute-done((bf16[16,16,512]{2,1,0:T(8,128)(2,1)S(1)}, bf16[16,16,512]{2,1,0:T(8,128)(2,1)S(1)}, u32[]{:S(2)}, u32[]{:S(2)}) %collective-permute-start.30) | collective-permute-done | bytes 262176 | tf_op jit(solution)/shard_map/ppermute | solution.py:248
  335.2 7.5 %collective-permute-start.52 = (bf16[16,16,512]{2,1,0:T(8,128)(2,1)S(1)}, bf16[16,16,512]{2,1,0:T(8,128)(2,1)S(1)}, u32[]{:S(2)}, u32[]{:S(2)}) collective-permute-start(bf16[16,16,512]{2,1,0:T(8,128)(2,1)S(1)} %copy-done.69), channel_id=1, source_target_pairs={{0,16},{8,24},{16,0},{24,8},{1,17},{9,25},{17,1},{25,9},{2,18},{10... | collective-permute-start | bytes 786440 | tf_op jit(solution)/shard_map/ppermute | solution.py:248
  374.4 4.9 %collective-permute-start.47 = (bf16[8,16,512]{2,1,0:T(8,128)(2,1)S(1)}, bf16[8,16,512]{2,1,0:T(8,128)(2,1)S(1)}, u32[]{:S(2)}, u32[]{:S(2)}) collective-permute-start(bf16[8,16,512]{2,1,0:T(8,128)(2,1)S(1)} %copy-done.79), channel_id=1, source_target_pairs={{0,16},{8,24},{16,0},{24,8},{1,17},{9,25},{17,1},{25,9},{2,18},{10... | collective-permute-start | bytes 393224 | tf_op jit(solution)/shard_map/ppermute | solution.py:248
  (301 shorter events, 213.4 us)
Async XLA Ops:
  20.9 35.5 %collective-permute-start = (bf16[16,16,512]{2,1,0:T(8,128)(2,1)}, bf16[16,16,512]{2,1,0:T(8,128)(2,1)S(1)}, u32[]{:S(2)}, u32[]{:S(2)}) collective-permute-start(bf16[16,16,512]{2,1,0:T(8,128)(2,1)} %get-tuple-element.93), channel_id=1, source_target_pairs={{0,8},{8,0},{16,24},{24,16},{1,9},{9,1},{17,25},{25,17},{2,10},{10... | collective-permute-start | bytes 786440 | tf_op jit(solution)/shard_map/ppermute | solution.py:248
  21.8 39.6 %collective-permute-start.1 = (bf16[16,16,512]{2,1,0:T(8,128)(2,1)}, bf16[16,16,512]{2,1,0:T(8,128)(2,1)S(1)}, u32[]{:S(2)}, u32[]{:S(2)}) collective-permute-start(bf16[16,16,512]{2,1,0:T(8,128)(2,1)} %get-tuple-element.94), channel_id=1, source_target_pairs={{0,16},{8,24},{16,0},{24,8},{1,17},{9,25},{17,1},{25,9},{2,18},{10... | collective-permute-start | bytes 786440 | tf_op jit(solution)/shard_map/ppermute | solution.py:248
  25.3 36.1 %collective-permute-start.2 = (bf16[16,16,512]{2,1,0:T(8,128)(2,1)}, bf16[16,16,512]{2,1,0:T(8,128)(2,1)S(1)}, u32[]{:S(2)}, u32[]{:S(2)}) collective-permute-start(bf16[16,16,512]{2,1,0:T(8,128)(2,1)} %get-tuple-element.95), channel_id=1, source_target_pairs={{0,24},{8,16},{16,8},{24,0},{1,25},{9,17},{17,9},{25,1},{2,26},{10... | collective-permute-start | bytes 786440 | tf_op jit(solution)/shard_map/ppermute | solution.py:248
  36.4 38.9 %collective-permute-start.9 = (bf16[16,16,512]{2,1,0:T(8,128)(2,1)}, bf16[16,16,512]{2,1,0:T(8,128)(2,1)S(1)}, u32[]{:S(2)}, u32[]{:S(2)}) collective-permute-start(bf16[16,16,512]{2,1,0:T(8,128)(2,1)} %get-tuple-element.106), channel_id=1, source_target_pairs={{0,8},{8,0},{16,24},{24,16},{1,9},{9,1},{17,25},{25,17},{2,10},{10... | collective-permute-start | bytes 786440 | tf_op jit(solution)/shard_map/ppermute | solution.py:248
  36.5 52.9 %collective-permute-start.10 = (bf16[16,16,512]{2,1,0:T(8,128)(2,1)}, bf16[16,16,512]{2,1,0:T(8,128)(2,1)S(1)}, u32[]{:S(2)}, u32[]{:S(2)}) collective-permute-start(bf16[16,16,512]{2,1,0:T(8,128)(2,1)} %get-tuple-element.107), channel_id=1, source_target_pairs={{0,16},{8,24},{16,0},{24,8},{1,17},{9,25},{17,1},{25,9},{2,18},{10... | collective-permute-start | bytes 786440 | tf_op jit(solution)/shard_map/ppermute | solution.py:248
  56.4 41.5 %collective-permute-start.12 = (bf16[16,16,512]{2,1,0:T(8,128)(2,1)}, bf16[16,16,512]{2,1,0:T(8,128)(2,1)S(1)}, u32[]{:S(2)}, u32[]{:S(2)}) collective-permute-start(bf16[16,16,512]{2,1,0:T(8,128)(2,1)} %get-tuple-element.109), channel_id=1, source_target_pairs={{0,8},{8,0},{16,24},{24,16},{1,9},{9,1},{17,25},{25,17},{2,10},{10... | collective-permute-start | bytes 786440 | tf_op jit(solution)/shard_map/ppermute | solution.py:248
  61.4 37.6 %collective-permute-start.13 = (bf16[16,16,512]{2,1,0:T(8,128)(2,1)}, bf16[16,16,512]{2,1,0:T(8,128)(2,1)S(1)}, u32[]{:S(2)}, u32[]{:S(2)}) collective-permute-start(bf16[16,16,512]{2,1,0:T(8,128)(2,1)} %get-tuple-element.110), channel_id=1, source_target_pairs={{0,16},{8,24},{16,0},{24,8},{1,17},{9,25},{17,1},{25,9},{2,18},{10... | collective-permute-start | bytes 786440 | tf_op jit(solution)/shard_map/ppermute | solution.py:248
  61.4 39.1 %collective-permute-start.14 = (bf16[16,16,512]{2,1,0:T(8,128)(2,1)}, bf16[16,16,512]{2,1,0:T(8,128)(2,1)S(1)}, u32[]{:S(2)}, u32[]{:S(2)}) collective-permute-start(bf16[16,16,512]{2,1,0:T(8,128)(2,1)} %get-tuple-element.111), channel_id=1, source_target_pairs={{0,24},{8,16},{16,8},{24,0},{1,25},{9,17},{17,9},{25,1},{2,26},{10... | collective-permute-start | bytes 786440 | tf_op jit(solution)/shard_map/ppermute | solution.py:248
  75.3 39.6 %collective-permute-start.11 = (bf16[16,16,512]{2,1,0:T(8,128)(2,1)S(1)}, bf16[16,16,512]{2,1,0:T(8,128)(2,1)S(1)}, u32[]{:S(2)}, u32[]{:S(2)}) collective-permute-start(bf16[16,16,512]{2,1,0:T(8,128)(2,1)S(1)} %copy-done.50), channel_id=1, source_target_pairs={{0,24},{8,16},{16,8},{24,0},{1,25},{9,17},{17,9},{25,1},{2,26},{10... | collective-permute-start | bytes 786440 | tf_op jit(solution)/shard_map/ppermute | solution.py:248
  97.9 31.0 %collective-permute-start.7 = (bf16[16,16,512]{2,1,0:T(8,128)(2,1)}, bf16[16,16,512]{2,1,0:T(8,128)(2,1)S(1)}, u32[]{:S(2)}, u32[]{:S(2)}) collective-permute-start(bf16[16,16,512]{2,1,0:T(8,128)(2,1)} %get-tuple-element.104), channel_id=1, source_target_pairs={{0,16},{8,24},{16,0},{24,8},{1,17},{9,25},{17,1},{25,9},{2,18},{10... | collective-permute-start | bytes 786440 | tf_op jit(solution)/shard_map/ppermute | solution.py:248
  99.0 37.1 %collective-permute-start.8 = (bf16[16,16,512]{2,1,0:T(8,128)(2,1)}, bf16[16,16,512]{2,1,0:T(8,128)(2,1)S(1)}, u32[]{:S(2)}, u32[]{:S(2)}) collective-permute-start(bf16[16,16,512]{2,1,0:T(8,128)(2,1)} %get-tuple-element.105), channel_id=1, source_target_pairs={{0,24},{8,16},{16,8},{24,0},{1,25},{9,17},{17,9},{25,1},{2,26},{10... | collective-permute-start | bytes 786440 | tf_op jit(solution)/shard_map/ppermute | solution.py:248
  100.5 40.2 %collective-permute-start.20 = (bf16[16,16,512]{2,1,0:T(8,128)(2,1)}, bf16[16,16,512]{2,1,0:T(8,128)(2,1)S(1)}, u32[]{:S(2)}, u32[]{:S(2)}) collective-permute-start(bf16[16,16,512]{2,1,0:T(8,128)(2,1)} %get-tuple-element.121), channel_id=1, source_target_pairs={{0,8},{8,0},{16,24},{24,16},{1,9},{9,1},{17,25},{25,17},{2,10},{10... | collective-permute-start | bytes 786440 | tf_op jit(solution)/shard_map/ppermute | solution.py:248
  115.0 33.4 %collective-permute-start.21 = (bf16[16,16,512]{2,1,0:T(8,128)(2,1)S(1)}, bf16[16,16,512]{2,1,0:T(8,128)(2,1)S(1)}, u32[]{:S(2)}, u32[]{:S(2)}) collective-permute-start(bf16[16,16,512]{2,1,0:T(8,128)(2,1)S(1)} %copy-done.48), channel_id=1, source_target_pairs={{0,16},{8,24},{16,0},{24,8},{1,17},{9,25},{17,1},{25,9},{2,18},{10... | collective-permute-start | bytes 786440 | tf_op jit(solution)/shard_map/ppermute | solution.py:248
  119.2 103.6 %collective-permute-start.16 = (bf16[16,64,512]{2,1,0:T(8,128)(2,1)}, bf16[16,64,512]{2,1,0:T(8,128)(2,1)S(1)}, u32[]{:S(2)}, u32[]{:S(2)}) collective-permute-start(bf16[16,64,512]{2,1,0:T(8,128)(2,1)} %get-tuple-element.117), channel_id=1, source_target_pairs={{0,4},{4,0},{1,5},{5,1},{2,6},{6,2},{3,7},{7,3},{8,12},{12,8},{9,1... | collective-permute-start | bytes 3145736 | tf_op jit(solution)/shard_map/ppermute | solution.py:248
  128.8 32.7 %collective-permute-start.22 = (bf16[16,16,512]{2,1,0:T(8,128)(2,1)S(1)}, bf16[16,16,512]{2,1,0:T(8,128)(2,1)S(1)}, u32[]{:S(2)}, u32[]{:S(2)}) collective-permute-start(bf16[16,16,512]{2,1,0:T(8,128)(2,1)S(1)} %copy-done.45), channel_id=1, source_target_pairs={{0,24},{8,16},{16,8},{24,0},{1,25},{9,17},{17,9},{25,1},{2,26},{10... | collective-permute-start | bytes 786440 | tf_op jit(solution)/shard_map/ppermute | solution.py:248
  161.6 88.5 %collective-permute-start.15 = (bf16[16,64,512]{2,1,0:T(8,128)(2,1)}, bf16[16,64,512]{2,1,0:T(8,128)(2,1)S(1)}, u32[]{:S(2)}, u32[]{:S(2)}) collective-permute-start(bf16[16,64,512]{2,1,0:T(8,128)(2,1)} %get-tuple-element.116), channel_id=1, source_target_pairs={{0,4},{4,0},{1,5},{5,1},{2,6},{6,2},{3,7},{7,3},{8,12},{12,8},{9,1... | collective-permute-start | bytes 3145736 | tf_op jit(solution)/shard_map/ppermute | solution.py:248
  168.2 30.5 %collective-permute-start.27 = (bf16[16,16,512]{2,1,0:T(8,128)(2,1)S(1)}, bf16[16,16,512]{2,1,0:T(8,128)(2,1)S(1)}, u32[]{:S(2)}, u32[]{:S(2)}) collective-permute-start(bf16[16,16,512]{2,1,0:T(8,128)(2,1)S(1)} %copy-done.57), channel_id=1, source_target_pairs={{0,16},{8,24},{16,0},{24,8},{1,17},{9,25},{17,1},{25,9},{2,18},{10... | collective-permute-start | bytes 786440 | tf_op jit(solution)/shard_map/ppermute | solution.py:248
  168.3 30.4 %collective-permute-start.28 = (bf16[16,16,512]{2,1,0:T(8,128)(2,1)S(1)}, bf16[16,16,512]{2,1,0:T(8,128)(2,1)S(1)}, u32[]{:S(2)}, u32[]{:S(2)}) collective-permute-start(bf16[16,16,512]{2,1,0:T(8,128)(2,1)S(1)} %copy-done.49), channel_id=1, source_target_pairs={{0,24},{8,16},{16,8},{24,0},{1,25},{9,17},{17,9},{25,1},{2,26},{10... | collective-permute-start | bytes 786440 | tf_op jit(solution)/shard_map/ppermute | solution.py:248
  207.1 91.4 %collective-permute-start.33 = (bf16[16,64,512]{2,1,0:T(8,128)(2,1)}, bf16[16,64,512]{2,1,0:T(8,128)(2,1)S(1)}, u32[]{:S(2)}, u32[]{:S(2)}) collective-permute-start(bf16[16,64,512]{2,1,0:T(8,128)(2,1)} %get-tuple-element.141), channel_id=1, source_target_pairs={{0,4},{4,0},{1,5},{5,1},{2,6},{6,2},{3,7},{7,3},{8,12},{12,8},{9,1... | collective-permute-start | bytes 3145736 | tf_op jit(solution)/shard_map/ppermute | solution.py:248
  250.1 92.6 %collective-permute-start.32 = (bf16[16,64,512]{2,1,0:T(8,128)(2,1)}, bf16[16,64,512]{2,1,0:T(8,128)(2,1)S(1)}, u32[]{:S(2)}, u32[]{:S(2)}) collective-permute-start(bf16[16,64,512]{2,1,0:T(8,128)(2,1)} %get-tuple-element.140), channel_id=1, source_target_pairs={{0,4},{4,0},{1,5},{5,1},{2,6},{6,2},{3,7},{7,3},{8,12},{12,8},{9,1... | collective-permute-start | bytes 3145736 | tf_op jit(solution)/shard_map/ppermute | solution.py:248
  251.5 33.6 %collective-permute-start.43 = (bf16[16,16,512]{2,1,0:T(8,128)(2,1)S(1)}, bf16[16,16,512]{2,1,0:T(8,128)(2,1)S(1)}, u32[]{:S(2)}, u32[]{:S(2)}) collective-permute-start(bf16[16,16,512]{2,1,0:T(8,128)(2,1)S(1)} %copy-done.65), channel_id=1, source_target_pairs={{0,8},{8,0},{16,24},{24,16},{1,9},{9,1},{17,25},{25,17},{2,10},{10... | collective-permute-start | bytes 786440 | tf_op jit(solution)/shard_map/ppermute | solution.py:248
  307.7 71.7 %collective-permute-start.50 = (bf16[16,64,512]{2,1,0:T(8,128)(2,1)S(1)}, bf16[16,64,512]{2,1,0:T(8,128)(2,1)S(1)}, u32[]{:S(2)}, u32[]{:S(2)}) collective-permute-start(bf16[16,64,512]{2,1,0:T(8,128)(2,1)S(1)} %copy-done.42), channel_id=1, source_target_pairs={{0,4},{4,0},{1,5},{5,1},{2,6},{6,2},{3,7},{7,3},{8,12},{12,8},{9,1... | collective-permute-start | bytes 3145736 | tf_op jit(solution)/shard_map/ppermute | solution.py:248
  322.2 66.8 %collective-permute-start.49 = (bf16[16,64,512]{2,1,0:T(8,128)(2,1)}, bf16[16,64,512]{2,1,0:T(8,128)(2,1)S(1)}, u32[]{:S(2)}, u32[]{:S(2)}) collective-permute-start(bf16[16,64,512]{2,1,0:T(8,128)(2,1)} %get-tuple-element.162), channel_id=1, source_target_pairs={{0,4},{4,0},{1,5},{5,1},{2,6},{6,2},{3,7},{7,3},{8,12},{12,8},{9,1... | collective-permute-start | bytes 3145736 | tf_op jit(solution)/shard_map/ppermute | solution.py:248
  359.7 40.2 %collective-permute-start.59 = (bf16[16,64,512]{2,1,0:T(8,128)(2,1)}, bf16[16,64,512]{2,1,0:T(8,128)(2,1)S(1)}, u32[]{:S(2)}, u32[]{:S(2)}) collective-permute-start(bf16[16,64,512]{2,1,0:T(8,128)(2,1)} %get-tuple-element.176), channel_id=1, source_target_pairs={{0,4},{4,0},{1,5},{5,1},{2,6},{6,2},{3,7},{7,3},{8,12},{12,8},{9,1... | collective-permute-start | bytes 3145736 | tf_op jit(solution)/shard_map/ppermute | solution.py:248
  (120 other events, 2335.9 us)

commit v3 on v2

v3 whole, which is shorter than its diff:
```python
import functools

import jax
import jax.numpy as jnp
from jax import lax
from jax.experimental import pallas as pl
from jax.experimental.pallas import tpu as pltpu
from jax.sharding import PartitionSpec as P

ROWS = 16
PER_A = 4
PER_C = 8
PER_D = 8
WIDTH = 512
TAIL = (8, 8)
ORDER = 'BGAP'
LEAD = 2
ZORDER = (3, 2, 1)
LAG = 3
COST_A = 5
COST_B = 5
COST_C = 5
COST_D = 1
COST_R = 1
DELAY = ''
ANCHOR = True
HOLD = 1
BEFORE = 1
VMEM = 56 * 1024 * 1024
BF16 = jnp.bfloat16
F32 = jnp.float32
ANY = pl.BlockSpec(memory_space=pl.ANY)


def call(kernel, grid, in_specs, out_specs, out_shape, scalar, args, deps=(), scratch=(), aliases=None, flops=0, nbytes=0):
    n, heads = len(args), 0 if scalar is None else 1

    def run(*refs):
        kernel(refs[0] if heads else None, refs[heads : heads + n], refs[heads + n + len(deps) :])

    return pl.pallas_call(
        run,
        grid_spec=pltpu.PrefetchScalarGridSpec(
            num_scalar_prefetch=heads,
            grid=grid,
            in_specs=list(in_specs) + [ANY] * len(deps),
            out_specs=out_specs,
            scratch_shapes=list(scratch),
        ),
        out_shape=out_shape,
        input_output_aliases=aliases or {},
        compiler_params=pltpu.CompilerParams(vmem_limit_bytes=VMEM),
        cost_estimate=pl.CostEstimate(flops=int(flops), bytes_accessed=int(nbytes), transcendentals=0),
    )(*([] if scalar is None else [scalar]), *args, *deps)


def fit(most, *sizes):
    return max(p for p in range(1, most + 1) if all(x % p == 0 for x in sizes))


def first_factor(tokens, weights, twiddle, steps, size, seqs, deps):
    blocks, inner, cols = tokens.shape
    sub = size // seqs
    per = min(PER_A, blocks)
    lanes = min(cols, 128)
    n = len(steps)
    low = steps[0] * size

    def kernel(place_ref, ins, outs):
        tok, wt, tw = ins
        outs, lhs, turned, scale = outs[:-3], outs[-3], outs[-2], outs[-1]
        me = lax.axis_index("seq")
        g = pl.program_id(0)

        @pl.when(g == 0)
        def _():
            turned[...] = tw[...].T
            for k in range(n):
                for m in range(seqs):
                    at = pl.ds(pl.multiple_of(low + k * size + (me ^ m) * sub, sub), sub)
                    to = slice(k * size + m * sub, k * size + (m + 1) * sub)
                    lhs[to, :] = wt[at, :]
                    column = turned[at, :]
                    for b in range(blocks):
                        scale[b, to, :] = jnp.broadcast_to(column[:, b : b + 1], (sub, lanes))

        for k in range(n):
            here = slice(k * size, (k + 1) * size)
            for b in range(per):
                got = jnp.dot(lhs[here, :], tok[b], preferred_element_type=F32)
                factor = scale[g * per + b, here, :]
                got = (got * jnp.concatenate([factor] * (cols // lanes), axis=1)).astype(BF16)
                for m in range(seqs):
                    outs[k * seqs + m][b] = got[m * sub : (m + 1) * sub]

    return call(
        kernel,
        (blocks // per,),
        [
            pl.BlockSpec((per, inner, cols), lambda g: (g, 0, 0)),
            pl.BlockSpec((inner, inner), lambda g: (0, 0)),
            pl.BlockSpec((blocks, inner), lambda g: (0, 0)),
        ],
        [pl.BlockSpec((per, sub, cols), lambda g: (g, 0, 0))] * (n * seqs),
        [jax.ShapeDtypeStruct((blocks, sub, cols), BF16)] * (n * seqs),
        None,
        (tokens, weights, twiddle),
        deps,
        scratch=[
            pltpu.VMEM((n * size, inner), BF16),
            pltpu.VMEM((inner, blocks), F32),
            pltpu.VMEM((blocks, n * size, lanes), F32),
        ],
        flops=(2 * blocks * n * size * inner * cols) * COST_A,
        nbytes=(2 * blocks * cols * (inner + n * size)) * COST_A,
    )


def released(parts, deps):
    def kernel(place_ref, ins, outs):
        pass

    return call(
        kernel,
        (1,),
        [ANY] * len(parts),
        [ANY] * len(parts),
        [jax.ShapeDtypeStruct(x.shape, x.dtype) for x in parts],
        None,
        tuple(parts),
        deps,
        aliases={k: k for k in range(len(parts))},
        flops=1000000000 * COST_R,
        nbytes=1000000 * COST_R,
    )


def spread_out(place, mixer, blocks, sub, seqs, deps):
    order = mixer.shape[0]
    height = order * sub
    here = blocks * sub
    tall = min(height, 1024)

    def source(rows, me):
        return ((rows // here) ^ me) * blocks + (rows % here) // sub

    def kernel(place_ref, ins, outs):
        me = place_ref[0]
        base = pl.program_id(0) * tall
        down = lax.broadcasted_iota(jnp.int32, (tall, order), 0) + base
        left = (source(down, me) == lax.broadcasted_iota(jnp.int32, (tall, order), 1)).astype(BF16)
        over = lax.broadcasted_iota(jnp.int32, (order, height), 1)
        right = (source(over, me) == lax.broadcasted_iota(jnp.int32, (order, height), 0)).astype(BF16)
        some = jnp.dot(left, ins[0][...], preferred_element_type=F32).astype(BF16)
        full = jnp.dot(some, right, preferred_element_type=F32).astype(BF16)
        same = (lax.broadcasted_iota(jnp.int32, (tall, height), 0) % sub) == (
            lax.broadcasted_iota(jnp.int32, (tall, height), 1) % sub
        )
        outs[0][...] = jnp.where(same, full, jnp.zeros_like(full))

    return call(
        kernel,
        (height // tall,),
        [pl.BlockSpec((order, order), lambda g, p: (0, 0))],
        [pl.BlockSpec((tall, height), lambda g, p: (g, 0))],
        [jax.ShapeDtypeStruct((height, height), BF16)],
        place,
        (mixer,),
        deps,
        flops=2 * height * height * order,
        nbytes=2 * height * height,
    )[0]


def second_factor(place, parts, spread, cuts, deps):
    seqs = len(parts)
    blocks, sub, cols = parts[0].shape
    height = blocks * sub
    width = min(cols, WIDTH)

    def kernel(place_ref, ins, outs):
        sp = ins[-1]
        rhs = [ins[m][...].reshape(height, width) for m in range(seqs)]
        for o in range(seqs):
            total = None
            for m in range(seqs):
                term = jnp.dot(
                    sp[o * height : (o + 1) * height, m * height : (m + 1) * height],
                    rhs[m],
                    preferred_element_type=F32,
                )
                total = term if total is None else total + term
            got = total.astype(BF16).reshape(blocks, sub, width)
            for c, (low, some) in enumerate(cuts):
                outs[c * seqs + o][...] = got[low : low + some]

    spec = pl.BlockSpec((blocks, sub, width), lambda g, p: (0, 0, g))
    return call(
        kernel,
        (cols // width,),
        [spec] * seqs + [pl.BlockSpec(spread.shape, lambda g, p: (0, 0))],
        [pl.BlockSpec((some, sub, width), lambda g, p: (0, 0, g)) for low, some in cuts for _ in range(seqs)],
        [jax.ShapeDtypeStruct((some, sub, cols), BF16) for low, some in cuts for _ in range(seqs)],
        place,
        (*parts, spread),
        deps,
        flops=(2 * (seqs * height) ** 2 * cols) * COST_B,
        nbytes=(4 * seqs * height * cols) * COST_B,
    )


def gate_project(place, parts, gate, proj, step, low, chans, deps):
    seqs = len(parts)
    blocks, sub, cols = parts[0].shape
    size = seqs * sub
    per = fit(PER_C, blocks, low)

    def kernel(place_ref, ins, outs):
        got, gt, ws = ins[:seqs], ins[seqs], ins[seqs + 1 :]
        outs, hidden = outs[:-1], outs[-1]
        me = place_ref[0]
        for m in range(seqs):
            rows = pl.ds(pl.multiple_of((me ^ m) * sub, sub), sub)
            hidden[:, rows, :] = (got[m][...].astype(F32) * gt[:, rows, :].astype(F32)).astype(BF16)
        lhs = hidden[...].reshape(per * size, cols)
        for q in range(chans):
            term = jnp.dot(lhs, ws[q][...], preferred_element_type=F32)
            outs[q][...] = term.astype(BF16).reshape(per, size, cols)

    out = pl.BlockSpec((per, size, cols), lambda g, p: (g, 0, 0))
    return call(
        kernel,
        (blocks // per,),
        [pl.BlockSpec((per, sub, cols), lambda g, p: (g, 0, 0))] * seqs
        + [pl.BlockSpec((per, size, cols), lambda g, p: (low // per + g, step, 0))]
        + [pl.BlockSpec((cols, cols), functools.partial(lambda q, g, p: (p[1], p[1] ^ q), q)) for q in range(chans)],
        [out] * chans,
        [jax.ShapeDtypeStruct((blocks, size, cols), BF16)] * chans,
        place,
        (*parts, gate) + (proj,) * chans,
        deps,
        scratch=[pltpu.VMEM((per, size, cols), BF16)],
        flops=(2 * blocks * size * cols * cols * chans) * COST_C,
        nbytes=(2 * blocks * size * cols * (2 + chans)) * COST_C,
    )


def add_up(place, parts, held, shape, step, low, deps):
    chans = len(parts)
    blocks, size, cols = parts[0].shape
    per = fit(PER_D, blocks, low)

    def kernel(place_ref, ins, outs):
        total = ins[0][...].astype(F32)
        for q in range(1, chans):
            total = total + ins[q][...].astype(F32)
        outs[0][...] = total.astype(BF16)

    spec = pl.BlockSpec((per, size, cols), lambda g, p: (g, 0, 0))
    carried = () if held is None else (held,)
    deps = [d for d in deps if d is not held]
    return call(
        kernel,
        (blocks // per,),
        [spec] * chans,
        [pl.BlockSpec((per, size, cols), lambda g, p: (low // per + g, step, 0))],
        [jax.ShapeDtypeStruct(shape, BF16)],
        place,
        tuple(parts),
        carried + tuple(deps),
        aliases={} if held is None else {1 + chans: 0},
        flops=(blocks * size * cols * chans) * COST_D,
        nbytes=(2 * blocks * size * cols * (1 + chans)) * COST_D,
    )[0]


def exchange(parts, axis, near=None):
    n = len(parts)
    order = [m for m in ZORDER if m < n] + [m for m in range(1, n) if m not in ZORDER]
    got = [parts[0]] + [None] * (n - 1)

    def send(m, x):
        got[m] = lax.ppermute(x, axis, [(d, d ^ m) for d in range(n)])

    for m in order:
        if m == 1 and near is not None:
            near.append(lambda deps: send(1, released([parts[1]], deps)[0]))
        else:
            send(m, parts[m])
    return got


def body(tokens, gate_in, mix_first, mix_second, twiddle, out_proj):
    rows, cols = tokens.shape
    inner = mix_first.shape[0]
    blocks = rows // inner
    seqs, chans = lax.axis_size("seq"), lax.axis_size("chan")
    seq, chan = lax.axis_index("seq"), lax.axis_index("chan")
    steps = max(1, min(8, inner // (seqs * ROWS)))
    size = inner // steps
    sub = size // seqs
    place = jnp.stack([seq, chan]).astype(jnp.int32)
    tokens = tokens.reshape(blocks, inner, cols)
    gate = gate_in.reshape(blocks, inner, cols)
    back, firsts, sums, out = {}, {}, {}, None
    whole = (blocks, inner, cols)

    def first(some, deps):
        got = first_factor(tokens, mix_first, twiddle, some, size, seqs, deps)
        return {t: got[k * seqs : (k + 1) * seqs] for k, t in enumerate(some)}

    def cuts(t):
        if t < steps - 1 or sum(TAIL) != blocks:
            return [(0, blocks)]
        return [(sum(TAIL[:c]), n) for c, n in enumerate(TAIL)]

    ends = cuts(steps - 1)

    def units(t):
        return [(t, 0)] if t >= 0 else []

    pieces = first([0], ())
    near = []

    def flush(deps):
        while near:
            near.pop(0)(deps)

    def listed(kind):
        return near if kind in DELAY else None

    firsts[0] = exchange(pieces[0], "seq", listed("0"))
    last = pieces[0][0]
    if ANCHOR and steps > 1:
        pieces.update(first(list(range(1, steps)), (last,)))
        last = pieces[1][0]
        flush((last,))
    for t in range(1, min(LEAD, steps)):
        if t not in pieces:
            pieces.update(first([t], (last,)))
            last = pieces[t][0]
            flush((last,))
        firsts[t] = exchange(pieces[t], "seq", listed("1"))
    spread = spread_out(place, mix_second, blocks, sub, seqs, (last,))
    last = spread
    flush((last,))
    def plan():
        for t in range(steps):
            for what in ORDER:
                yield what, t, units(t - 1) if what == "G" else units(t - LAG) if what == "P" else []
        over = [(t, 0) for t in range(max(0, steps - LAG), steps - 1)]
        final = [(steps - 1, low) for low, n in ends]
        for u in over[:BEFORE]:
            yield "P", steps, [u]
        yield "G", steps, final
        yield "P", steps, over[BEFORE:] + final

    for what, t, some_units in plan():
        if what == "B" and t < steps:
            got = second_factor(place, firsts[t], spread, cuts(t), (last,))
            last = got[0]
            flush((last,))
            for c, (low, n) in enumerate(cuts(t)):
                kind = "B" if t < steps - 1 else "E"
                back[t, low] = exchange(got[c * seqs : (c + 1) * seqs], "seq", listed(kind))
        if what == "A" and t + LEAD < steps:
            ahead = t + LEAD
            if ANCHOR:
                sent = released(pieces[ahead][HOLD:], (last,))
                pieces[ahead] = list(pieces[ahead][:HOLD]) + list(sent)
                last = sent[0]
            else:
                pieces.update(first([ahead], (last,)))
                last = pieces[ahead][0]
                flush((last,))
            firsts[ahead] = exchange(pieces[ahead], "seq", listed("A"))
        if what == "G":
            for u in some_units:
                if None in back[u]:
                    flush((last,))
                got = gate_project(place, back[u], gate, out_proj, *u, chans, (last,))
                last = got[0]
                flush((last,))
                sums[u] = exchange(got, "chan")
        if what == "P":
            for u in some_units:
                flush((last,))
                out = add_up(place, sums[u], out, whole, *u, (last,))
                last = out
    return out.reshape(rows, cols)


def solution(mesh):
    placed = (
        P(("batch", "seq"), "chan"),
        P(("batch", "seq"), "chan"),
        P(),
        P(),
        P("seq", None),
        P(),
    )
    return jax.shard_map(
        body, mesh=mesh, in_specs=placed, out_specs=P(("batch", "seq"), "chan"), check_vma=False
    )
```

time: 415 us -> 408 us (0.983); the launches traced: 413 us -> 402 us
  Pallas kernels: 164 us -> 133 us
  waiting for transfers between devices: 63.1 us -> 93.2 us
  starting transfers between devices: 180 us -> 166 us
    pallas_call x35, Pallas kernels: 164 us -> 133 us  [call(): pl.pallas_call(run, grid_spec=pltpu.PrefetchScalarGridSpec(num_scalar_pre...]
    ppermute x60, waiting for transfers between devices: 63.1 us -> 93.2 us  [send(): got[m] = lax.ppermute(x, axis, [(d, d ^ m) for d in range(n)])]
    ppermute x60, starting transfers between devices: 180 us -> 166 us  [send(): got[m] = lax.ppermute(x, axis, [(d, d ^ m) for d in range(n)])]
    unnamed x168 -> x190, local copies, waits for them, and re-layouts: 4.37 us -> 8.49 us
  transfers between devices with their start and end apart: 60 -> 60, of which waited for: 14 -> 11; matrix products, arithmetic and copies ran while one was open for 0% -> 0% of each run, Pallas kernels for 37% -> 31%
where the time goes in v3:
time: 408 us; the launch traced here: 402 us
  starting transfers between devices  166 us (41%)
  Pallas kernels  133 us (33%)
  waiting for transfers between devices  93.2 us (23%)
  local copies, waits for them, and re-layouts  8.49 us (2%)
    ppermute x60, starting transfers between devices, send(): got[m] = lax.ppermute(x, axis, [(d, d ^ m) for d in range(n)])  166 us
    pallas_call x35, Pallas kernels, call(): pl.pallas_call(run, grid_spec=pltpu.PrefetchScalarGridSpec(num_scalar_pre...  133 us
    ppermute x60, waiting for transfers between devices, send(): got[m] = lax.ppermute(x, axis, [(d, d ^ m) for d in range(n)])  93.2 us
    unnamed x190, local copies, waits for them, and re-layouts  8.49 us
  transfers between devices with their start and end apart: 60, of which 11 were waited for; matrix products, arithmetic and copies ran while one was open for 0% of the time, Pallas kernels for 31%

profile of v3, /device:TPU:0, one launch (start us, length us, event | category | flops | bytes accessed | tf_op | source)
XLA Modules:
  0.0 402.1 jit_solution(3324831159664444750)
XLA Ops:
  0.0 6.2 %shard_map.64 = (bf16[16,16,512]{2,1,0:T(8,128)(2,1)}, bf16[16,16,512]{2,1,0:T(8,128)(2,1)}, bf16[16,16,512]{2,1,0:T(8,128)(2,1)}, bf16[16,16,512]{2,1,0:T(8,128)(2,1)}) custom-call(bf16[16,512,512]{2,1,0:T(8,128)(2,1)} %bitcast.14, bf16[512,512]{1,0:T(8,128)(2,1)} %refs_1_.4, f32[16,512]{1,0:T(8,128)} %refs_2_.3), custom_call_target="tpu_custom_call" | custom-call | flops 2684354560 | bytes 47185920 | tf_op jit(solution)/shard_map/pallas_call | solution.py:41
  11.9 15.3 %shard_map.65 = (bf16[16,16,512]{2,1,0:T(8,128)(2,1)}, bf16[16,16,512]{2,1,0:T(8,128)(2,1)}, bf16[16,16,512]{2,1,0:T(8,128)(2,1)}, bf16[16,16,512]{2,1,0:T(8,128...) custom-call(bf16[16,512,512]{2,1,0:T(8,128)(2,1)} %bitcast.15, ...), custom_call_target="tpu_custom_call" | custom-call | flops 18790481920 | bytes 78643200 | tf_op jit(solution)/shard_map/pallas_call | solution.py:41
  41.9 9.8 %collective-permute-start.9 = (bf16[16,16,512]{2,1,0:T(8,128)(2,1)}, bf16[16,16,512]{2,1,0:T(8,128)(2,1)S(1)}, u32[]{:S(2)}, u32[]{:S(2)}) collective-permute-start(bf16[16,16,512]{2,1,0:T(8,128)(2,1)} %get-tuple-element.129.refs_6_), channel_id=1, source_target_pairs={{0,8},{8,0},{16,24},{24,16},{1,9},{9,1},{17,25},{25,17},{2,10},{10... | collective-permute-start | bytes 786440 | tf_op jit(solution)/shard_map/ppermute | solution.py:283
  64.9 10.3 %collective-permute-start.6 = (bf16[16,16,512]{2,1,0:T(8,128)(2,1)}, bf16[16,16,512]{2,1,0:T(8,128)(2,1)S(1)}, u32[]{:S(2)}, u32[]{:S(2)}) collective-permute-start(bf16[16,16,512]{2,1,0:T(8,128)(2,1)} %get-tuple-element.131), channel_id=1, source_target_pairs={{0,8},{8,0},{16,24},{24,16},{1,9},{9,1},{17,25},{25,17},{2,10},{10... | collective-permute-start | bytes 786440 | tf_op jit(solution)/shard_map/ppermute | solution.py:283
  78.7 13.7 %collective-permute-start.11 = (bf16[16,16,512]{2,1,0:T(8,128)(2,1)S(1)}, bf16[16,16,512]{2,1,0:T(8,128)(2,1)S(1)}, u32[]{:S(2)}, u32[]{:S(2)}) collective-permute-start(bf16[16,16,512]{2,1,0:T(8,128)(2,1)S(1)} %copy-done.60), channel_id=1, source_target_pairs={{0,24},{8,16},{16,8},{24,0},{1,25},{9,17},{17,9},{25,1},{2,26},{10... | collective-permute-start | bytes 786440 | tf_op jit(solution)/shard_map/ppermute | solution.py:283
  92.4 5.0 %shard_map.70 = (bf16[16,64,512]{2,1,0:T(8,128)(2,1)}, bf16[16,64,512]{2,1,0:T(8,128)(2,1)}) custom-call(s32[2]{0:T(128)} %pad_add_fusion.refs_0_, bf16[16,16,512]{2,1,0:T(8,128)(2,1)} %get-tuple-element.128.refs_3_.refs_1_, bf16[16,16,512]{2,1,0:T(8,128)(2,1)} %copy-done.71, bf16[16,16,512]{2,1,0:T(8,128)(2,1)} %copy-done.76, ...), custom_call_target="tpu_custom_call" | custom-call | flops 5368709120 | bytes 20971520 | tf_op jit(solution)/shard_map/pallas_call | solution.py:41
  97.5 12.1 %collective-permute-done.10.refs_3_ = bf16[16,16,512]{2,1,0:T(8,128)(2,1)S(1)} collective-permute-done((bf16[16,16,512]{2,1,0:T(8,128)(2,1)S(1)}, bf16[16,16,512]{2,1,0:T(8,128)(2,1)S(1)}, u32[]{:S(2)}, u32[]{:S(2)}) %collective-permute-start.10) | collective-permute-done | bytes 262176 | tf_op jit(solution)/shard_map/ppermute | solution.py:283
  112.0 9.4 %collective-permute-start.22 = (bf16[16,16,512]{2,1,0:T(8,128)(2,1)}, bf16[16,16,512]{2,1,0:T(8,128)(2,1)S(1)}, u32[]{:S(2)}, u32[]{:S(2)}) collective-permute-start(bf16[16,16,512]{2,1,0:T(8,128)(2,1)} %get-tuple-element.144.refs_6_), channel_id=1, source_target_pairs={{0,8},{8,0},{16,24},{24,16},{1,9},{9,1},{17,25},{25,17},{2,10},{10... | collective-permute-start | bytes 786440 | tf_op jit(solution)/shard_map/ppermute | solution.py:283
  132.4 5.1 %shard_map.73 = (bf16[16,64,512]{2,1,0:T(8,128)(2,1)}, bf16[16,64,512]{2,1,0:T(8,128)(2,1)}) custom-call(s32[2]{0:T(128)} %pad_add_fusion.refs_0_, bf16[16,16,512]{2,1,0:T(8,128)(2,1)} %get-tuple-element.130.refs_8_.refs_1_, bf16[16,16,512]{2,1,0:T(8,128)(2,1)} %copy-done.39, bf16[16,16,512]{2,1,0:T(8,128)(2,1)} %copy-done.48, ...), custom_call_target="tpu_custom_call" | custom-call | flops 5368709120 | bytes 20971520 | tf_op jit(solution)/shard_map/pallas_call | solution.py:41
  137.5 24.9 %collective-permute-done.23.refs_3_ = bf16[16,16,512]{2,1,0:T(8,128)(2,1)S(1)} collective-permute-done((bf16[16,16,512]{2,1,0:T(8,128)(2,1)S(1)}, bf16[16,16,512]{2,1,0:T(8,128)(2,1)S(1)}, u32[]{:S(2)}, u32[]{:S(2)}) %collective-permute-start.23) | collective-permute-done | bytes 262176 | tf_op jit(solution)/shard_map/ppermute | solution.py:283
  177.1 4.9 %shard_map.76 = (bf16[16,64,512]{2,1,0:T(8,128)(2,1)}, bf16[16,64,512]{2,1,0:T(8,128)(2,1)}) custom-call(s32[2]{0:T(128)} %pad_add_fusion.refs_0_, bf16[16,16,512]{2,1,0:T(8,128)(2,1)} %get-tuple-element.145.refs_8_.refs_1_, bf16[16,16,512]{2,1,0:T(8,128)(2,1)} %copy-done.38, bf16[16,16,512]{2,1,0:T(8,128)(2,1)} %copy-done.47, ...), custom_call_target="tpu_custom_call" | custom-call | flops 5368709120 | bytes 20971520 | tf_op jit(solution)/shard_map/pallas_call | solution.py:41
  182.1 11.6 %collective-permute-done.18.refs_2_ = bf16[16,64,512]{2,1,0:T(8,128)(2,1)S(1)} collective-permute-done((bf16[16,64,512]{2,1,0:T(8,128)(2,1)S(1)}, bf16[16,64,512]{2,1,0:T(8,128)(2,1)S(1)}, u32[]{:S(2)}, u32[]{:S(2)}) %collective-permute-start.18) | collective-permute-done | bytes 1048608 | tf_op jit(solution)/shard_map/ppermute | solution.py:283
  209.7 15.3 %collective-permute-done.33.refs_3_ = bf16[16,16,512]{2,1,0:T(8,128)(2,1)S(1)} collective-permute-done((bf16[16,16,512]{2,1,0:T(8,128)(2,1)S(1)}, bf16[16,16,512]{2,1,0:T(8,128)(2,1)S(1)}, u32[]{:S(2)}, u32[]{:S(2)}) %collective-permute-start.33) | collective-permute-done | bytes 262176 | tf_op jit(solution)/shard_map/ppermute | solution.py:283
  228.9 4.9 %shard_map.80 = (bf16[16,64,512]{2,1,0:T(8,128)(2,1)}, bf16[16,64,512]{2,1,0:T(8,128)(2,1)}) custom-call(s32[2]{0:T(128)} %pad_add_fusion.refs_0_, bf16[16,16,512]{2,1,0:T(8,128)(2,1)} %get-tuple-element.160.refs_8_.refs_1_, bf16[16,16,512]{2,1,0:T(8,128)(2,1)} %copy-done.79, bf16[16,16,512]{2,1,0:T(8,128)(2,1)} %copy-done.83, ...), custom_call_target="tpu_custom_call" | custom-call | flops 5368709120 | bytes 20971520 | tf_op jit(solution)/shard_map/pallas_call | solution.py:41
  242.0 8.1 %collective-permute-start.26 = (bf16[16,16,512]{2,1,0:T(8,128)(2,1)S(1)}, bf16[16,16,512]{2,1,0:T(8,128)(2,1)S(1)}, u32[]{:S(2)}, u32[]{:S(2)}) collective-permute-start(bf16[16,16,512]{2,1,0:T(8,128)(2,1)S(1)} %copy-done.42), channel_id=1, source_target_pairs={{0,16},{8,24},{16,0},{24,8},{1,17},{9,25},{17,1},{25,9},{2,18},{10... | collective-permute-start | bytes 786440 | tf_op jit(solution)/shard_map/ppermute | solution.py:283
  256.3 13.3 %collective-permute-done.26.refs_3_ = bf16[16,16,512]{2,1,0:T(8,128)(2,1)S(1)} collective-permute-done((bf16[16,16,512]{2,1,0:T(8,128)(2,1)S(1)}, bf16[16,16,512]{2,1,0:T(8,128)(2,1)S(1)}, u32[]{:S(2)}, u32[]{:S(2)}) %collective-permute-start.26) | collective-permute-done | bytes 262176 | tf_op jit(solution)/shard_map/ppermute | solution.py:283
  273.4 5.1 %shard_map.84 = (bf16[16,64,512]{2,1,0:T(8,128)(2,1)}, bf16[16,64,512]{2,1,0:T(8,128)(2,1)}) custom-call(s32[2]{0:T(128)} %pad_add_fusion.refs_0_, bf16[16,16,512]{2,1,0:T(8,128)(2,1)} %get-tuple-element.163.refs_8_.refs_1_, bf16[16,16,512]{2,1,0:T(8,128)(2,1)} %copy-done.80, bf16[16,16,512]{2,1,0:T(8,128)(2,1)} %copy-done.84, ...), custom_call_target="tpu_custom_call" | custom-call | flops 5368709120 | bytes 20971520 | tf_op jit(solution)/shard_map/pallas_call | solution.py:41
  278.5 5.3 %collective-permute-start.40 = (bf16[16,16,512]{2,1,0:T(8,128)(2,1)S(1)}, bf16[16,16,512]{2,1,0:T(8,128)(2,1)S(1)}, u32[]{:S(2)}, u32[]{:S(2)}) collective-permute-start(bf16[16,16,512]{2,1,0:T(8,128)(2,1)S(1)} %copy-done.50), channel_id=1, source_target_pairs={{0,8},{8,0},{16,24},{24,16},{1,9},{9,1},{17,25},{25,17},{2,10},{10... | collective-permute-start | bytes 786440 | tf_op jit(solution)/shard_map/ppermute | solution.py:283
  291.2 16.4 %collective-permute-start.35 = (bf16[16,16,512]{2,1,0:T(8,128)(2,1)S(1)}, bf16[16,16,512]{2,1,0:T(8,128)(2,1)S(1)}, u32[]{:S(2)}, u32[]{:S(2)}) collective-permute-start(bf16[16,16,512]{2,1,0:T(8,128)(2,1)S(1)} %copy-done.9), channel_id=1, source_target_pairs={{0,8},{8,0},{16,24},{24,16},{1,9},{9,1},{17,25},{25,17},{2,10},{10... | collective-permute-start | bytes 786440 | tf_op jit(solution)/shard_map/ppermute | solution.py:283
  317.5 4.9 %shard_map.88 = (bf16[16,64,512]{2,1,0:T(8,128)(2,1)}, bf16[16,64,512]{2,1,0:T(8,128)(2,1)}) custom-call(s32[2]{0:T(128)} %pad_add_fusion.refs_0_, bf16[16,16,512]{2,1,0:T(8,128)(2,1)} %get-tuple-element.179.refs_8_.refs_1_, bf16[16,16,512]{2,1,0:T(8,128)(2,1)} %copy-done.68, bf16[16,16,512]{2,1,0:T(8,128)(2,1)} %copy-done.75, ...), custom_call_target="tpu_custom_call" | custom-call | flops 5368709120 | bytes 20971520 | tf_op jit(solution)/shard_map/pallas_call | solution.py:41
  327.4 6.5 %collective-permute-start.54 = (bf16[16,16,512]{2,1,0:T(8,128)(2,1)S(1)}, bf16[16,16,512]{2,1,0:T(8,128)(2,1)S(1)}, u32[]{:S(2)}, u32[]{:S(2)}) collective-permute-start(bf16[16,16,512]{2,1,0:T(8,128)(2,1)S(1)} %copy-done.51), channel_id=1, source_target_pairs={{0,8},{8,0},{16,24},{24,16},{1,9},{9,1},{17,25},{25,17},{2,10},{10... | collective-permute-start | bytes 786440 | tf_op jit(solution)/shard_map/ppermute | solution.py:283
  334.0 5.8 %collective-permute-start.55 = (bf16[16,16,512]{2,1,0:T(8,128)(2,1)S(1)}, bf16[16,16,512]{2,1,0:T(8,128)(2,1)S(1)}, u32[]{:S(2)}, u32[]{:S(2)}) collective-permute-start(bf16[16,16,512]{2,1,0:T(8,128)(2,1)S(1)} %copy-done.44), channel_id=1, source_target_pairs={{0,16},{8,24},{16,0},{24,8},{1,17},{9,25},{17,1},{25,9},{2,18},{10... | collective-permute-start | bytes 786440 | tf_op jit(solution)/shard_map/ppermute | solution.py:283
  345.1 9.1 %collective-permute-done.55.refs_3_ = bf16[16,16,512]{2,1,0:T(8,128)(2,1)S(1)} collective-permute-done((bf16[16,16,512]{2,1,0:T(8,128)(2,1)S(1)}, bf16[16,16,512]{2,1,0:T(8,128)(2,1)S(1)}, u32[]{:S(2)}, u32[]{:S(2)}) %collective-permute-start.55) | collective-permute-done | bytes 262176 | tf_op jit(solution)/shard_map/ppermute | solution.py:283
  366.1 6.1 %collective-permute-start.46 = (bf16[8,16,512]{2,1,0:T(8,128)(2,1)S(1)}, bf16[8,16,512]{2,1,0:T(8,128)(2,1)S(1)}, u32[]{:S(2)}, u32[]{:S(2)}) collective-permute-start(bf16[8,16,512]{2,1,0:T(8,128)(2,1)S(1)} %copy-done.94), channel_id=1, source_target_pairs={{0,8},{8,0},{16,24},{24,16},{1,9},{9,1},{17,25},{25,17},{2,10},{10... | collective-permute-start | bytes 393224 | tf_op jit(solution)/shard_map/ppermute | solution.py:283
  (322 shorter events, 172.3 us)
Async XLA Ops:
  6.2 29.6 %collective-permute-start.3 = (bf16[16,16,512]{2,1,0:T(8,128)(2,1)}, bf16[16,16,512]{2,1,0:T(8,128)(2,1)S(1)}, u32[]{:S(2)}, u32[]{:S(2)}) collective-permute-start(bf16[16,16,512]{2,1,0:T(8,128)(2,1)} %get-tuple-element.125), channel_id=1, source_target_pairs={{0,8},{8,0},{16,24},{24,16},{1,9},{9,1},{17,25},{25,17},{2,10},{10... | collective-permute-start | bytes 786440 | tf_op jit(solution)/shard_map/ppermute | solution.py:283
  41.9 79.5 %collective-permute-start.9 = (bf16[16,16,512]{2,1,0:T(8,128)(2,1)}, bf16[16,16,512]{2,1,0:T(8,128)(2,1)S(1)}, u32[]{:S(2)}, u32[]{:S(2)}) collective-permute-start(bf16[16,16,512]{2,1,0:T(8,128)(2,1)} %get-tuple-element.129.refs_6_), channel_id=1, source_target_pairs={{0,8},{8,0},{16,24},{24,16},{1,9},{9,1},{17,25},{25,17},{2,10},{10... | collective-permute-start | bytes 786440 | tf_op jit(solution)/shard_map/ppermute | solution.py:283
  64.9 62.0 %collective-permute-start.6 = (bf16[16,16,512]{2,1,0:T(8,128)(2,1)}, bf16[16,16,512]{2,1,0:T(8,128)(2,1)S(1)}, u32[]{:S(2)}, u32[]{:S(2)}) collective-permute-start(bf16[16,16,512]{2,1,0:T(8,128)(2,1)} %get-tuple-element.131), channel_id=1, source_target_pairs={{0,8},{8,0},{16,24},{24,16},{1,9},{9,1},{17,25},{25,17},{2,10},{10... | collective-permute-start | bytes 786440 | tf_op jit(solution)/shard_map/ppermute | solution.py:283
  75.2 54.6 %collective-permute-start.7 = (bf16[16,16,512]{2,1,0:T(8,128)(2,1)}, bf16[16,16,512]{2,1,0:T(8,128)(2,1)S(1)}, u32[]{:S(2)}, u32[]{:S(2)}) collective-permute-start(bf16[16,16,512]{2,1,0:T(8,128)(2,1)} %get-tuple-element.132), channel_id=1, source_target_pairs={{0,16},{8,24},{16,0},{24,8},{1,17},{9,25},{17,1},{25,9},{2,18},{10... | collective-permute-start | bytes 786440 | tf_op jit(solution)/shard_map/ppermute | solution.py:283
  78.7 30.9 %collective-permute-start.10 = (bf16[16,16,512]{2,1,0:T(8,128)(2,1)S(1)}, bf16[16,16,512]{2,1,0:T(8,128)(2,1)S(1)}, u32[]{:S(2)}, u32[]{:S(2)}) collective-permute-start(bf16[16,16,512]{2,1,0:T(8,128)(2,1)S(1)} %copy-done.59), channel_id=1, source_target_pairs={{0,16},{8,24},{16,0},{24,8},{1,17},{9,25},{17,1},{25,9},{2,18},{10... | collective-permute-start | bytes 786440 | tf_op jit(solution)/shard_map/ppermute | solution.py:283
  78.7 33.3 %collective-permute-start.11 = (bf16[16,16,512]{2,1,0:T(8,128)(2,1)S(1)}, bf16[16,16,512]{2,1,0:T(8,128)(2,1)S(1)}, u32[]{:S(2)}, u32[]{:S(2)}) collective-permute-start(bf16[16,16,512]{2,1,0:T(8,128)(2,1)S(1)} %copy-done.60), channel_id=1, source_target_pairs={{0,24},{8,16},{16,8},{24,0},{1,25},{9,17},{17,9},{25,1},{2,26},{10... | collective-permute-start | bytes 786440 | tf_op jit(solution)/shard_map/ppermute | solution.py:283
  112.0 55.6 %collective-permute-start.22 = (bf16[16,16,512]{2,1,0:T(8,128)(2,1)}, bf16[16,16,512]{2,1,0:T(8,128)(2,1)S(1)}, u32[]{:S(2)}, u32[]{:S(2)}) collective-permute-start(bf16[16,16,512]{2,1,0:T(8,128)(2,1)} %get-tuple-element.144.refs_6_), channel_id=1, source_target_pairs={{0,8},{8,0},{16,24},{24,16},{1,9},{9,1},{17,25},{25,17},{2,10},{10... | collective-permute-start | bytes 786440 | tf_op jit(solution)/shard_map/ppermute | solution.py:283
  126.8 47.0 %collective-permute-start.19 = (bf16[16,16,512]{2,1,0:T(8,128)(2,1)}, bf16[16,16,512]{2,1,0:T(8,128)(2,1)S(1)}, u32[]{:S(2)}, u32[]{:S(2)}) collective-permute-start(bf16[16,16,512]{2,1,0:T(8,128)(2,1)} %get-tuple-element.154), channel_id=1, source_target_pairs={{0,8},{8,0},{16,24},{24,16},{1,9},{9,1},{17,25},{25,17},{2,10},{10... | collective-permute-start | bytes 786440 | tf_op jit(solution)/shard_map/ppermute | solution.py:283
  126.9 47.9 %collective-permute-start.20 = (bf16[16,16,512]{2,1,0:T(8,128)(2,1)}, bf16[16,16,512]{2,1,0:T(8,128)(2,1)S(1)}, u32[]{:S(2)}, u32[]{:S(2)}) collective-permute-start(bf16[16,16,512]{2,1,0:T(8,128)(2,1)} %get-tuple-element.155), channel_id=1, source_target_pairs={{0,16},{8,24},{16,0},{24,8},{1,17},{9,25},{17,1},{25,9},{2,18},{10... | collective-permute-start | bytes 786440 | tf_op jit(solution)/shard_map/ppermute | solution.py:283
  129.8 32.6 %collective-permute-start.23 = (bf16[16,16,512]{2,1,0:T(8,128)(2,1)S(1)}, bf16[16,16,512]{2,1,0:T(8,128)(2,1)S(1)}, u32[]{:S(2)}, u32[]{:S(2)}) collective-permute-start(bf16[16,16,512]{2,1,0:T(8,128)(2,1)S(1)} %copy-done.29), channel_id=1, source_target_pairs={{0,16},{8,24},{16,0},{24,8},{1,17},{9,25},{17,1},{25,9},{2,18},{10... | collective-permute-start | bytes 786440 | tf_op jit(solution)/shard_map/ppermute | solution.py:283
  129.9 34.3 %collective-permute-start.24 = (bf16[16,16,512]{2,1,0:T(8,128)(2,1)S(1)}, bf16[16,16,512]{2,1,0:T(8,128)(2,1)S(1)}, u32[]{:S(2)}, u32[]{:S(2)}) collective-permute-start(bf16[16,16,512]{2,1,0:T(8,128)(2,1)S(1)} %copy-done.30), channel_id=1, source_target_pairs={{0,24},{8,16},{16,8},{24,0},{1,25},{9,17},{17,9},{25,1},{2,26},{10... | collective-permute-start | bytes 786440 | tf_op jit(solution)/shard_map/ppermute | solution.py:283
  164.3 36.6 %collective-permute-start.15 = (bf16[16,16,512]{2,1,0:T(8,128)(2,1)}, bf16[16,16,512]{2,1,0:T(8,128)(2,1)S(1)}, u32[]{:S(2)}, u32[]{:S(2)}) collective-permute-start(bf16[16,16,512]{2,1,0:T(8,128)(2,1)} %get-tuple-element.147.refs_6_), channel_id=1, source_target_pairs={{0,8},{8,0},{16,24},{24,16},{1,9},{9,1},{17,25},{25,17},{2,10},{10... | collective-permute-start | bytes 786440 | tf_op jit(solution)/shard_map/ppermute | solution.py:283
  176.4 57.5 %collective-permute-start.31 = (bf16[16,64,512]{2,1,0:T(8,128)(2,1)S(1)}, bf16[16,64,512]{2,1,0:T(8,128)(2,1)S(1)}, u32[]{:S(2)}, u32[]{:S(2)}) collective-permute-start(bf16[16,64,512]{2,1,0:T(8,128)(2,1)S(1)} %copy-done.19), channel_id=1, source_target_pairs={{0,4},{4,0},{1,5},{5,1},{2,6},{6,2},{3,7},{7,3},{8,12},{12,8},{9,1... | collective-permute-start | bytes 3145736 | tf_op jit(solution)/shard_map/ppermute | solution.py:283
  193.7 56.4 %collective-permute-start.28 = (bf16[16,16,512]{2,1,0:T(8,128)(2,1)}, bf16[16,16,512]{2,1,0:T(8,128)(2,1)S(1)}, u32[]{:S(2)}, u32[]{:S(2)}) collective-permute-start(bf16[16,16,512]{2,1,0:T(8,128)(2,1)} %get-tuple-element.162.refs_3_), channel_id=1, source_target_pairs={{0,8},{8,0},{16,24},{24,16},{1,9},{9,1},{17,25},{25,17},{2,10},{10... | collective-permute-start | bytes 786440 | tf_op jit(solution)/shard_map/ppermute | solution.py:283
  208.3 32.8 %collective-permute-start.29 = (bf16[16,16,512]{2,1,0:T(8,128)(2,1)S(1)}, bf16[16,16,512]{2,1,0:T(8,128)(2,1)S(1)}, u32[]{:S(2)}, u32[]{:S(2)}) collective-permute-start(bf16[16,16,512]{2,1,0:T(8,128)(2,1)S(1)} %copy-done.25), channel_id=1, source_target_pairs={{0,16},{8,24},{16,0},{24,8},{1,17},{9,25},{17,1},{25,9},{2,18},{10... | collective-permute-start | bytes 786440 | tf_op jit(solution)/shard_map/ppermute | solution.py:283
  227.5 50.9 %collective-permute-start.39 = (bf16[16,64,512]{2,1,0:T(8,128)(2,1)S(1)}, bf16[16,64,512]{2,1,0:T(8,128)(2,1)S(1)}, u32[]{:S(2)}, u32[]{:S(2)}) collective-permute-start(bf16[16,64,512]{2,1,0:T(8,128)(2,1)S(1)} %copy-done.16), channel_id=1, source_target_pairs={{0,4},{4,0},{1,5},{5,1},{2,6},{6,2},{3,7},{7,3},{8,12},{12,8},{9,1... | collective-permute-start | bytes 3145736 | tf_op jit(solution)/shard_map/ppermute | solution.py:283
  233.9 57.3 %collective-permute-start.43 = (bf16[16,16,512]{2,1,0:T(8,128)(2,1)}, bf16[16,16,512]{2,1,0:T(8,128)(2,1)S(1)}, u32[]{:S(2)}, u32[]{:S(2)}) collective-permute-start(bf16[16,16,512]{2,1,0:T(8,128)(2,1)} %get-tuple-element.178.refs_4_), channel_id=1, source_target_pairs={{0,8},{8,0},{16,24},{24,16},{1,9},{9,1},{17,25},{25,17},{2,10},{10... | collective-permute-start | bytes 786440 | tf_op jit(solution)/shard_map/ppermute | solution.py:283
  256.2 33.1 %collective-permute-start.44 = (bf16[16,16,512]{2,1,0:T(8,128)(2,1)S(1)}, bf16[16,16,512]{2,1,0:T(8,128)(2,1)S(1)}, u32[]{:S(2)}, u32[]{:S(2)}) collective-permute-start(bf16[16,16,512]{2,1,0:T(8,128)(2,1)S(1)} %copy-done.23), channel_id=1, source_target_pairs={{0,16},{8,24},{16,0},{24,8},{1,17},{9,25},{17,1},{25,9},{2,18},{10... | collective-permute-start | bytes 786440 | tf_op jit(solution)/shard_map/ppermute | solution.py:283
  271.4 51.0 %collective-permute-start.38 = (bf16[16,64,512]{2,1,0:T(8,128)(2,1)S(1)}, bf16[16,64,512]{2,1,0:T(8,128)(2,1)S(1)}, u32[]{:S(2)}, u32[]{:S(2)}) collective-permute-start(bf16[16,64,512]{2,1,0:T(8,128)(2,1)S(1)} %copy-done.17), channel_id=1, source_target_pairs={{0,4},{4,0},{1,5},{5,1},{2,6},{6,2},{3,7},{7,3},{8,12},{12,8},{9,1... | collective-permute-start | bytes 3145736 | tf_op jit(solution)/shard_map/ppermute | solution.py:283
  278.5 33.9 %collective-permute-start.40 = (bf16[16,16,512]{2,1,0:T(8,128)(2,1)S(1)}, bf16[16,16,512]{2,1,0:T(8,128)(2,1)S(1)}, u32[]{:S(2)}, u32[]{:S(2)}) collective-permute-start(bf16[16,16,512]{2,1,0:T(8,128)(2,1)S(1)} %copy-done.50), channel_id=1, source_target_pairs={{0,8},{8,0},{16,24},{24,16},{1,9},{9,1},{17,25},{25,17},{2,10},{10... | collective-permute-start | bytes 786440 | tf_op jit(solution)/shard_map/ppermute | solution.py:283
  291.2 48.5 %collective-permute-start.35 = (bf16[16,16,512]{2,1,0:T(8,128)(2,1)S(1)}, bf16[16,16,512]{2,1,0:T(8,128)(2,1)S(1)}, u32[]{:S(2)}, u32[]{:S(2)}) collective-permute-start(bf16[16,16,512]{2,1,0:T(8,128)(2,1)S(1)} %copy-done.9), channel_id=1, source_target_pairs={{0,8},{8,0},{16,24},{24,16},{1,9},{9,1},{17,25},{25,17},{2,10},{10... | collective-permute-start | bytes 786440 | tf_op jit(solution)/shard_map/ppermute | solution.py:283
  315.5 45.4 %collective-permute-start.53 = (bf16[16,64,512]{2,1,0:T(8,128)(2,1)S(1)}, bf16[16,64,512]{2,1,0:T(8,128)(2,1)S(1)}, u32[]{:S(2)}, u32[]{:S(2)}) collective-permute-start(bf16[16,64,512]{2,1,0:T(8,128)(2,1)S(1)} %copy-done.18), channel_id=1, source_target_pairs={{0,4},{4,0},{1,5},{5,1},{2,6},{6,2},{3,7},{7,3},{8,12},{12,8},{9,1... | collective-permute-start | bytes 3145736 | tf_op jit(solution)/shard_map/ppermute | solution.py:283
  322.4 43.7 %collective-permute-start.52 = (bf16[16,64,512]{2,1,0:T(8,128)(2,1)}, bf16[16,64,512]{2,1,0:T(8,128)(2,1)S(1)}, u32[]{:S(2)}, u32[]{:S(2)}) collective-permute-start(bf16[16,64,512]{2,1,0:T(8,128)(2,1)} %get-tuple-element.202), channel_id=1, source_target_pairs={{0,4},{4,0},{1,5},{5,1},{2,6},{6,2},{3,7},{7,3},{8,12},{12,8},{9,1... | collective-permute-start | bytes 3145736 | tf_op jit(solution)/shard_map/ppermute | solution.py:283
  345.0 30.3 %collective-permute-start.49 = (bf16[8,16,512]{2,1,0:T(8,128)(2,1)}, bf16[8,16,512]{2,1,0:T(8,128)(2,1)S(1)}, u32[]{:S(2)}, u32[]{:S(2)}) collective-permute-start(bf16[8,16,512]{2,1,0:T(8,128)(2,1)} %get-tuple-element.199), channel_id=1, source_target_pairs={{0,8},{8,0},{16,24},{24,16},{1,9},{9,1},{17,25},{25,17},{2,10},{10... | collective-permute-start | bytes 393224 | tf_op jit(solution)/shard_map/ppermute | solution.py:283
  (131 other events, 1497.2 us)

commit v4 on v3

--- a/solution.py
+++ b/solution.py
@@ -26,7 +26,7 @@
 ANCHOR = True
 HOLD = 1
 BEFORE = 1
-VMEM = 56 * 1024 * 1024
+VMEM = 62 * 1024 * 1024
 BF16 = jnp.bfloat16
 F32 = jnp.float32
 ANY = pl.BlockSpec(memory_space=pl.ANY)

time: 408 us -> 405 us (level); the launches traced: 402 us -> 404 us
  waiting for transfers between devices: 93.2 us -> 97.7 us
    ppermute x60, waiting for transfers between devices: 93.2 us -> 97.7 us  [send(): got[m] = lax.ppermute(x, axis, [(d, d ^ m) for d in range(n)])]
    unnamed x190 -> x102, local copies, waits for them, and re-layouts: 8.49 us -> 8.34 us
  transfers between devices with their start and end apart: 60 -> 60, of which waited for: 11 -> 14; matrix products, arithmetic and copies ran while one was open for 0% -> 0% of each run, Pallas kernels for 31% -> 31%
where the time goes in v4:
time: 405 us; the launch traced here: 404 us
  starting transfers between devices  165 us (41%)
  Pallas kernels  132 us (33%)
  waiting for transfers between devices  97.7 us (24%)
  local copies, waits for them, and re-layouts  8.34 us (2%)
    ppermute x60, starting transfers between devices, send(): got[m] = lax.ppermute(x, axis, [(d, d ^ m) for d in range(n)])  165 us
    pallas_call x35, Pallas kernels, call(): pl.pallas_call(run, grid_spec=pltpu.PrefetchScalarGridSpec(num_scalar_pre...  132 us
    ppermute x60, waiting for transfers between devices, send(): got[m] = lax.ppermute(x, axis, [(d, d ^ m) for d in range(n)])  97.7 us
    unnamed x102, local copies, waits for them, and re-layouts  8.34 us
  transfers between devices with their start and end apart: 60, of which 14 were waited for; matrix products, arithmetic and copies ran while one was open for 0% of the time, Pallas kernels for 31%

profile of v4, /device:TPU:0, one launch (start us, length us, event | category | flops | bytes accessed | tf_op | source)
XLA Modules:
  0.0 403.7 jit_solution(2752679266322250972)
XLA Ops:
  0.0 6.2 %shard_map.64 = (bf16[16,16,512]{2,1,0:T(8,128)(2,1)}, bf16[16,16,512]{2,1,0:T(8,128)(2,1)}, bf16[16,16,512]{2,1,0:T(8,128)(2,1)}, bf16[16,16,512]{2,1,0:T(8,128)(2,1)}) custom-call(bf16[16,512,512]{2,1,0:T(8,128)(2,1)} %bitcast.14, bf16[512,512]{1,0:T(8,128)(2,1)} %refs_1_.4, f32[16,512]{1,0:T(8,128)} %refs_2_.3), custom_call_target="tpu_custom_call" | custom-call | flops 2684354560 | bytes 47185920 | tf_op jit(solution)/shard_map/pallas_call | solution.py:41
  11.9 15.3 %shard_map.65 = (bf16[16,16,512]{2,1,0:T(8,128)(2,1)}, bf16[16,16,512]{2,1,0:T(8,128)(2,1)}, bf16[16,16,512]{2,1,0:T(8,128)(2,1)}, bf16[16,16,512]{2,1,0:T(8,128...) custom-call(bf16[16,512,512]{2,1,0:T(8,128)(2,1)} %bitcast.15, ...), custom_call_target="tpu_custom_call" | custom-call | flops 18790481920 | bytes 78643200 | tf_op jit(solution)/shard_map/pallas_call | solution.py:41
  41.9 9.8 %collective-permute-start.9 = (bf16[16,16,512]{2,1,0:T(8,128)(2,1)}, bf16[16,16,512]{2,1,0:T(8,128)(2,1)S(1)}, u32[]{:S(2)}, u32[]{:S(2)}) collective-permute-start(bf16[16,16,512]{2,1,0:T(8,128)(2,1)} %get-tuple-element.129.refs_6_), channel_id=1, source_target_pairs={{0,8},{8,0},{16,24},{24,16},{1,9},{9,1},{17,25},{25,17},{2,10},{10... | collective-permute-start | bytes 786440 | tf_op jit(solution)/shard_map/ppermute | solution.py:283
  64.9 10.3 %collective-permute-start.6 = (bf16[16,16,512]{2,1,0:T(8,128)(2,1)}, bf16[16,16,512]{2,1,0:T(8,128)(2,1)S(1)}, u32[]{:S(2)}, u32[]{:S(2)}) collective-permute-start(bf16[16,16,512]{2,1,0:T(8,128)(2,1)} %get-tuple-element.131), channel_id=1, source_target_pairs={{0,8},{8,0},{16,24},{24,16},{1,9},{9,1},{17,25},{25,17},{2,10},{10... | collective-permute-start | bytes 786440 | tf_op jit(solution)/shard_map/ppermute | solution.py:283
  78.8 13.7 %collective-permute-start.11 = (bf16[16,16,512]{2,1,0:T(8,128)(2,1)S(1)}, bf16[16,16,512]{2,1,0:T(8,128)(2,1)}, u32[]{:S(2)}, u32[]{:S(2)}) collective-permute-start(bf16[16,16,512]{2,1,0:T(8,128)(2,1)S(1)} %copy-done.33), channel_id=1, source_target_pairs={{0,24},{8,16},{16,8},{24,0},{1,25},{9,17},{17,9},{25,1},{2,26},{10... | collective-permute-start | bytes 786440 | tf_op jit(solution)/shard_map/ppermute | solution.py:283
  92.5 5.0 %shard_map.70 = (bf16[16,64,512]{2,1,0:T(8,128)(2,1)}, bf16[16,64,512]{2,1,0:T(8,128)(2,1)}) custom-call(s32[2]{0:T(128)} %pad_add_fusion.refs_0_, bf16[16,16,512]{2,1,0:T(8,128)(2,1)} %get-tuple-element.128.refs_3_.refs_1_, bf16[16,16,512]{2,1,0:T(8,128)(2,1)} %copy-done.35, bf16[16,16,512]{2,1,0:T(8,128)(2,1)} %collective-permute-done.13.refs_3_, ...), custom_call_target="tpu_custom_call" | custom-call | flops 5368709120 | bytes 20971520 | tf_op jit(solution)/shard_map/pallas_call | solution.py:41
  97.5 12.1 %collective-permute-done.10.refs_3_ = bf16[16,16,512]{2,1,0:T(8,128)(2,1)S(1)} collective-permute-done((bf16[16,16,512]{2,1,0:T(8,128)(2,1)S(1)}, bf16[16,16,512]{2,1,0:T(8,128)(2,1)S(1)}, u32[]{:S(2)}, u32[]{:S(2)}) %collective-permute-start.10) | collective-permute-done | bytes 262176 | tf_op jit(solution)/shard_map/ppermute | solution.py:283
  112.0 9.5 %collective-permute-start.22 = (bf16[16,16,512]{2,1,0:T(8,128)(2,1)}, bf16[16,16,512]{2,1,0:T(8,128)(2,1)}, u32[]{:S(2)}, u32[]{:S(2)}) collective-permute-start(bf16[16,16,512]{2,1,0:T(8,128)(2,1)} %get-tuple-element.144.refs_6_), channel_id=1, source_target_pairs={{0,8},{8,0},{16,24},{24,16},{1,9},{9,1},{17,25},{25,17},{2,10},{10... | collective-permute-start | bytes 786440 | tf_op jit(solution)/shard_map/ppermute | solution.py:283
  132.4 4.9 %shard_map.73 = (bf16[16,64,512]{2,1,0:T(8,128)(2,1)}, bf16[16,64,512]{2,1,0:T(8,128)(2,1)}) custom-call(s32[2]{0:T(128)} %pad_add_fusion.refs_0_, bf16[16,16,512]{2,1,0:T(8,128)(2,1)} %get-tuple-element.130.refs_8_.refs_1_, bf16[16,16,512]{2,1,0:T(8,128)(2,1)} %copy-done.25, bf16[16,16,512]{2,1,0:T(8,128)(2,1)} %copy-done.27, ...), custom_call_target="tpu_custom_call" | custom-call | flops 5368709120 | bytes 20971520 | tf_op jit(solution)/shard_map/pallas_call | solution.py:41
  137.3 25.2 %collective-permute-done.23.refs_3_ = bf16[16,16,512]{2,1,0:T(8,128)(2,1)S(1)} collective-permute-done((bf16[16,16,512]{2,1,0:T(8,128)(2,1)S(1)}, bf16[16,16,512]{2,1,0:T(8,128)(2,1)S(1)}, u32[]{:S(2)}, u32[]{:S(2)}) %collective-permute-start.23) | collective-permute-done | bytes 262176 | tf_op jit(solution)/shard_map/ppermute | solution.py:283
  176.9 4.9 %shard_map.76 = (bf16[16,64,512]{2,1,0:T(8,128)(2,1)}, bf16[16,64,512]{2,1,0:T(8,128)(2,1)}) custom-call(s32[2]{0:T(128)} %pad_add_fusion.refs_0_, bf16[16,16,512]{2,1,0:T(8,128)(2,1)} %get-tuple-element.145.refs_8_.refs_1_, bf16[16,16,512]{2,1,0:T(8,128)(2,1)} %copy-done.24, bf16[16,16,512]{2,1,0:T(8,128)(2,1)} %collective-permute-done.20.refs_3_, ...), custom_call_target="tpu_custom_call" | custom-call | flops 5368709120 | bytes 20971520 | tf_op jit(solution)/shard_map/pallas_call | solution.py:41
  181.8 12.1 %collective-permute-done.18.refs_2_ = bf16[16,64,512]{2,1,0:T(8,128)(2,1)S(1)} collective-permute-done((bf16[16,64,512]{2,1,0:T(8,128)(2,1)}, bf16[16,64,512]{2,1,0:T(8,128)(2,1)S(1)}, u32[]{:S(2)}, u32[]{:S(2)}) %collective-permute-start.18) | collective-permute-done | bytes 1048608 | tf_op jit(solution)/shard_map/ppermute | solution.py:283
  202.6 4.7 %shard_map.79 = (bf16[16,16,512]{2,1,0:T(8,128)(2,1)}, bf16[16,16,512]{2,1,0:T(8,128)(2,1)}, bf16[16,16,512]{2,1,0:T(8,128)(2,1)}, bf16[16,16,512]{2,1,0:T(8,128)(2,1)}) custom-call(s32[2]{0:T(128)} %pad_add_fusion.refs_0_, bf16[16,16,512]{2,1,0:T(8,128)(2,1)} %get-tuple-element.114.refs_1_, bf16[16,16,512]{2,1,0:T(8,128)(2,1)} %collective-permute-done.15.refs_2_, ...), custom_call_target="tpu_custom_call" | custom-call | flops 5368709120 | bytes 10485760 | tf_op jit(solution)/shard_map/pallas_call | solution.py:41
  209.9 15.8 %collective-permute-done.33.refs_3_ = bf16[16,16,512]{2,1,0:T(8,128)(2,1)S(1)} collective-permute-done((bf16[16,16,512]{2,1,0:T(8,128)(2,1)}, bf16[16,16,512]{2,1,0:T(8,128)(2,1)S(1)}, u32[]{:S(2)}, u32[]{:S(2)}) %collective-permute-start.33) | collective-permute-done | bytes 262176 | tf_op jit(solution)/shard_map/ppermute | solution.py:283
  230.3 4.9 %shard_map.80 = (bf16[16,64,512]{2,1,0:T(8,128)(2,1)}, bf16[16,64,512]{2,1,0:T(8,128)(2,1)}) custom-call(s32[2]{0:T(128)} %pad_add_fusion.refs_0_, bf16[16,16,512]{2,1,0:T(8,128)(2,1)} %get-tuple-element.160.refs_8_.refs_1_, bf16[16,16,512]{2,1,0:T(8,128)(2,1)} %copy-done.40, bf16[16,16,512]{2,1,0:T(8,128)(2,1)} %copy-done.44, ...), custom_call_target="tpu_custom_call" | custom-call | flops 5368709120 | bytes 20971520 | tf_op jit(solution)/shard_map/pallas_call | solution.py:41
  242.5 10.5 %collective-permute-start.26 = (bf16[16,16,512]{2,1,0:T(8,128)(2,1)}, bf16[16,16,512]{2,1,0:T(8,128)(2,1)}, u32[]{:S(2)}, u32[]{:S(2)}) collective-permute-start(bf16[16,16,512]{2,1,0:T(8,128)(2,1)} %get-tuple-element.165), channel_id=1, source_target_pairs={{0,16},{8,24},{16,0},{24,8},{1,17},{9,25},{17,1},{25,9},{2,18},{10... | collective-permute-start | bytes 786440 | tf_op jit(solution)/shard_map/ppermute | solution.py:283
  261.4 10.4 %collective-permute-done.26.refs_3_ = bf16[16,16,512]{2,1,0:T(8,128)(2,1)} collective-permute-done((bf16[16,16,512]{2,1,0:T(8,128)(2,1)}, bf16[16,16,512]{2,1,0:T(8,128)(2,1)}, u32[]{:S(2)}, u32[]{:S(2)}) %collective-permute-start.26) | collective-permute-done | bytes 262176 | tf_op jit(solution)/shard_map/ppermute | solution.py:283
  276.2 4.9 %shard_map.84 = (bf16[16,64,512]{2,1,0:T(8,128)(2,1)}, bf16[16,64,512]{2,1,0:T(8,128)(2,1)}) custom-call(s32[2]{0:T(128)} %pad_add_fusion.refs_0_, bf16[16,16,512]{2,1,0:T(8,128)(2,1)} %get-tuple-element.163.refs_8_.refs_1_, bf16[16,16,512]{2,1,0:T(8,128)(2,1)} %copy-done.41, bf16[16,16,512]{2,1,0:T(8,128)(2,1)} %collective-permute-done.26.refs_3_, ...), custom_call_target="tpu_custom_call" | custom-call | flops 5368709120 | bytes 20971520 | tf_op jit(solution)/shard_map/pallas_call | solution.py:41
  281.1 5.5 %collective-permute-start.40 = (bf16[16,16,512]{2,1,0:T(8,128)(2,1)}, bf16[16,16,512]{2,1,0:T(8,128)(2,1)}, u32[]{:S(2)}, u32[]{:S(2)}) collective-permute-start(bf16[16,16,512]{2,1,0:T(8,128)(2,1)} %get-tuple-element.186), channel_id=1, source_target_pairs={{0,8},{8,0},{16,24},{24,16},{1,9},{9,1},{17,25},{25,17},{2,10},{10... | collective-permute-start | bytes 786440 | tf_op jit(solution)/shard_map/ppermute | solution.py:283
  293.2 15.3 %collective-permute-start.35 = (bf16[16,16,512]{2,1,0:T(8,128)(2,1)S(1)}, bf16[16,16,512]{2,1,0:T(8,128)(2,1)}, u32[]{:S(2)}, u32[]{:S(2)}) collective-permute-start(bf16[16,16,512]{2,1,0:T(8,128)(2,1)S(1)} %copy-done.5), channel_id=1, source_target_pairs={{0,8},{8,0},{16,24},{24,16},{1,9},{9,1},{17,25},{25,17},{2,10},{10... | collective-permute-start | bytes 786440 | tf_op jit(solution)/shard_map/ppermute | solution.py:283
  318.7 4.9 %shard_map.88 = (bf16[16,64,512]{2,1,0:T(8,128)(2,1)}, bf16[16,64,512]{2,1,0:T(8,128)(2,1)}) custom-call(s32[2]{0:T(128)} %pad_add_fusion.refs_0_, bf16[16,16,512]{2,1,0:T(8,128)(2,1)} %get-tuple-element.179.refs_8_.refs_1_, bf16[16,16,512]{2,1,0:T(8,128)(2,1)} %collective-permute-done.40.refs_2_, bf16[16,16,512]{2,1,0:T(8,128)(2,1)} %copy-done.38, ...), custom_call_target="tpu_custom_call" | custom-call | flops 5368709120 | bytes 20971520 | tf_op jit(solution)/shard_map/pallas_call | solution.py:41
  328.2 7.9 %collective-permute-start.54 = (bf16[16,16,512]{2,1,0:T(8,128)(2,1)}, bf16[16,16,512]{2,1,0:T(8,128)(2,1)S(1)}, u32[]{:S(2)}, u32[]{:S(2)}) collective-permute-start(bf16[16,16,512]{2,1,0:T(8,128)(2,1)} %get-tuple-element.204), channel_id=1, source_target_pairs={{0,8},{8,0},{16,24},{24,16},{1,9},{9,1},{17,25},{25,17},{2,10},{10... | collective-permute-start | bytes 786440 | tf_op jit(solution)/shard_map/ppermute | solution.py:283
  346.6 9.4 %collective-permute-done.55.refs_3_ = bf16[16,16,512]{2,1,0:T(8,128)(2,1)S(1)} collective-permute-done((bf16[16,16,512]{2,1,0:T(8,128)(2,1)}, bf16[16,16,512]{2,1,0:T(8,128)(2,1)S(1)}, u32[]{:S(2)}, u32[]{:S(2)}) %collective-permute-start.55) | collective-permute-done | bytes 262176 | tf_op jit(solution)/shard_map/ppermute | solution.py:283
  357.7 4.9 %shard_map.91 = (bf16[16,64,512]{2,1,0:T(8,128)(2,1)}, bf16[16,64,512]{2,1,0:T(8,128)(2,1)}) custom-call(s32[2]{0:T(128)} %pad_add_fusion.refs_0_, bf16[16,16,512]{2,1,0:T(8,128)(2,1)} %get-tuple-element.192.refs_8_.refs_1_, bf16[16,16,512]{2,1,0:T(8,128)(2,1)} %copy-done.37, bf16[16,16,512]{2,1,0:T(8,128)(2,1)} %copy-done.42, ...), custom_call_target="tpu_custom_call" | custom-call | flops 5368709120 | bytes 20971520 | tf_op jit(solution)/shard_map/pallas_call | solution.py:41
  (234 shorter events, 175.2 us)
Async XLA Ops:
  6.2 29.6 %collective-permute-start.3 = (bf16[16,16,512]{2,1,0:T(8,128)(2,1)}, bf16[16,16,512]{2,1,0:T(8,128)(2,1)S(1)}, u32[]{:S(2)}, u32[]{:S(2)}) collective-permute-start(bf16[16,16,512]{2,1,0:T(8,128)(2,1)} %get-tuple-element.125), channel_id=1, source_target_pairs={{0,8},{8,0},{16,24},{24,16},{1,9},{9,1},{17,25},{25,17},{2,10},{10... | collective-permute-start | bytes 786440 | tf_op jit(solution)/shard_map/ppermute | solution.py:283
  41.9 79.6 %collective-permute-start.9 = (bf16[16,16,512]{2,1,0:T(8,128)(2,1)}, bf16[16,16,512]{2,1,0:T(8,128)(2,1)S(1)}, u32[]{:S(2)}, u32[]{:S(2)}) collective-permute-start(bf16[16,16,512]{2,1,0:T(8,128)(2,1)} %get-tuple-element.129.refs_6_), channel_id=1, source_target_pairs={{0,8},{8,0},{16,24},{24,16},{1,9},{9,1},{17,25},{25,17},{2,10},{10... | collective-permute-start | bytes 786440 | tf_op jit(solution)/shard_map/ppermute | solution.py:283
  64.9 62.0 %collective-permute-start.6 = (bf16[16,16,512]{2,1,0:T(8,128)(2,1)}, bf16[16,16,512]{2,1,0:T(8,128)(2,1)S(1)}, u32[]{:S(2)}, u32[]{:S(2)}) collective-permute-start(bf16[16,16,512]{2,1,0:T(8,128)(2,1)} %get-tuple-element.131), channel_id=1, source_target_pairs={{0,8},{8,0},{16,24},{24,16},{1,9},{9,1},{17,25},{25,17},{2,10},{10... | collective-permute-start | bytes 786440 | tf_op jit(solution)/shard_map/ppermute | solution.py:283
  75.2 54.6 %collective-permute-start.7 = (bf16[16,16,512]{2,1,0:T(8,128)(2,1)}, bf16[16,16,512]{2,1,0:T(8,128)(2,1)S(1)}, u32[]{:S(2)}, u32[]{:S(2)}) collective-permute-start(bf16[16,16,512]{2,1,0:T(8,128)(2,1)} %get-tuple-element.132), channel_id=1, source_target_pairs={{0,16},{8,24},{16,0},{24,8},{1,17},{9,25},{17,1},{25,9},{2,18},{10... | collective-permute-start | bytes 786440 | tf_op jit(solution)/shard_map/ppermute | solution.py:283
  78.8 30.8 %collective-permute-start.10 = (bf16[16,16,512]{2,1,0:T(8,128)(2,1)S(1)}, bf16[16,16,512]{2,1,0:T(8,128)(2,1)S(1)}, u32[]{:S(2)}, u32[]{:S(2)}) collective-permute-start(bf16[16,16,512]{2,1,0:T(8,128)(2,1)S(1)} %copy-done.32), channel_id=1, source_target_pairs={{0,16},{8,24},{16,0},{24,8},{1,17},{9,25},{17,1},{25,9},{2,18},{10... | collective-permute-start | bytes 786440 | tf_op jit(solution)/shard_map/ppermute | solution.py:283
  78.8 33.2 %collective-permute-start.11 = (bf16[16,16,512]{2,1,0:T(8,128)(2,1)S(1)}, bf16[16,16,512]{2,1,0:T(8,128)(2,1)}, u32[]{:S(2)}, u32[]{:S(2)}) collective-permute-start(bf16[16,16,512]{2,1,0:T(8,128)(2,1)S(1)} %copy-done.33), channel_id=1, source_target_pairs={{0,24},{8,16},{16,8},{24,0},{1,25},{9,17},{17,9},{25,1},{2,26},{10... | collective-permute-start | bytes 786440 | tf_op jit(solution)/shard_map/ppermute | solution.py:283
  112.0 55.6 %collective-permute-start.22 = (bf16[16,16,512]{2,1,0:T(8,128)(2,1)}, bf16[16,16,512]{2,1,0:T(8,128)(2,1)}, u32[]{:S(2)}, u32[]{:S(2)}) collective-permute-start(bf16[16,16,512]{2,1,0:T(8,128)(2,1)} %get-tuple-element.144.refs_6_), channel_id=1, source_target_pairs={{0,8},{8,0},{16,24},{24,16},{1,9},{9,1},{17,25},{25,17},{2,10},{10... | collective-permute-start | bytes 786440 | tf_op jit(solution)/shard_map/ppermute | solution.py:283
  126.9 46.9 %collective-permute-start.19 = (bf16[16,16,512]{2,1,0:T(8,128)(2,1)}, bf16[16,16,512]{2,1,0:T(8,128)(2,1)S(1)}, u32[]{:S(2)}, u32[]{:S(2)}) collective-permute-start(bf16[16,16,512]{2,1,0:T(8,128)(2,1)} %get-tuple-element.154), channel_id=1, source_target_pairs={{0,8},{8,0},{16,24},{24,16},{1,9},{9,1},{17,25},{25,17},{2,10},{10... | collective-permute-start | bytes 786440 | tf_op jit(solution)/shard_map/ppermute | solution.py:283
  126.9 47.9 %collective-permute-start.20 = (bf16[16,16,512]{2,1,0:T(8,128)(2,1)}, bf16[16,16,512]{2,1,0:T(8,128)(2,1)}, u32[]{:S(2)}, u32[]{:S(2)}) collective-permute-start(bf16[16,16,512]{2,1,0:T(8,128)(2,1)} %get-tuple-element.155), channel_id=1, source_target_pairs={{0,16},{8,24},{16,0},{24,8},{1,17},{9,25},{17,1},{25,9},{2,18},{10... | collective-permute-start | bytes 786440 | tf_op jit(solution)/shard_map/ppermute | solution.py:283
  129.8 32.6 %collective-permute-start.23 = (bf16[16,16,512]{2,1,0:T(8,128)(2,1)S(1)}, bf16[16,16,512]{2,1,0:T(8,128)(2,1)S(1)}, u32[]{:S(2)}, u32[]{:S(2)}) collective-permute-start(bf16[16,16,512]{2,1,0:T(8,128)(2,1)S(1)} %copy-done.20), channel_id=1, source_target_pairs={{0,16},{8,24},{16,0},{24,8},{1,17},{9,25},{17,1},{25,9},{2,18},{10... | collective-permute-start | bytes 786440 | tf_op jit(solution)/shard_map/ppermute | solution.py:283
  130.0 34.4 %collective-permute-start.24 = (bf16[16,16,512]{2,1,0:T(8,128)(2,1)S(1)}, bf16[16,16,512]{2,1,0:T(8,128)(2,1)S(1)}, u32[]{:S(2)}, u32[]{:S(2)}) collective-permute-start(bf16[16,16,512]{2,1,0:T(8,128)(2,1)S(1)} %copy-done.21), channel_id=1, source_target_pairs={{0,24},{8,16},{16,8},{24,0},{1,25},{9,17},{17,9},{25,1},{2,26},{10... | collective-permute-start | bytes 786440 | tf_op jit(solution)/shard_map/ppermute | solution.py:283
  164.4 36.7 %collective-permute-start.15 = (bf16[16,16,512]{2,1,0:T(8,128)(2,1)}, bf16[16,16,512]{2,1,0:T(8,128)(2,1)}, u32[]{:S(2)}, u32[]{:S(2)}) collective-permute-start(bf16[16,16,512]{2,1,0:T(8,128)(2,1)} %get-tuple-element.147.refs_6_), channel_id=1, source_target_pairs={{0,8},{8,0},{16,24},{24,16},{1,9},{9,1},{17,25},{25,17},{2,10},{10... | collective-permute-start | bytes 786440 | tf_op jit(solution)/shard_map/ppermute | solution.py:283
  176.3 58.9 %collective-permute-start.31 = (bf16[16,64,512]{2,1,0:T(8,128)(2,1)}, bf16[16,64,512]{2,1,0:T(8,128)(2,1)}, u32[]{:S(2)}, u32[]{:S(2)}) collective-permute-start(bf16[16,64,512]{2,1,0:T(8,128)(2,1)} %get-tuple-element.170), channel_id=1, source_target_pairs={{0,4},{4,0},{1,5},{5,1},{2,6},{6,2},{3,7},{7,3},{8,12},{12,8},{9,1... | collective-permute-start | bytes 3145736 | tf_op jit(solution)/shard_map/ppermute | solution.py:283
  193.9 59.1 %collective-permute-start.28 = (bf16[16,16,512]{2,1,0:T(8,128)(2,1)}, bf16[16,16,512]{2,1,0:T(8,128)(2,1)S(1)}, u32[]{:S(2)}, u32[]{:S(2)}) collective-permute-start(bf16[16,16,512]{2,1,0:T(8,128)(2,1)} %get-tuple-element.162.refs_3_), channel_id=1, source_target_pairs={{0,8},{8,0},{16,24},{24,16},{1,9},{9,1},{17,25},{25,17},{2,10},{10... | collective-permute-start | bytes 786440 | tf_op jit(solution)/shard_map/ppermute | solution.py:283
  209.1 33.4 %collective-permute-start.29 = (bf16[16,16,512]{2,1,0:T(8,128)(2,1)S(1)}, bf16[16,16,512]{2,1,0:T(8,128)(2,1)}, u32[]{:S(2)}, u32[]{:S(2)}) collective-permute-start(bf16[16,16,512]{2,1,0:T(8,128)(2,1)S(1)} %copy-done.16), channel_id=1, source_target_pairs={{0,16},{8,24},{16,0},{24,8},{1,17},{9,25},{17,1},{25,9},{2,18},{10... | collective-permute-start | bytes 786440 | tf_op jit(solution)/shard_map/ppermute | solution.py:283
  228.8 52.2 %collective-permute-start.39 = (bf16[16,64,512]{2,1,0:T(8,128)(2,1)}, bf16[16,64,512]{2,1,0:T(8,128)(2,1)S(1)}, u32[]{:S(2)}, u32[]{:S(2)}) collective-permute-start(bf16[16,64,512]{2,1,0:T(8,128)(2,1)} %get-tuple-element.185), channel_id=1, source_target_pairs={{0,4},{4,0},{1,5},{5,1},{2,6},{6,2},{3,7},{7,3},{8,12},{12,8},{9,1... | collective-permute-start | bytes 3145736 | tf_op jit(solution)/shard_map/ppermute | solution.py:283
  235.2 58.0 %collective-permute-start.43 = (bf16[16,16,512]{2,1,0:T(8,128)(2,1)}, bf16[16,16,512]{2,1,0:T(8,128)(2,1)}, u32[]{:S(2)}, u32[]{:S(2)}) collective-permute-start(bf16[16,16,512]{2,1,0:T(8,128)(2,1)} %get-tuple-element.178.refs_4_), channel_id=1, source_target_pairs={{0,8},{8,0},{16,24},{24,16},{1,9},{9,1},{17,25},{25,17},{2,10},{10... | collective-permute-start | bytes 786440 | tf_op jit(solution)/shard_map/ppermute | solution.py:283
  242.5 29.3 %collective-permute-start.26 = (bf16[16,16,512]{2,1,0:T(8,128)(2,1)}, bf16[16,16,512]{2,1,0:T(8,128)(2,1)}, u32[]{:S(2)}, u32[]{:S(2)}) collective-permute-start(bf16[16,16,512]{2,1,0:T(8,128)(2,1)} %get-tuple-element.165), channel_id=1, source_target_pairs={{0,16},{8,24},{16,0},{24,8},{1,17},{9,25},{17,1},{25,9},{2,18},{10... | collective-permute-start | bytes 786440 | tf_op jit(solution)/shard_map/ppermute | solution.py:283
  261.3 30.5 %collective-permute-start.44 = (bf16[16,16,512]{2,1,0:T(8,128)(2,1)S(1)}, bf16[16,16,512]{2,1,0:T(8,128)(2,1)}, u32[]{:S(2)}, u32[]{:S(2)}) collective-permute-start(bf16[16,16,512]{2,1,0:T(8,128)(2,1)S(1)} %copy-done.14), channel_id=1, source_target_pairs={{0,16},{8,24},{16,0},{24,8},{1,17},{9,25},{17,1},{25,9},{2,18},{10... | collective-permute-start | bytes 786440 | tf_op jit(solution)/shard_map/ppermute | solution.py:283
  275.4 48.2 %collective-permute-start.38 = (bf16[16,64,512]{2,1,0:T(8,128)(2,1)}, bf16[16,64,512]{2,1,0:T(8,128)(2,1)}, u32[]{:S(2)}, u32[]{:S(2)}) collective-permute-start(bf16[16,64,512]{2,1,0:T(8,128)(2,1)} %get-tuple-element.184), channel_id=1, source_target_pairs={{0,4},{4,0},{1,5},{5,1},{2,6},{6,2},{3,7},{7,3},{8,12},{12,8},{9,1... | collective-permute-start | bytes 3145736 | tf_op jit(solution)/shard_map/ppermute | solution.py:283
  281.1 32.1 %collective-permute-start.40 = (bf16[16,16,512]{2,1,0:T(8,128)(2,1)}, bf16[16,16,512]{2,1,0:T(8,128)(2,1)}, u32[]{:S(2)}, u32[]{:S(2)}) collective-permute-start(bf16[16,16,512]{2,1,0:T(8,128)(2,1)} %get-tuple-element.186), channel_id=1, source_target_pairs={{0,8},{8,0},{16,24},{24,16},{1,9},{9,1},{17,25},{25,17},{2,10},{10... | collective-permute-start | bytes 786440 | tf_op jit(solution)/shard_map/ppermute | solution.py:283
  293.2 47.3 %collective-permute-start.35 = (bf16[16,16,512]{2,1,0:T(8,128)(2,1)S(1)}, bf16[16,16,512]{2,1,0:T(8,128)(2,1)}, u32[]{:S(2)}, u32[]{:S(2)}) collective-permute-start(bf16[16,16,512]{2,1,0:T(8,128)(2,1)S(1)} %copy-done.5), channel_id=1, source_target_pairs={{0,8},{8,0},{16,24},{24,16},{1,9},{9,1},{17,25},{25,17},{2,10},{10... | collective-permute-start | bytes 786440 | tf_op jit(solution)/shard_map/ppermute | solution.py:283
  316.9 45.7 %collective-permute-start.53 = (bf16[16,64,512]{2,1,0:T(8,128)(2,1)}, bf16[16,64,512]{2,1,0:T(8,128)(2,1)S(1)}, u32[]{:S(2)}, u32[]{:S(2)}) collective-permute-start(bf16[16,64,512]{2,1,0:T(8,128)(2,1)} %get-tuple-element.203), channel_id=1, source_target_pairs={{0,4},{4,0},{1,5},{5,1},{2,6},{6,2},{3,7},{7,3},{8,12},{12,8},{9,1... | collective-permute-start | bytes 3145736 | tf_op jit(solution)/shard_map/ppermute | solution.py:283
  323.6 44.2 %collective-permute-start.52 = (bf16[16,64,512]{2,1,0:T(8,128)(2,1)}, bf16[16,64,512]{2,1,0:T(8,128)(2,1)}, u32[]{:S(2)}, u32[]{:S(2)}) collective-permute-start(bf16[16,64,512]{2,1,0:T(8,128)(2,1)} %get-tuple-element.202), channel_id=1, source_target_pairs={{0,4},{4,0},{1,5},{5,1},{2,6},{6,2},{3,7},{7,3},{8,12},{12,8},{9,1... | collective-permute-start | bytes 3145736 | tf_op jit(solution)/shard_map/ppermute | solution.py:283
  (87 other events, 1045.2 us)

commit v5 on v4

--- a/solution.py
+++ b/solution.py
@@ -17,7 +17,7 @@
 LEAD = 2
 ZORDER = (3, 2, 1)
 LAG = 3
-COST_A = 5
+COST_A = 1
 COST_B = 5
 COST_C = 5
 COST_D = 1
@@ -26,7 +26,7 @@
 ANCHOR = True
 HOLD = 1
 BEFORE = 1
-VMEM = 62 * 1024 * 1024
+VMEM = 64 * 1024 * 1024
 BF16 = jnp.bfloat16
 F32 = jnp.float32
 ANY = pl.BlockSpec(memory_space=pl.ANY)

time: 405 us -> 404 us (level)
  waiting for transfers between devices: 97.7 us -> 113 us
  starting transfers between devices: 165 us -> 155 us
  local copies, waits for them, and re-layouts: 8.34 us -> 0 us
    ppermute x60, waiting for transfers between devices: 97.7 us -> 113 us  [send(): got[m] = lax.ppermute(x, axis, [(d, d ^ m) for d in range(n)])]
    ppermute x60, starting transfers between devices: 165 us -> 155 us  [send(): got[m] = lax.ppermute(x, axis, [(d, d ^ m) for d in range(n)])]
    unnamed x102 -> x0, local copies, waits for them, and re-layouts: 8.34 us -> none
  transfers between devices with their start and end apart: 60 -> 60, of which waited for: 14 -> 13; matrix products, arithmetic and copies ran while one was open for 0% -> 0% of each run, Pallas kernels for 31% -> 30%
where the time goes in v5:
time: 404 us; the launch traced here: 400 us
  starting transfers between devices  155 us (38%)
  Pallas kernels  131 us (32%)
  waiting for transfers between devices  113 us (28%)
    ppermute x60, starting transfers between devices, send(): got[m] = lax.ppermute(x, axis, [(d, d ^ m) for d in range(n)])  155 us
    pallas_call x35, Pallas kernels, call(): pl.pallas_call(run, grid_spec=pltpu.PrefetchScalarGridSpec(num_scalar_pre...  131 us
    ppermute x60, waiting for transfers between devices, send(): got[m] = lax.ppermute(x, axis, [(d, d ^ m) for d in range(n)])  113 us
  transfers between devices with their start and end apart: 60, of which 13 were waited for; matrix products, arithmetic and copies ran while one was open for 0% of the time, Pallas kernels for 30%

profile of v5, /device:TPU:0, one launch (start us, length us, event | category | flops | bytes accessed | tf_op | source)
XLA Modules:
  0.0 400.4 jit_solution(6277590680516931200)
XLA Ops:
  0.0 6.2 %shard_map.64 = (bf16[16,16,512]{2,1,0:T(8,128)(2,1)}, bf16[16,16,512]{2,1,0:T(8,128)(2,1)}, bf16[16,16,512]{2,1,0:T(8,128)(2,1)}, bf16[16,16,512]{2,1,0:T(8,128)(2,1)}) custom-call(bf16[16,512,512]{2,1,0:T(8,128)(2,1)} %bitcast.14, bf16[512,512]{1,0:T(8,128)(2,1)} %refs_1_.4, f32[16,512]{1,0:T(8,128)} %refs_2_.3), custom_call_target="tpu_custom_call" | custom-call | flops 536870912 | bytes 9437184 | tf_op jit(solution)/shard_map/pallas_call | solution.py:41
  11.9 15.3 %shard_map.65 = (bf16[16,16,512]{2,1,0:T(8,128)(2,1)}, bf16[16,16,512]{2,1,0:T(8,128)(2,1)}, bf16[16,16,512]{2,1,0:T(8,128)(2,1)}, bf16[16,16,512]{2,1,0:T(8,128...) custom-call(bf16[16,512,512]{2,1,0:T(8,128)(2,1)} %bitcast.15, ...), custom_call_target="tpu_custom_call" | custom-call | flops 3758096384 | bytes 15728640 | tf_op jit(solution)/shard_map/pallas_call | solution.py:41
  40.4 10.6 %collective-permute-start.9 = (bf16[16,16,512]{2,1,0:T(8,128)(2,1)}, bf16[16,16,512]{2,1,0:T(8,128)(2,1)}, u32[]{:S(2)}, u32[]{:S(2)}) collective-permute-start(bf16[16,16,512]{2,1,0:T(8,128)(2,1)} %get-tuple-element.129.refs_6_), channel_id=1, source_target_pairs={{0,8},{8,0},{16,24},{24,16},{1,9},{9,1},{17,25},{25,17},{2,10},{10... | collective-permute-start | bytes 786440 | tf_op jit(solution)/shard_map/ppermute | solution.py:283
  64.1 10.4 %collective-permute-start.6 = (bf16[16,16,512]{2,1,0:T(8,128)(2,1)}, bf16[16,16,512]{2,1,0:T(8,128)(2,1)}, u32[]{:S(2)}, u32[]{:S(2)}) collective-permute-start(bf16[16,16,512]{2,1,0:T(8,128)(2,1)} %get-tuple-element.131), channel_id=1, source_target_pairs={{0,8},{8,0},{16,24},{24,16},{1,9},{9,1},{17,25},{25,17},{2,10},{10... | collective-permute-start | bytes 786440 | tf_op jit(solution)/shard_map/ppermute | solution.py:283
  78.8 5.9 %collective-permute-start.11 = (bf16[16,16,512]{2,1,0:T(8,128)(2,1)}, bf16[16,16,512]{2,1,0:T(8,128)(2,1)}, u32[]{:S(2)}, u32[]{:S(2)}) collective-permute-start(bf16[16,16,512]{2,1,0:T(8,128)(2,1)} %get-tuple-element.136), channel_id=1, source_target_pairs={{0,24},{8,16},{16,8},{24,0},{1,25},{9,17},{17,9},{25,1},{2,26},{10... | collective-permute-start | bytes 786440 | tf_op jit(solution)/shard_map/ppermute | solution.py:283
  84.7 4.9 %shard_map.70 = (bf16[16,64,512]{2,1,0:T(8,128)(2,1)}, bf16[16,64,512]{2,1,0:T(8,128)(2,1)}) custom-call(s32[2]{0:T(128)} %pad_add_fusion.refs_0_, bf16[16,16,512]{2,1,0:T(8,128)(2,1)} %get-tuple-element.128.refs_3_.refs_1_, bf16[16,16,512]{2,1,0:T(8,128)(2,1)} %collective-permute-done.12.refs_2_, bf16[16,16,512]{2,1,0:T(8,128)(2,1)} %collective-permute-done.13.refs_3_, ...), custom_call_target="tpu_custom_call" | custom-call | flops 5368709120 | bytes 20971520 | tf_op jit(solution)/shard_map/pallas_call | solution.py:41
  89.6 20.1 %collective-permute-done.10.refs_3_ = bf16[16,16,512]{2,1,0:T(8,128)(2,1)} collective-permute-done((bf16[16,16,512]{2,1,0:T(8,128)(2,1)}, bf16[16,16,512]{2,1,0:T(8,128)(2,1)}, u32[]{:S(2)}, u32[]{:S(2)}) %collective-permute-start.10) | collective-permute-done | bytes 262176 | tf_op jit(solution)/shard_map/ppermute | solution.py:283
  112.1 9.4 %collective-permute-start.22 = (bf16[16,16,512]{2,1,0:T(8,128)(2,1)}, bf16[16,16,512]{2,1,0:T(8,128)(2,1)}, u32[]{:S(2)}, u32[]{:S(2)}) collective-permute-start(bf16[16,16,512]{2,1,0:T(8,128)(2,1)} %get-tuple-element.144.refs_6_), channel_id=1, source_target_pairs={{0,8},{8,0},{16,24},{24,16},{1,9},{9,1},{17,25},{25,17},{2,10},{10... | collective-permute-start | bytes 786440 | tf_op jit(solution)/shard_map/ppermute | solution.py:283
  131.4 4.9 %shard_map.73 = (bf16[16,64,512]{2,1,0:T(8,128)(2,1)}, bf16[16,64,512]{2,1,0:T(8,128)(2,1)}) custom-call(s32[2]{0:T(128)} %pad_add_fusion.refs_0_, bf16[16,16,512]{2,1,0:T(8,128)(2,1)} %get-tuple-element.130.refs_8_.refs_1_, bf16[16,16,512]{2,1,0:T(8,128)(2,1)} %collective-permute-done.6.refs_2_, bf16[16,16,512]{2,1,0:T(8,128)(2,1)} %collective-permute-done.7.refs_3_, ...), custom_call_target="tpu_custom_call" | custom-call | flops 5368709120 | bytes 20971520 | tf_op jit(solution)/shard_map/pallas_call | solution.py:41
  136.3 23.8 %collective-permute-done.23.refs_3_ = bf16[16,16,512]{2,1,0:T(8,128)(2,1)} collective-permute-done((bf16[16,16,512]{2,1,0:T(8,128)(2,1)}, bf16[16,16,512]{2,1,0:T(8,128)(2,1)}, u32[]{:S(2)}, u32[]{:S(2)}) %collective-permute-start.23) | collective-permute-done | bytes 262176 | tf_op jit(solution)/shard_map/ppermute | solution.py:283
  174.1 4.9 %shard_map.76 = (bf16[16,64,512]{2,1,0:T(8,128)(2,1)}, bf16[16,64,512]{2,1,0:T(8,128)(2,1)}) custom-call(s32[2]{0:T(128)} %pad_add_fusion.refs_0_, bf16[16,16,512]{2,1,0:T(8,128)(2,1)} %get-tuple-element.145.refs_8_.refs_1_, bf16[16,16,512]{2,1,0:T(8,128)(2,1)} %collective-permute-done.19.refs_2_, bf16[16,16,512]{2,1,0:T(8,128)(2,1)} %collective-permute-done.20.refs_3_, ...), custom_call_target="tpu_custom_call" | custom-call | flops 5368709120 | bytes 20971520 | tf_op jit(solution)/shard_map/pallas_call | solution.py:41
  179.0 12.5 %collective-permute-done.18.refs_2_ = bf16[16,64,512]{2,1,0:T(8,128)(2,1)} collective-permute-done((bf16[16,64,512]{2,1,0:T(8,128)(2,1)}, bf16[16,64,512]{2,1,0:T(8,128)(2,1)}, u32[]{:S(2)}, u32[]{:S(2)}) %collective-permute-start.18) | collective-permute-done | bytes 1048608 | tf_op jit(solution)/shard_map/ppermute | solution.py:283
  207.4 16.0 %collective-permute-done.33.refs_3_ = bf16[16,16,512]{2,1,0:T(8,128)(2,1)} collective-permute-done((bf16[16,16,512]{2,1,0:T(8,128)(2,1)}, bf16[16,16,512]{2,1,0:T(8,128)(2,1)}, u32[]{:S(2)}, u32[]{:S(2)}) %collective-permute-start.33) | collective-permute-done | bytes 262176 | tf_op jit(solution)/shard_map/ppermute | solution.py:283
  227.3 4.9 %shard_map.80 = (bf16[16,64,512]{2,1,0:T(8,128)(2,1)}, bf16[16,64,512]{2,1,0:T(8,128)(2,1)}) custom-call(s32[2]{0:T(128)} %pad_add_fusion.refs_0_, bf16[16,16,512]{2,1,0:T(8,128)(2,1)} %get-tuple-element.160.refs_8_.refs_1_, bf16[16,16,512]{2,1,0:T(8,128)(2,1)} %collective-permute-done.32.refs_2_, bf16[16,16,512]{2,1,0:T(8,128)(2,1)} %collective-permute-done.33.refs_3_, ...), custom_call_target="tpu_custom_call" | custom-call | flops 5368709120 | bytes 20971520 | tf_op jit(solution)/shard_map/pallas_call | solution.py:41
  239.2 10.8 %collective-permute-start.26 = (bf16[16,16,512]{2,1,0:T(8,128)(2,1)}, bf16[16,16,512]{2,1,0:T(8,128)(2,1)}, u32[]{:S(2)}, u32[]{:S(2)}) collective-permute-start(bf16[16,16,512]{2,1,0:T(8,128)(2,1)} %get-tuple-element.165), channel_id=1, source_target_pairs={{0,16},{8,24},{16,0},{24,8},{1,17},{9,25},{17,1},{25,9},{2,18},{10... | collective-permute-start | bytes 786440 | tf_op jit(solution)/shard_map/ppermute | solution.py:283
  257.9 10.9 %collective-permute-done.26.refs_3_ = bf16[16,16,512]{2,1,0:T(8,128)(2,1)} collective-permute-done((bf16[16,16,512]{2,1,0:T(8,128)(2,1)}, bf16[16,16,512]{2,1,0:T(8,128)(2,1)}, u32[]{:S(2)}, u32[]{:S(2)}) %collective-permute-start.26) | collective-permute-done | bytes 262176 | tf_op jit(solution)/shard_map/ppermute | solution.py:283
  272.9 4.9 %shard_map.84 = (bf16[16,64,512]{2,1,0:T(8,128)(2,1)}, bf16[16,64,512]{2,1,0:T(8,128)(2,1)}) custom-call(s32[2]{0:T(128)} %pad_add_fusion.refs_0_, bf16[16,16,512]{2,1,0:T(8,128)(2,1)} %get-tuple-element.163.refs_8_.refs_1_, bf16[16,16,512]{2,1,0:T(8,128)(2,1)} %collective-permute-done.25.refs_2_, bf16[16,16,512]{2,1,0:T(8,128)(2,1)} %collective-permute-done.26.refs_3_, ...), custom_call_target="tpu_custom_call" | custom-call | flops 5368709120 | bytes 20971520 | tf_op jit(solution)/shard_map/pallas_call | solution.py:41
  289.9 16.5 %collective-permute-start.35 = (bf16[16,16,512]{2,1,0:T(8,128)(2,1)}, bf16[16,16,512]{2,1,0:T(8,128)(2,1)}, u32[]{:S(2)}, u32[]{:S(2)}) collective-permute-start(bf16[16,16,512]{2,1,0:T(8,128)(2,1)} %get-tuple-element.181.refs_4_), channel_id=1, source_target_pairs={{0,8},{8,0},{16,24},{24,16},{1,9},{9,1},{17,25},{25,17},{2,10},{10... | collective-permute-start | bytes 786440 | tf_op jit(solution)/shard_map/ppermute | solution.py:283
  315.7 4.9 %shard_map.88 = (bf16[16,64,512]{2,1,0:T(8,128)(2,1)}, bf16[16,64,512]{2,1,0:T(8,128)(2,1)}) custom-call(s32[2]{0:T(128)} %pad_add_fusion.refs_0_, bf16[16,16,512]{2,1,0:T(8,128)(2,1)} %get-tuple-element.179.refs_8_.refs_1_, bf16[16,16,512]{2,1,0:T(8,128)(2,1)} %collective-permute-done.40.refs_2_, bf16[16,16,512]{2,1,0:T(8,128)(2,1)} %collective-permute-done.41.refs_3_, ...), custom_call_target="tpu_custom_call" | custom-call | flops 5368709120 | bytes 20971520 | tf_op jit(solution)/shard_map/pallas_call | solution.py:41
  325.7 7.3 %collective-permute-start.54 = (bf16[16,16,512]{2,1,0:T(8,128)(2,1)}, bf16[16,16,512]{2,1,0:T(8,128)(2,1)}, u32[]{:S(2)}, u32[]{:S(2)}) collective-permute-start(bf16[16,16,512]{2,1,0:T(8,128)(2,1)} %get-tuple-element.204), channel_id=1, source_target_pairs={{0,8},{8,0},{16,24},{24,16},{1,9},{9,1},{17,25},{25,17},{2,10},{10... | collective-permute-start | bytes 786440 | tf_op jit(solution)/shard_map/ppermute | solution.py:283
  332.9 5.2 %collective-permute-start.55 = (bf16[16,16,512]{2,1,0:T(8,128)(2,1)}, bf16[16,16,512]{2,1,0:T(8,128)(2,1)}, u32[]{:S(2)}, u32[]{:S(2)}) collective-permute-start(bf16[16,16,512]{2,1,0:T(8,128)(2,1)} %get-tuple-element.205), channel_id=1, source_target_pairs={{0,16},{8,24},{16,0},{24,8},{1,17},{9,25},{17,1},{25,9},{2,18},{10... | collective-permute-start | bytes 786440 | tf_op jit(solution)/shard_map/ppermute | solution.py:283
  343.9 9.8 %collective-permute-done.55.refs_3_ = bf16[16,16,512]{2,1,0:T(8,128)(2,1)} collective-permute-done((bf16[16,16,512]{2,1,0:T(8,128)(2,1)}, bf16[16,16,512]{2,1,0:T(8,128)(2,1)}, u32[]{:S(2)}, u32[]{:S(2)}) %collective-permute-start.55) | collective-permute-done | bytes 262176 | tf_op jit(solution)/shard_map/ppermute | solution.py:283
  355.0 4.9 %shard_map.91 = (bf16[16,64,512]{2,1,0:T(8,128)(2,1)}, bf16[16,64,512]{2,1,0:T(8,128)(2,1)}) custom-call(s32[2]{0:T(128)} %pad_add_fusion.refs_0_, bf16[16,16,512]{2,1,0:T(8,128)(2,1)} %get-tuple-element.192.refs_8_.refs_1_, bf16[16,16,512]{2,1,0:T(8,128)(2,1)} %collective-permute-done.54.refs_2_, bf16[16,16,512]{2,1,0:T(8,128)(2,1)} %collective-permute-done.55.refs_3_, ...), custom_call_target="tpu_custom_call" | custom-call | flops 5368709120 | bytes 20971520 | tf_op jit(solution)/shard_map/pallas_call | solution.py:41
  386.9 5.0 %collective-permute-done.58.refs_2_ = bf16[8,64,512]{2,1,0:T(8,128)(2,1)} collective-permute-done((bf16[8,64,512]{2,1,0:T(8,128)(2,1)}, bf16[8,64,512]{2,1,0:T(8,128)(2,1)}, u32[]{:S(2)}, u32[]{:S(2)}) %collective-permute-start.58) | collective-permute-done | bytes 524320 | tf_op jit(solution)/shard_map/ppermute | solution.py:283
  (132 shorter events, 170.1 us)
Async XLA Ops:
  6.2 29.6 %collective-permute-start.3 = (bf16[16,16,512]{2,1,0:T(8,128)(2,1)}, bf16[16,16,512]{2,1,0:T(8,128)(2,1)}, u32[]{:S(2)}, u32[]{:S(2)}) collective-permute-start(bf16[16,16,512]{2,1,0:T(8,128)(2,1)} %get-tuple-element.125), channel_id=1, source_target_pairs={{0,8},{8,0},{16,24},{24,16},{1,9},{9,1},{17,25},{25,17},{2,10},{10... | collective-permute-start | bytes 786440 | tf_op jit(solution)/shard_map/ppermute | solution.py:283
  40.4 81.1 %collective-permute-start.9 = (bf16[16,16,512]{2,1,0:T(8,128)(2,1)}, bf16[16,16,512]{2,1,0:T(8,128)(2,1)}, u32[]{:S(2)}, u32[]{:S(2)}) collective-permute-start(bf16[16,16,512]{2,1,0:T(8,128)(2,1)} %get-tuple-element.129.refs_6_), channel_id=1, source_target_pairs={{0,8},{8,0},{16,24},{24,16},{1,9},{9,1},{17,25},{25,17},{2,10},{10... | collective-permute-start | bytes 786440 | tf_op jit(solution)/shard_map/ppermute | solution.py:283
  64.1 62.0 %collective-permute-start.6 = (bf16[16,16,512]{2,1,0:T(8,128)(2,1)}, bf16[16,16,512]{2,1,0:T(8,128)(2,1)}, u32[]{:S(2)}, u32[]{:S(2)}) collective-permute-start(bf16[16,16,512]{2,1,0:T(8,128)(2,1)} %get-tuple-element.131), channel_id=1, source_target_pairs={{0,8},{8,0},{16,24},{24,16},{1,9},{9,1},{17,25},{25,17},{2,10},{10... | collective-permute-start | bytes 786440 | tf_op jit(solution)/shard_map/ppermute | solution.py:283
  74.5 54.5 %collective-permute-start.7 = (bf16[16,16,512]{2,1,0:T(8,128)(2,1)}, bf16[16,16,512]{2,1,0:T(8,128)(2,1)}, u32[]{:S(2)}, u32[]{:S(2)}) collective-permute-start(bf16[16,16,512]{2,1,0:T(8,128)(2,1)} %get-tuple-element.132), channel_id=1, source_target_pairs={{0,16},{8,24},{16,0},{24,8},{1,17},{9,25},{17,1},{25,9},{2,18},{10... | collective-permute-start | bytes 786440 | tf_op jit(solution)/shard_map/ppermute | solution.py:283
  78.8 30.9 %collective-permute-start.10 = (bf16[16,16,512]{2,1,0:T(8,128)(2,1)}, bf16[16,16,512]{2,1,0:T(8,128)(2,1)}, u32[]{:S(2)}, u32[]{:S(2)}) collective-permute-start(bf16[16,16,512]{2,1,0:T(8,128)(2,1)} %get-tuple-element.135), channel_id=1, source_target_pairs={{0,16},{8,24},{16,0},{24,8},{1,17},{9,25},{17,1},{25,9},{2,18},{10... | collective-permute-start | bytes 786440 | tf_op jit(solution)/shard_map/ppermute | solution.py:283
  78.8 33.3 %collective-permute-start.11 = (bf16[16,16,512]{2,1,0:T(8,128)(2,1)}, bf16[16,16,512]{2,1,0:T(8,128)(2,1)}, u32[]{:S(2)}, u32[]{:S(2)}) collective-permute-start(bf16[16,16,512]{2,1,0:T(8,128)(2,1)} %get-tuple-element.136), channel_id=1, source_target_pairs={{0,24},{8,16},{16,8},{24,0},{1,25},{9,17},{17,9},{25,1},{2,26},{10... | collective-permute-start | bytes 786440 | tf_op jit(solution)/shard_map/ppermute | solution.py:283
  112.1 53.0 %collective-permute-start.22 = (bf16[16,16,512]{2,1,0:T(8,128)(2,1)}, bf16[16,16,512]{2,1,0:T(8,128)(2,1)}, u32[]{:S(2)}, u32[]{:S(2)}) collective-permute-start(bf16[16,16,512]{2,1,0:T(8,128)(2,1)} %get-tuple-element.144.refs_6_), channel_id=1, source_target_pairs={{0,8},{8,0},{16,24},{24,16},{1,9},{9,1},{17,25},{25,17},{2,10},{10... | collective-permute-start | bytes 786440 | tf_op jit(solution)/shard_map/ppermute | solution.py:283
  126.0 45.1 %collective-permute-start.19 = (bf16[16,16,512]{2,1,0:T(8,128)(2,1)}, bf16[16,16,512]{2,1,0:T(8,128)(2,1)}, u32[]{:S(2)}, u32[]{:S(2)}) collective-permute-start(bf16[16,16,512]{2,1,0:T(8,128)(2,1)} %get-tuple-element.154), channel_id=1, source_target_pairs={{0,8},{8,0},{16,24},{24,16},{1,9},{9,1},{17,25},{25,17},{2,10},{10... | collective-permute-start | bytes 786440 | tf_op jit(solution)/shard_map/ppermute | solution.py:283
  126.1 46.0 %collective-permute-start.20 = (bf16[16,16,512]{2,1,0:T(8,128)(2,1)}, bf16[16,16,512]{2,1,0:T(8,128)(2,1)}, u32[]{:S(2)}, u32[]{:S(2)}) collective-permute-start(bf16[16,16,512]{2,1,0:T(8,128)(2,1)} %get-tuple-element.155), channel_id=1, source_target_pairs={{0,16},{8,24},{16,0},{24,8},{1,17},{9,25},{17,1},{25,9},{2,18},{10... | collective-permute-start | bytes 786440 | tf_op jit(solution)/shard_map/ppermute | solution.py:283
  129.0 31.1 %collective-permute-start.23 = (bf16[16,16,512]{2,1,0:T(8,128)(2,1)}, bf16[16,16,512]{2,1,0:T(8,128)(2,1)}, u32[]{:S(2)}, u32[]{:S(2)}) collective-permute-start(bf16[16,16,512]{2,1,0:T(8,128)(2,1)} %get-tuple-element.158), channel_id=1, source_target_pairs={{0,16},{8,24},{16,0},{24,8},{1,17},{9,25},{17,1},{25,9},{2,18},{10... | collective-permute-start | bytes 786440 | tf_op jit(solution)/shard_map/ppermute | solution.py:283
  129.1 32.9 %collective-permute-start.24 = (bf16[16,16,512]{2,1,0:T(8,128)(2,1)}, bf16[16,16,512]{2,1,0:T(8,128)(2,1)}, u32[]{:S(2)}, u32[]{:S(2)}) collective-permute-start(bf16[16,16,512]{2,1,0:T(8,128)(2,1)} %get-tuple-element.159), channel_id=1, source_target_pairs={{0,24},{8,16},{16,8},{24,0},{1,25},{9,17},{17,9},{25,1},{2,26},{10... | collective-permute-start | bytes 786440 | tf_op jit(solution)/shard_map/ppermute | solution.py:283
  162.0 35.6 %collective-permute-start.15 = (bf16[16,16,512]{2,1,0:T(8,128)(2,1)}, bf16[16,16,512]{2,1,0:T(8,128)(2,1)}, u32[]{:S(2)}, u32[]{:S(2)}) collective-permute-start(bf16[16,16,512]{2,1,0:T(8,128)(2,1)} %get-tuple-element.147.refs_6_), channel_id=1, source_target_pairs={{0,8},{8,0},{16,24},{24,16},{1,9},{9,1},{17,25},{25,17},{2,10},{10... | collective-permute-start | bytes 786440 | tf_op jit(solution)/shard_map/ppermute | solution.py:283
  173.6 58.6 %collective-permute-start.31 = (bf16[16,64,512]{2,1,0:T(8,128)(2,1)}, bf16[16,64,512]{2,1,0:T(8,128)(2,1)}, u32[]{:S(2)}, u32[]{:S(2)}) collective-permute-start(bf16[16,64,512]{2,1,0:T(8,128)(2,1)} %get-tuple-element.170), channel_id=1, source_target_pairs={{0,4},{4,0},{1,5},{5,1},{2,6},{6,2},{3,7},{7,3},{8,12},{12,8},{9,1... | collective-permute-start | bytes 3145736 | tf_op jit(solution)/shard_map/ppermute | solution.py:283
  191.5 58.6 %collective-permute-start.28 = (bf16[16,16,512]{2,1,0:T(8,128)(2,1)}, bf16[16,16,512]{2,1,0:T(8,128)(2,1)}, u32[]{:S(2)}, u32[]{:S(2)}) collective-permute-start(bf16[16,16,512]{2,1,0:T(8,128)(2,1)} %get-tuple-element.162.refs_3_), channel_id=1, source_target_pairs={{0,8},{8,0},{16,24},{24,16},{1,9},{9,1},{17,25},{25,17},{2,10},{10... | collective-permute-start | bytes 786440 | tf_op jit(solution)/shard_map/ppermute | solution.py:283
  206.1 33.1 %collective-permute-start.29 = (bf16[16,16,512]{2,1,0:T(8,128)(2,1)}, bf16[16,16,512]{2,1,0:T(8,128)(2,1)}, u32[]{:S(2)}, u32[]{:S(2)}) collective-permute-start(bf16[16,16,512]{2,1,0:T(8,128)(2,1)} %get-tuple-element.168), channel_id=1, source_target_pairs={{0,16},{8,24},{16,0},{24,8},{1,17},{9,25},{17,1},{25,9},{2,18},{10... | collective-permute-start | bytes 786440 | tf_op jit(solution)/shard_map/ppermute | solution.py:283
  225.7 52.1 %collective-permute-start.39 = (bf16[16,64,512]{2,1,0:T(8,128)(2,1)}, bf16[16,64,512]{2,1,0:T(8,128)(2,1)}, u32[]{:S(2)}, u32[]{:S(2)}) collective-permute-start(bf16[16,64,512]{2,1,0:T(8,128)(2,1)} %get-tuple-element.185), channel_id=1, source_target_pairs={{0,4},{4,0},{1,5},{5,1},{2,6},{6,2},{3,7},{7,3},{8,12},{12,8},{9,1... | collective-permute-start | bytes 3145736 | tf_op jit(solution)/shard_map/ppermute | solution.py:283
  232.2 57.7 %collective-permute-start.43 = (bf16[16,16,512]{2,1,0:T(8,128)(2,1)}, bf16[16,16,512]{2,1,0:T(8,128)(2,1)}, u32[]{:S(2)}, u32[]{:S(2)}) collective-permute-start(bf16[16,16,512]{2,1,0:T(8,128)(2,1)} %get-tuple-element.178.refs_4_), channel_id=1, source_target_pairs={{0,8},{8,0},{16,24},{24,16},{1,9},{9,1},{17,25},{25,17},{2,10},{10... | collective-permute-start | bytes 786440 | tf_op jit(solution)/shard_map/ppermute | solution.py:283
  239.2 29.6 %collective-permute-start.26 = (bf16[16,16,512]{2,1,0:T(8,128)(2,1)}, bf16[16,16,512]{2,1,0:T(8,128)(2,1)}, u32[]{:S(2)}, u32[]{:S(2)}) collective-permute-start(bf16[16,16,512]{2,1,0:T(8,128)(2,1)} %get-tuple-element.165), channel_id=1, source_target_pairs={{0,16},{8,24},{16,0},{24,8},{1,17},{9,25},{17,1},{25,9},{2,18},{10... | collective-permute-start | bytes 786440 | tf_op jit(solution)/shard_map/ppermute | solution.py:283
  257.9 30.6 %collective-permute-start.44 = (bf16[16,16,512]{2,1,0:T(8,128)(2,1)}, bf16[16,16,512]{2,1,0:T(8,128)(2,1)}, u32[]{:S(2)}, u32[]{:S(2)}) collective-permute-start(bf16[16,16,512]{2,1,0:T(8,128)(2,1)} %get-tuple-element.190), channel_id=1, source_target_pairs={{0,16},{8,24},{16,0},{24,8},{1,17},{9,25},{17,1},{25,9},{2,18},{10... | collective-permute-start | bytes 786440 | tf_op jit(solution)/shard_map/ppermute | solution.py:283
  272.1 48.5 %collective-permute-start.38 = (bf16[16,64,512]{2,1,0:T(8,128)(2,1)}, bf16[16,64,512]{2,1,0:T(8,128)(2,1)}, u32[]{:S(2)}, u32[]{:S(2)}) collective-permute-start(bf16[16,64,512]{2,1,0:T(8,128)(2,1)} %get-tuple-element.184), channel_id=1, source_target_pairs={{0,4},{4,0},{1,5},{5,1},{2,6},{6,2},{3,7},{7,3},{8,12},{12,8},{9,1... | collective-permute-start | bytes 3145736 | tf_op jit(solution)/shard_map/ppermute | solution.py:283
  277.8 33.1 %collective-permute-start.40 = (bf16[16,16,512]{2,1,0:T(8,128)(2,1)}, bf16[16,16,512]{2,1,0:T(8,128)(2,1)}, u32[]{:S(2)}, u32[]{:S(2)}) collective-permute-start(bf16[16,16,512]{2,1,0:T(8,128)(2,1)} %get-tuple-element.186), channel_id=1, source_target_pairs={{0,8},{8,0},{16,24},{24,16},{1,9},{9,1},{17,25},{25,17},{2,10},{10... | collective-permute-start | bytes 786440 | tf_op jit(solution)/shard_map/ppermute | solution.py:283
  289.9 48.2 %collective-permute-start.35 = (bf16[16,16,512]{2,1,0:T(8,128)(2,1)}, bf16[16,16,512]{2,1,0:T(8,128)(2,1)}, u32[]{:S(2)}, u32[]{:S(2)}) collective-permute-start(bf16[16,16,512]{2,1,0:T(8,128)(2,1)} %get-tuple-element.181.refs_4_), channel_id=1, source_target_pairs={{0,8},{8,0},{16,24},{24,16},{1,9},{9,1},{17,25},{25,17},{2,10},{10... | collective-permute-start | bytes 786440 | tf_op jit(solution)/shard_map/ppermute | solution.py:283
  313.5 46.5 %collective-permute-start.53 = (bf16[16,64,512]{2,1,0:T(8,128)(2,1)}, bf16[16,64,512]{2,1,0:T(8,128)(2,1)}, u32[]{:S(2)}, u32[]{:S(2)}) collective-permute-start(bf16[16,64,512]{2,1,0:T(8,128)(2,1)} %get-tuple-element.203), channel_id=1, source_target_pairs={{0,4},{4,0},{1,5},{5,1},{2,6},{6,2},{3,7},{7,3},{8,12},{12,8},{9,1... | collective-permute-start | bytes 3145736 | tf_op jit(solution)/shard_map/ppermute | solution.py:283
  320.6 43.7 %collective-permute-start.52 = (bf16[16,64,512]{2,1,0:T(8,128)(2,1)}, bf16[16,64,512]{2,1,0:T(8,128)(2,1)}, u32[]{:S(2)}, u32[]{:S(2)}) collective-permute-start(bf16[16,64,512]{2,1,0:T(8,128)(2,1)} %get-tuple-element.202), channel_id=1, source_target_pairs={{0,4},{4,0},{1,5},{5,1},{2,6},{6,2},{3,7},{7,3},{8,12},{12,8},{9,1... | collective-permute-start | bytes 3145736 | tf_op jit(solution)/shard_map/ppermute | solution.py:283
  (36 other events, 735.5 us)
